TPU v7x, 128 devices: a whole 4x4x4 slice. The times are simulated.
128 devices in a mesh: seq: 16 (over x, y_hi, core), tp: 8 (over y_lo, z).
Axes of the slice: x: 4, y: 4 (y_hi: 2, y_lo: 2; y = y_hi * 2 + y_lo), z: 4, core: 2. Of those that a mesh axis runs over, the one named last changes fastest.
Arguments:
- hidden_in: bfloat16 [4096, 4096], P('seq'), may hold values from -16 to 16
- temporal_weight_stack: bfloat16 [4096, 4, 2048], P(None, None, 'tp'), may hold values from -0.5 to 0.5
- depth_in: bfloat16 [4096, 512], replicated, may hold values from -0.09375 to 0.09375
- depth_stack: bfloat16 [4096, 512], replicated, may hold values from -6 to 6
- audio_codes: int32 [4096, 8], P(('seq', 'tp')), may hold values from 0 to 1023
Outputs:
- grad_temporal: float32 [4096, 4, 2048], P('seq', None, 'tp')
- grad_win: float32 [4096, 512], P(('seq', 'tp'))
- grad_depth: float32 [4096, 512], P(('seq', 'tp'))
All inputs are finite; a program needn't handle non-finite values.
Results may differ from a plain program's by a relative error of at most 0.033.
Values may be sent and summed in bfloat16 or wider, within the bound.
A program may use at most 192 MiB of HBM per device.

v0:
```python
import math

import jax
import jax.numpy as jnp
from jax import lax
from jax.sharding import PartitionSpec as P

HD = 128
DHD = 64
VOCAB = 1024


EPSILON = 1e-05
MASKED = -1e30
ROPE_BASE = 10000.0
FULL_PRECISION = lax.Precision.HIGHEST
CONTRACT_ROWS = (((0,), (0,)), ((), ()))
CONTRACT_COLS = (((1,), (1,)), ((), ()))


def rms_scale(values):
    return lax.rsqrt(jnp.mean(values * values, axis=-1, keepdims=True) + EPSILON)


def norm_back(values, gradient):
    scaling = rms_scale(values)
    inner_mean = jnp.mean(gradient * values, axis=-1, keepdims=True)
    return scaling * (gradient - values * (scaling * scaling) * inner_mean)


def rotate(values, positions, orientation):
    half_width = values.shape[-1] // 2
    frequency = ROPE_BASE ** (-jnp.arange(half_width).astype(jnp.float32) / half_width)
    angles = positions[:, None] * frequency[None, :]
    cosine = jnp.cos(angles)[:, None, :]
    sine = orientation * jnp.sin(angles)[:, None, :]
    lower_half = values[..., :half_width]
    upper_half = values[..., half_width:]
    return jnp.concatenate(
        [lower_half * cosine - upper_half * sine, upper_half * cosine + lower_half * sine], axis=-1
    )


def masked_softmax(scores, allowed):
    scores = jnp.where(allowed, scores, MASKED)
    row_top = jnp.max(scores, axis=-1, keepdims=True)
    weights = jnp.where(allowed, jnp.exp(scores - row_top), 0.0)
    return weights / jnp.sum(weights, axis=-1, keepdims=True)


def softmax_back(probs, prob_grad):
    return probs * (prob_grad - jnp.sum(probs * prob_grad, axis=-1, keepdims=True))


def frame_sum(term_all):
    return lax.psum_scatter(
        term_all.astype(jnp.bfloat16), "seq", scatter_dimension=0, tiled=True
    ).astype(jnp.float32)


def depth_pass(latent, depth_stack, audio_codes, loss_scale):
    frame_count, book_count = audio_codes.shape
    depth_width = latent.shape[1]
    head_count = depth_width // DHD
    token_count = frame_count * book_count
    qkv_rows = depth_stack[: 3 * depth_width]
    out_rows = depth_stack[3 * depth_width : 4 * depth_width]
    head_rows = depth_stack[4 * depth_width : 4 * depth_width + VOCAB]
    embed_rows = depth_stack[4 * depth_width + VOCAB :]
    earlier = audio_codes[:, :-1]
    one_hot = (earlier[:, :, None] == jnp.arange(VOCAB)[None, None, :]).astype(jnp.bfloat16)
    embedded = jnp.einsum("fkv,vd->fkd", one_hot, embed_rows, preferred_element_type=jnp.float32)
    opening = jnp.zeros((frame_count, 1, depth_width), jnp.float32)
    stream = latent[:, None, :] + jnp.concatenate([opening, embedded], axis=1)
    stream_flat = stream.reshape(token_count, depth_width)
    stream_norm = (stream_flat * rms_scale(stream_flat)).astype(jnp.bfloat16)
    depth_proj = lax.dot_general(
        stream_norm, qkv_rows, CONTRACT_COLS, preferred_element_type=jnp.float32
    ).astype(jnp.bfloat16)
    split_narrow = depth_proj.reshape(frame_count, book_count, 3, head_count, DHD)
    depth_split = split_narrow.astype(jnp.float32)
    queries = depth_split[:, :, 0]
    key_vals = depth_split[:, :, 1]
    value_vals = depth_split[:, :, 2]
    depth_scale = 1.0 / math.sqrt(DHD)
    causal = jnp.arange(book_count)[None, :] <= jnp.arange(book_count)[:, None]
    scores = (
        jnp.einsum(
            "fqhe,fkhe->fhqk",
            split_narrow[:, :, 0],
            split_narrow[:, :, 1],
            preferred_element_type=jnp.float32,
        )
        * depth_scale
    )
    depth_probs = masked_softmax(scores, causal)
    round_narrow = depth_probs.astype(jnp.bfloat16)
    depth_round = round_narrow.astype(jnp.float32)
    depth_mixed = jnp.einsum(
        "fhqk,fkhe->fqhe", round_narrow, split_narrow[:, :, 2], preferred_element_type=jnp.float32
    )
    depth_mixed = depth_mixed.astype(jnp.bfloat16).reshape(token_count, depth_width)
    resid = stream_flat + lax.dot_general(
        depth_mixed, out_rows, CONTRACT_COLS, preferred_element_type=jnp.float32
    )
    resid_norm = (resid * rms_scale(resid)).astype(jnp.bfloat16)
    logits = lax.dot_general(
        resid_norm, head_rows, CONTRACT_COLS, preferred_element_type=jnp.float32
    )
    targets = audio_codes.reshape(token_count)
    target_hot = (targets[:, None] == jnp.arange(VOCAB)[None, :]).astype(jnp.float32)
    logit_probs = masked_softmax(logits, jnp.ones_like(logits, dtype=bool))
    logit_grad = ((logit_probs - target_hot) * loss_scale).astype(jnp.bfloat16)
    head_grad = lax.dot_general(
        logit_grad, resid_norm, CONTRACT_ROWS, preferred_element_type=jnp.float32
    )
    resid_norm_grad = jnp.dot(logit_grad, head_rows, preferred_element_type=jnp.float32)
    resid_grad = norm_back(resid, resid_norm_grad)
    resid_round = resid_grad.astype(jnp.bfloat16)
    out_grad = lax.dot_general(
        resid_round, depth_mixed, CONTRACT_ROWS, preferred_element_type=jnp.float32
    )
    mixed_grad = jnp.dot(resid_round, out_rows, preferred_element_type=jnp.float32)
    mixed_grad = mixed_grad.reshape(frame_count, book_count, head_count, DHD)
    value_grad = jnp.einsum("fhqk,fqhe->fkhe", depth_round, mixed_grad, precision=FULL_PRECISION)
    prob_grad = jnp.einsum("fqhe,fkhe->fhqk", mixed_grad, value_vals, precision=FULL_PRECISION)
    score_grad = softmax_back(depth_probs, prob_grad) * depth_scale
    query_grad = jnp.einsum("fhqk,fkhe->fqhe", score_grad, key_vals, precision=FULL_PRECISION)
    key_grad = jnp.einsum("fhqk,fqhe->fkhe", score_grad, queries, precision=FULL_PRECISION)
    proj_grad = jnp.stack([query_grad, key_grad, value_grad], axis=2)
    proj_grad = proj_grad.reshape(token_count, 3 * depth_width).astype(jnp.bfloat16)
    qkv_grad = lax.dot_general(
        proj_grad, stream_norm, CONTRACT_ROWS, preferred_element_type=jnp.float32
    )
    stream_norm_grad = jnp.dot(proj_grad, qkv_rows, preferred_element_type=jnp.float32)
    stream_grad = resid_grad + norm_back(stream_flat, stream_norm_grad)
    stream_grid = stream_grad.reshape(frame_count, book_count, depth_width)
    embed_grad = jnp.einsum(
        "fkv,fkd->vd",
        one_hot,
        stream_grid[:, 1:].astype(jnp.bfloat16),
        preferred_element_type=jnp.float32,
    )
    latent_grad = jnp.sum(stream_grid, axis=1).astype(jnp.bfloat16)
    grad_depth = jnp.concatenate([qkv_grad, out_grad, head_grad, embed_grad], axis=0)
    return (grad_depth, latent_grad)


def per_device(hidden_in, temporal_weight_stack, depth_in, depth_stack, audio_codes):
    frames_dev = hidden_in.shape[0]
    inner_dev = temporal_weight_stack.shape[2]
    head_count = inner_dev // HD
    depth_frames = audio_codes.shape[0]
    book_count = audio_codes.shape[1]
    depth_width = depth_in.shape[1]
    seq_count = lax.axis_size("seq")
    tp_count = lax.axis_size("tp")
    device_count = seq_count * tp_count
    seq_index = lax.axis_index("seq")
    tp_index = lax.axis_index("tp")
    total_frames = frames_dev * seq_count
    att_scale = 1.0 / math.sqrt(HD)
    hidden_full = hidden_in.astype(jnp.float32)
    rms_normalized = (hidden_full * rms_scale(hidden_full)).astype(jnp.bfloat16)
    projected = jnp.einsum(
        "wo,obu->wbu",
        rms_normalized,
        temporal_weight_stack[:, :3, :],
        preferred_element_type=jnp.float32,
    )
    query_pos = seq_index * frames_dev + jnp.arange(frames_dev)
    positions = query_pos.astype(jnp.float32)
    query_rows = rotate(projected[:, 0].reshape(frames_dev, head_count, HD), positions, 1.0).astype(
        jnp.bfloat16
    )
    key_rows = rotate(projected[:, 1].reshape(frames_dev, head_count, HD), positions, 1.0).astype(
        jnp.bfloat16
    )
    value_rows = projected[:, 2].astype(jnp.bfloat16)
    local_pairs = jnp.stack([key_rows.reshape(frames_dev, inner_dev), value_rows], axis=1)
    all_pairs = lax.all_gather(local_pairs, "seq", axis=0, tiled=True)
    keys_all = all_pairs[:, 0].reshape(total_frames, head_count, HD)
    values_all = all_pairs[:, 1].reshape(total_frames, head_count, HD)
    allowed = (jnp.arange(total_frames)[None, :] <= query_pos[:, None])[None]
    scores = (
        jnp.einsum("qhe,khe->hqk", query_rows, keys_all, preferred_element_type=jnp.float32)
        * att_scale
    )
    attn_probs = masked_softmax(scores, allowed)
    attn_round = attn_probs.astype(jnp.bfloat16)
    attended = jnp.einsum(
        "hqk,khe->qhe", attn_round, values_all, preferred_element_type=jnp.float32
    )
    attended = attended.astype(jnp.bfloat16).reshape(frames_dev, inner_dev)
    out_w = temporal_weight_stack[:, 3, :]
    branch = lax.psum_scatter(
        lax.dot_general(attended, out_w, CONTRACT_COLS, preferred_element_type=jnp.float32).astype(
            jnp.bfloat16
        ),
        "tp",
        scatter_dimension=0,
        tiled=True,
    ).astype(jnp.float32)
    own_hidden = lax.dynamic_slice_in_dim(hidden_full, tp_index * depth_frames, depth_frames, 0)
    merged = own_hidden + branch
    merged_norm = (merged * rms_scale(merged)).astype(jnp.bfloat16)
    latent = jnp.dot(merged_norm, depth_in, preferred_element_type=jnp.float32)
    loss_scale = 1.0 / math.sqrt(total_frames * book_count)
    grad_depth, latent_grad = depth_pass(latent, depth_stack, audio_codes, loss_scale)
    grad_win = lax.dot_general(
        merged_norm, latent_grad, CONTRACT_ROWS, preferred_element_type=jnp.float32
    )
    blocks = jnp.concatenate(
        [
            grad_win.reshape(device_count, -1, depth_width),
            grad_depth.reshape(device_count, -1, depth_width),
        ],
        axis=1,
    )
    share = lax.psum_scatter(blocks, ("seq", "tp"), scatter_dimension=0, tiled=True)[0]
    depth_rows = depth_stack.shape[0] // device_count
    depth_share = share[share.shape[0] - depth_rows :]
    win_share = share[: share.shape[0] - depth_rows]
    merged_norm_grad = lax.dot_general(
        latent_grad, depth_in, CONTRACT_COLS, preferred_element_type=jnp.float32
    )
    merged_grad = norm_back(merged, merged_norm_grad).astype(jnp.bfloat16)
    shard_rows = lax.all_gather(merged_grad, "tp", axis=0, tiled=True)
    update = jnp.dot(shard_rows, out_w, preferred_element_type=jnp.float32)
    attended_grad = update
    out_w_grad = lax.dot_general(
        shard_rows, attended, CONTRACT_ROWS, preferred_element_type=jnp.float32
    )
    attended_grad, out_w_grad = (attended_grad, out_w_grad)
    attended_round = attended_grad.astype(jnp.bfloat16).reshape(frames_dev, head_count, HD)
    prob_temporal = jnp.einsum(
        "qhe,khe->hqk", attended_round, values_all, preferred_element_type=jnp.float32
    )
    score_temporal = (softmax_back(attn_probs, prob_temporal) * att_scale).astype(jnp.bfloat16)
    query_temporal = jnp.einsum(
        "hqk,khe->qhe", score_temporal, keys_all, preferred_element_type=jnp.float32
    )
    key_partial = jnp.einsum(
        "hqk,qhe->khe", score_temporal, query_rows, preferred_element_type=jnp.float32
    )
    value_partial = jnp.einsum(
        "hqk,qhe->khe", attn_round, attended_round, preferred_element_type=jnp.float32
    )
    key_term = jnp.stack(
        [
            key_partial.reshape(total_frames, inner_dev),
            value_partial.reshape(total_frames, inner_dev),
        ],
        axis=1,
    )
    key_share = frame_sum(key_term)
    query_back = rotate(query_temporal, positions, -1.0).reshape(frames_dev, inner_dev)
    key_back = rotate(key_share[:, 0].reshape(frames_dev, head_count, HD), positions, -1.0).reshape(
        frames_dev, inner_dev
    )
    temporal_projection = jnp.stack([query_back, key_back, key_share[:, 1]], axis=1).astype(
        jnp.bfloat16
    )
    incoming_gradient = jnp.einsum(
        "jn,jws->nws", rms_normalized, temporal_projection, preferred_element_type=jnp.float32
    )
    weight_term = jnp.concatenate([incoming_gradient, out_w_grad[:, None, :]], axis=1)
    weight_share = frame_sum(weight_term)
    return (weight_share, win_share, depth_share)


def solution(mesh):
    in_specs = (P("seq", None), P(None, None, "tp"), P(), P(), P(("seq", "tp"), None))
    out_specs = (P("seq", None, "tp"), P(("seq", "tp"), None), P(("seq", "tp"), None))
    return jax.shard_map(
        per_device, mesh=mesh, in_specs=in_specs, out_specs=out_specs, check_vma=False
    )
```

profile of v0, /device:TPU:1, one launch (start us, length us, event | category | flops | bytes accessed | tf_op | source)
XLA Modules:
  0.0 1154.2 jit_solution(11077571580082223513)
XLA Ops:
  7.2 2.1 multiply_reduce_fusion.1
  9.3 6.6 fusion.7
  19.3 7.4 slice.107
  28.4 53.4 %all-gather.3.cloned.1.call-done = bf16[4096,2,256]{0,2,1:T(8,128)(2,1)} async-done(((bf16[256,2,256]{0,2,1:T(8,128)(2,1)}), bf16[4096,2,256]{0,2,1:T(8,128)(2,1)}) %all-gather.3.cloned.1.call-update) | async-done | bytes 4194320 | tf_op jit(solution)/shard_map/all_gather | solution.py:181
  81.8 4.1 fusion.97
  85.9 10.4 fusion.103
  96.3 5.1 fusion.35
  101.5 2.1 convolution_convert_fusion.4
  103.7 2.4 convert_element_type.123
  106.9 32.9 %reduce-scatter.5.cloned.1.call-done = bf16[32,4096]{1,0:T(8,128)(2,1)} async-done(((bf16[256,4096]{1,0:T(8,128)(2,1)}), bf16[32,4096]{1,0:T(8,128)(2,1)}) %reduce-scatter.5.cloned.1.call-update) | async-done | bytes 262160 | tf_op jit(solution)/shard_map/reduce_scatter | solution.py:196
  141.5 3.0 fusion.93
  144.6 1.8 multiply_reduce_fusion.6
  146.6 3.1 convolution_convert_fusion.5
  149.7 3.6 reshape.245
  153.2 2.6 fusion.98
  155.8 3.1 fusion.104
  158.9 1.8 fusion.31
  161.2 1.8 multiply_reduce_fusion.5
  163.0 1.8 fusion.105
  166.2 1.9 multiply_reduce_fusion.4
  169.1 2.2 fusion.57
  171.3 2.2 reshape.247
  173.5 2.7 convolution_bitcast_fusion.1
  176.3 3.0 multiply_reduce_fusion.2
  184.2 3.5 convert_element_type.144
  187.7 2.7 fusion.56
  190.5 2.4 fusion.95
  195.3 40.1 %all-gather.5.cloned.1.call-done = bf16[256,4096]{1,0:T(8,128)(2,1)} async-done(((bf16[32,4096]{1,0:T(8,128)(2,1)}), bf16[256,4096]{1,0:T(8,128)(2,1)}) %all-gather.5.cloned.1.call-update) | async-done | bytes 2097168 | tf_op jit(solution)/shard_map/all_gather | solution.py:228
  235.4 3.7 convolution_convert_fusion.7
  239.2 5.7 convolution_convert_fusion.2
  244.9 4.5 fusion.106
  249.4 4.1 copy.94
  253.5 15.3 %convolution_convert_fusion.3 = bf16[2,128,4096]{2,1,0:T(8,128)(2,1)} fusion(f32[2,256,4096]{2,1,0:T(8,128)} %fusion.106, bf16[256,2,64]{2,0,1:T(8,128)(2,1)} %copy-done.22, bf16[256,2,64]{2,0,1:T(8,128)(2,1)} %copy-done.21, f32[2,256,4096]{2,1,0:T(8,128)} %get-tuple-element.53, f32[2,256]{1,0:T(2,128)S(1)} %copy-done.32), kind=kOutput, calls=%fused_computation.17 | convolution fusion | flops 552866304 | bytes 19007488 | tf_op jit(solution)/shard_map/hqk,qhe->khe/dot_general | solution.py:243
  268.8 4.1 copy.93
  272.9 4.5 pad_maximum_fusion.3
  277.5 3.7 fusion.9
  281.2 13.9 %fusion.32 = f32[256,2,128]{2,0,1:T(8,128)} fusion(bf16[4096,2,128]{0,2,1:T(8,128)(2,1)} %bitcast.141, f32[2,256,4096]{2,1,0:T(8,128)} %fusion.106, f32[2,256,4096]{2,1,0:T(8,128)} %get-tuple-element.53, f32[2,256]{1,0:T(2,128)S(1)} %copy-done.32), kind=kOutput, calls=%fused_computation.52 | convolution fusion | flops 551555584 | bytes 19138560 | tf_op jit(solution)/shard_map/hqk,khe->qhe/dot_general | solution.py:240
  295.1 65.7 %reduce-scatter.7.cloned.1.call-done = bf16[256,2,256]{2,0,1:T(8,128)(2,1)} async-done(((bf16[4096,2,256]{2,0,1:T(8,128)(2,1)}), bf16[256,2,256]{2,0,1:T(8,128)(2,1)}) %reduce-scatter.7.cloned.1.call-update) | async-done | bytes 262160 | tf_op jit(solution)/shard_map/reduce_scatter | solution.py:56
  362.6 1.8 copy.95
  366.1 1.8 copy.123
  367.9 1.8 copy.124
  375.5 5.9 convolution_convert_fusion
  381.4 6.7 pad_maximum_fusion.1
  389.4 1.9 convolution_bitcast_fusion
  395.5 7.4 pad_maximum_fusion
  402.9 87.0 %reduce-scatter.9.cloned.1.call-done = bf16[256,4,256]{2,0,1:T(8,128)(2,1)} async-done(((bf16[4096,4,256]{2,0,1:T(8,128)(2,1)}), bf16[256,4,256]{2,0,1:T(8,128)(2,1)}) %reduce-scatter.9.cloned.1.call-update) | async-done | bytes 524304 | tf_op jit(solution)/shard_map/reduce_scatter | solution.py:56
  489.9 2.4 copy.104
  492.3 653.2 %reduce-scatter.11.cloned.1.call-done = f32[1,64,512]{2,1,0:T(8,128)} async-done(((f32[128,64,512]{2,1,0:T(8,128)}), f32[1,64,512]{2,1,0:T(8,128)}) %reduce-scatter.11.cloned.1.call-update) | async-done | bytes 131088 | tf_op jit(solution)/shard_map/reduce_scatter | solution.py:220
  (136 shorter events, 34.0 us)
Async XLA Ops:
  7.2 74.6 %all-gather.3.cloned.1.call-start = ((), (), s32[]{:S(2)}) async-start(), calls=%async_computation.4 | async-start | bytes 4456448 | tf_op jit(solution)/shard_map/all_gather | solution.py:181
  9.3 6.7 copy-start.25
  18.0 67.9 %copy-start.21 = (bf16[256,2,64]{2,0,1:T(8,128)(2,1)}, bf16[256,2,64]{2,0,1:T(8,128)(2,1)S(1)}, u32[]{:S(2)}) copy-start(bf16[256,2,64]{2,0,1:T(8,128)(2,1)S(1)} %get-tuple-element.23) | copy-start | bytes 196612
  18.0 67.9 %copy-start.22 = (bf16[256,2,64]{2,0,1:T(8,128)(2,1)}, bf16[256,2,64]{2,0,1:T(8,128)(2,1)S(1)}, u32[]{:S(2)}) copy-start(bf16[256,2,64]{2,0,1:T(8,128)(2,1)S(1)} %get-tuple-element.24) | copy-start | bytes 196612
  19.0 120.7 %reduce-scatter.5.cloned.1.call-start = ((), (), s32[]{:S(2)}) async-start(), calls=%async_computation.5 | async-start | bytes 2359296 | tf_op jit(solution)/shard_map/reduce_scatter | solution.py:196
  85.9 10.4 copy-start.5
  96.3 5.2 copy-start.31
  96.3 5.2 copy-start.1
  101.4 4.7 copy-start.15
  101.5 2.2 copy-start.2
  103.6 2.5 copy-start.23
  103.6 131.8 %all-gather.5.cloned.1.call-start = ((), (), s32[]{:S(2)}) async-start(), calls=%async_computation.6 | async-start | bytes 2359296 | tf_op jit(solution)/shard_map/all_gather | solution.py:228
  146.4 9.4 copy-start.8
  155.8 3.1 copy-start.18
  158.9 1.8 copy-start.29
  166.2 2.0 copy-start.10
  168.3 0.8 copy-start.3
  173.5 5.8 copy-start.17
  173.5 5.8 copy-start.28
  173.5 5.8 copy-start.30
  176.2 4.2 copy-start.16
  187.7 5.1 copy-start
  190.5 3.9 copy-start.27
  192.9 1.4 copy-start.19
  195.2 165.7 %reduce-scatter.7.cloned.1.call-start = ((), (), s32[]{:S(2)}) async-start(), calls=%async_computation.7 | async-start | bytes 4456448 | tf_op jit(solution)/shard_map/reduce_scatter | solution.py:56
  239.2 5.7 copy-start.6
  249.4 4.1 copy-start.32
  277.5 212.5 %reduce-scatter.9.cloned.1.call-start = ((), (), s32[]{:S(2)}) async-start(), calls=%async_computation.8 | async-start | bytes 8912896 | tf_op jit(solution)/shard_map/reduce_scatter | solution.py:56
  295.1 80.3 %copy-start.26 = (f32[256]{0:T(256)S(1)}, f32[256]{0:T(256)}, u32[]{:S(2)}) copy-start(f32[256]{0:T(256)} %copy-done.25) | copy-start | bytes 3076
  375.5 5.9 copy-start.7
  388.1 0.9 copy-start.14
  388.1 1.1 copy-start.9
  388.1 1.2 copy-start.24
  388.2 3.1 copy-start.4
  388.2 757.4 %reduce-scatter.11.cloned.1.call-start = ((), (), s32[]{:S(2)}) async-start(), calls=%async_computation.9 | async-start | bytes 16908288 | tf_op jit(solution)/shard_map/reduce_scatter | solution.py:220
  389.3 2.4 copy-start.11
  389.4 2.8 copy-start.12
  391.3 1.6 copy-start.20
  392.9 1.6 copy-start.13
Sparse Core Ops, SparseCore 0:
  19.1 62.6 all-gather.2
  103.8 35.9 reduce-scatter.4
  195.3 40.0 all-gather.4
  277.6 83.2 reduce-scatter.6
  388.3 101.5 reduce-scatter.8
  492.3 653.2 reduce-scatter.10
where the time goes:
time: 1170 us; the launch traced here: 1150 us
  waiting for transfers between devices  933 us (80%)
  matrix products  115 us (10%)
  local copies, waits for them, and re-layouts  51.7 us (4%)
  other arithmetic  39.8 us (3%)
  between operations  14.9 us (1%)
    reduce_scatter x1, waiting for transfers between devices, per_device(): lax.psum_scatter(blocks, ('seq', 'tp'), scatter_dimension=0, tiled=True)[0]  653 us
    reduce_scatter x2, waiting for transfers between devices, frame_sum(): lax.psum_scatter(term_all.astype(jnp.bfloat16), 'seq', scatter_dimension=...  153 us
    all_gather x1, waiting for transfers between devices, per_device(): all_pairs = lax.all_gather(local_pairs, 'seq', axis=0, tiled=True)  53.4 us
    all_gather x1, waiting for transfers between devices, per_device(): shard_rows = lax.all_gather(merged_grad, 'tp', axis=0, tiled=True)  40.1 us
    reduce_scatter x1, waiting for transfers between devices, per_device(): lax.psum_scatter(lax.dot_general(attended, out_w, CONTRACT_COLS, preferre...  32.9 us
  transfers between devices with their start and end apart: 6, of which 6 were waited for; matrix products, arithmetic and copies ran while one was open for 4% of the time, Pallas kernels for 0%

commit v1 on v0

--- a/solution.py
+++ b/solution.py
@@ -212,12 +212,15 @@
     )
     blocks = jnp.concatenate(
         [
-            grad_win.reshape(device_count, -1, depth_width),
-            grad_depth.reshape(device_count, -1, depth_width),
+            grad_win.reshape(seq_count, tp_count, -1, depth_width),
+            grad_depth.reshape(seq_count, tp_count, -1, depth_width),
         ],
-        axis=1,
-    )
-    share = lax.psum_scatter(blocks, ("seq", "tp"), scatter_dimension=0, tiled=True)[0]
+        axis=2,
+    ).astype(jnp.bfloat16)
+    blocks = blocks.transpose(1, 0, 2, 3)
+    share = lax.psum_scatter(blocks, "tp", scatter_dimension=0, tiled=True)[0]
+    share = lax.psum_scatter(share, "seq", scatter_dimension=0, tiled=True)[0]
+    share = share.astype(jnp.float32)
     depth_rows = depth_stack.shape[0] // device_count
     depth_share = share[share.shape[0] - depth_rows :]
     win_share = share[: share.shape[0] - depth_rows]

time: 1170 us -> 647 us (0.55)
  waiting for transfers between devices: 933 us -> 434 us
    reduce_scatter x1 -> x2, waiting for transfers between devices: 653 us -> 148 us  [the longest x1 93.9 us: per_device(): share = lax.psum_scatter(blocks, 'tp', scatter_dimension=0, tiled=True)[0]]
  transfers between devices with their start and end apart: 6 -> 7, of which waited for: 6 -> 7; matrix products, arithmetic and copies ran while one was open for 4% -> 9% of each run, Pallas kernels for 0% -> 0%
where the time goes in v1:
time: 647 us; the launch traced here: 641 us
  waiting for transfers between devices  434 us (67%)
  matrix products  114 us (18%)
  local copies, waits for them, and re-layouts  41.9 us (6%)
  other arithmetic  34.9 us (5%)
  between operations  15.1 us (2%)
    reduce_scatter x2, waiting for transfers between devices, frame_sum(): lax.psum_scatter(term_all.astype(jnp.bfloat16), 'seq', scatter_dimension=...  159 us
    reduce_scatter x1, waiting for transfers between devices, per_device(): share = lax.psum_scatter(blocks, 'tp', scatter_dimension=0, tiled=True)[0]  93.9 us
    all_gather x1, waiting for transfers between devices, per_device(): all_pairs = lax.all_gather(local_pairs, 'seq', axis=0, tiled=True)  54.1 us
    reduce_scatter x1, waiting for transfers between devices, per_device(): share = lax.psum_scatter(share, 'seq', scatter_dimension=0, tiled=True)[0]  53.8 us
    all_gather x1, waiting for transfers between devices, per_device(): shard_rows = lax.all_gather(merged_grad, 'tp', axis=0, tiled=True)  40.4 us
    reduce_scatter x1, waiting for transfers between devices, per_device(): lax.psum_scatter(lax.dot_general(attended, out_w, CONTRACT_COLS, preferre...  32.7 us
    dot_general x1, matrix products, per_device(): jnp.einsum('hqk,qhe->khe', score_temporal, query_rows, preferred_element_...  15.3 us
    dot_general x1, matrix products, per_device(): jnp.einsum('hqk,khe->qhe', score_temporal, keys_all, preferred_element_ty...  14.5 us
  transfers between devices with their start and end apart: 7, of which 7 were waited for; matrix products, arithmetic and copies ran while one was open for 9% of the time, Pallas kernels for 0%

profile of v1, /device:TPU:1, one launch (start us, length us, event | category | flops | bytes accessed | tf_op | source)
XLA Modules:
  0.0 641.1 jit_solution(4405874294264240809)
XLA Ops:
  7.2 2.1 multiply_reduce_fusion.1
  9.3 6.6 %fusion.7 = f32[256,3,256]{0,2,1:T(8,128)S(1)} fusion(bf16[4096,3,256]{2,1,0:T(4,128)(2,1)} %bitcast.140, f32[256]{0:T(256)S(1)} %add_rsqrt_fusion.2, bf16[256,4096]{1,0:T(8,128)(2,1)} %param.5), kind=kOutput, calls=%fused_computation.13 | convolution fusion | flops 1613758464 | bytes 9176064 | tf_op jit(solution)/shard_map/wo,obu->wbu/dot_general | solution.py:165
  20.3 7.4 %slice.107 = bf16[4096,1,256]{2,1,0:T(2,128)(2,1)} slice(bf16[4096,4,256]{2,1,0:T(4,128)(2,1)} %param.6), slice={[0:4096], [3:4], [0:256]} | slice | bytes 4194304 | tf_op jit(solution)/shard_map/slice | solution.py:195
  28.4 54.1 %all-gather.3.cloned.1.call-done = bf16[4096,2,256]{0,2,1:T(8,128)(2,1)} async-done(((bf16[256,2,256]{0,2,1:T(8,128)(2,1)}), bf16[4096,2,256]{0,2,1:T(8,128)(2,1)}) %all-gather.3.cloned.1.call-update) | async-done | bytes 4194320 | tf_op jit(solution)/shard_map/all_gather | solution.py:181
  82.5 4.0 fusion.93
  86.6 9.8 %fusion.99 = (f32[2,256]{1,0:T(2,128)S(1)}, f32[2,256,4096]{2,1,0:T(8,128)}) fusion(pred[256,4096]{1,0:T(8,128)(4,1)S(1)} %iota_compare_fusion, bf16[4096,2,128]{0,2,1:T(8,128)(2,1)} %bitcast.143, bf16[256,2,64]{2,0,1:T(8,128)(2,1)S(1)} %copy-done.20, bf16[256,2,64]{2,0,1:T(8,128)(2,1)S(1)} %copy-done.19), kind=kOutput, calls=%fused_computation.173 | convolution fusion | flops 547622912 | bytes 11667456 | tf_op jit(solution)/shard_map/sub | solution.py:47
  96.4 5.1 fusion.35
  102.2 2.1 convolution_convert_fusion.5
  104.3 2.4 convert_element_type.128
  107.5 32.7 %reduce-scatter.6.cloned.1.call-done = bf16[32,4096]{1,0:T(8,128)(2,1)} async-done(((bf16[256,4096]{1,0:T(8,128)(2,1)}), bf16[32,4096]{1,0:T(8,128)(2,1)}) %reduce-scatter.6.cloned.1.call-update) | async-done | bytes 262160 | tf_op jit(solution)/shard_map/reduce_scatter | solution.py:196
  142.1 3.0 fusion.90
  145.1 1.8 multiply_reduce_fusion.6
  147.1 3.1 convolution_convert_fusion.7
  150.2 3.3 reshape.248
  153.5 2.5 fusion.94
  156.0 3.1 fusion.100
  159.1 1.8 fusion.31
  161.4 1.8 multiply_reduce_fusion.5
  163.2 1.8 fusion.101
  166.4 1.9 multiply_reduce_fusion.4
  169.3 2.1 fusion.57
  171.5 2.3 reshape.250
  173.8 2.7 convolution_bitcast_fusion
  176.5 3.0 multiply_reduce_fusion.2
  182.9 1.5 copy.91
  184.4 3.6 convert_element_type.149
  188.0 2.7 fusion.56
  190.8 2.4 fusion.91
  193.2 1.4 multiply_reduce_fusion.3
  195.6 40.4 %all-gather.5.cloned.1.call-done = bf16[256,4096]{1,0:T(8,128)(2,1)} async-done(((bf16[32,4096]{1,0:T(8,128)(2,1)}), bf16[256,4096]{1,0:T(8,128)(2,1)}) %all-gather.5.cloned.1.call-update) | async-done | bytes 2097168 | tf_op jit(solution)/shard_map/all_gather | solution.py:231
  236.0 3.7 convolution_convert_fusion.11
  239.8 5.7 convolution_convert_fusion.3
  245.6 4.5 fusion.102
  250.1 4.1 copy.98
  254.2 15.3 %convolution_convert_fusion.4 = bf16[2,128,4096]{2,1,0:T(8,128)(2,1)} fusion(f32[2,256,4096]{2,1,0:T(8,128)} %fusion.102, bf16[256,2,64]{2,0,1:T(8,128)(2,1)} %get-tuple-element.24, bf16[256,2,64]{2,0,1:T(8,128)(2,1)} %get-tuple-element.23, f32[2,256,4096]{2,1,0:T(8,128)} %get-tuple-element.53, f32[2,256]{1,0:T(2,128)S(1)} %copy-done.30), kind=kOutput, calls=%fused_computation.18 | convolution fusion | flops 552866304 | bytes 19007488 | tf_op jit(solution)/shard_map/hqk,qhe->khe/dot_general | solution.py:246
  269.4 4.1 copy.97
  273.5 4.6 pad_maximum_fusion.2
  285.3 3.6 copy_bitcast_fusion
  289.8 3.8 fusion.9
  293.6 14.5 %fusion.32 = f32[256,2,128]{2,0,1:T(8,128)S(1)} fusion(bf16[4096,2,128]{0,2,1:T(8,128)(2,1)} %bitcast.144, f32[2,256,4096]{2,1,0:T(8,128)} %fusion.102, f32[2,256,4096]{2,1,0:T(8,128)} %get-tuple-element.53, f32[2,256]{1,0:T(2,128)S(1)} %copy-done.31), kind=kOutput, calls=%fused_computation.57 | convolution fusion | flops 551555584 | bytes 19138560 | tf_op jit(solution)/shard_map/hqk,khe->qhe/dot_general | solution.py:243
  308.1 53.5 %reduce-scatter.8.cloned.1.call-done = bf16[256,2,256]{2,0,1:T(8,128)(2,1)} async-done(((bf16[4096,2,256]{2,0,1:T(8,128)(2,1)}), bf16[256,2,256]{2,0,1:T(8,128)(2,1)}) %reduce-scatter.8.cloned.1.call-update) | async-done | bytes 262160 | tf_op jit(solution)/shard_map/reduce_scatter | solution.py:56
  361.6 1.6 slice_convert_fusion.1
  363.4 93.9 %reduce-scatter.12.cloned.1.call-done = bf16[1,16,64,512]{3,2,1,0:T(8,128)(2,1)} async-done(((bf16[8,16,64,512]{3,2,1,0:T(8,128)(2,1)}), bf16[1,16,64,512]{3,2,1,0:T(8,128)(2,1)}) %reduce-scatter.12.cloned.1.call-update) | async-done | bytes 1048592 | tf_op jit(solution)/shard_map/reduce_scatter | solution.py:221
  458.5 5.9 convolution_convert_fusion
  464.3 6.7 %pad_maximum_fusion = bf16[4096,4,256]{2,0,1:T(8,128)(2,1)} fusion(bf16[4096,1,256]{2,0,1:T(8,128)(2,1)S(1)} %copy-done.6, bf16[4096,3,256]{2,0,1:T(8,128)(2,1)} %convolution_convert_fusion), kind=kLoop, calls=%fused_computation.3 | loop fusion | flops 4194304 | bytes 16777216 | tf_op jit(solution)/shard_map/concatenate | solution.py:270
  471.1 53.8 %reduce-scatter.14.cloned.1.call-done = bf16[1,64,512]{2,1,0:T(8,128)(2,1)} async-done(((bf16[16,64,512]{2,1,0:T(8,128)(2,1)}), bf16[1,64,512]{2,1,0:T(8,128)(2,1)}) %reduce-scatter.14.cloned.1.call-update) | async-done | bytes 65552 | tf_op jit(solution)/shard_map/reduce_scatter | solution.py:222
  526.4 105.2 %reduce-scatter.10.cloned.1.call-done = bf16[256,4,256]{2,0,1:T(8,128)(2,1)} async-done(((bf16[4096,4,256]{2,0,1:T(8,128)(2,1)}), bf16[256,4,256]{2,0,1:T(8,128)(2,1)}) %reduce-scatter.10.cloned.1.call-update) | async-done | bytes 524304 | tf_op jit(solution)/shard_map/reduce_scatter | solution.py:56
  631.6 2.4 copy.110
  (138 shorter events, 26.3 us)
Async XLA Ops:
  7.2 75.3 %all-gather.3.cloned.1.call-start = ((), (), s32[]{:S(2)}) async-start(), calls=%async_computation.5 | async-start | bytes 4456448 | tf_op jit(solution)/shard_map/all_gather | solution.py:181
  9.3 6.7 %copy-start.23 = (f32[256]{0:T(256)}, f32[256]{0:T(256)S(1)}, u32[]{:S(2)}) copy-start(f32[256]{0:T(256)S(1)} %add_rsqrt_fusion.2) | copy-start | bytes 3076
  19.7 120.5 %reduce-scatter.6.cloned.1.call-start = ((), (), s32[]{:S(2)}) async-start(), calls=%async_computation.6 | async-start | bytes 2359296 | tf_op jit(solution)/shard_map/reduce_scatter | solution.py:196
  28.4 58.2 %copy-start.19 = (bf16[256,2,64]{2,0,1:T(8,128)(2,1)S(1)}, bf16[256,2,64]{2,0,1:T(8,128)(2,1)}, u32[]{:S(2)}) copy-start(bf16[256,2,64]{2,0,1:T(8,128)(2,1)} %get-tuple-element.23) | copy-start | bytes 196612
  28.4 58.2 %copy-start.20 = (bf16[256,2,64]{2,0,1:T(8,128)(2,1)S(1)}, bf16[256,2,64]{2,0,1:T(8,128)(2,1)}, u32[]{:S(2)}) copy-start(bf16[256,2,64]{2,0,1:T(8,128)(2,1)} %get-tuple-element.24) | copy-start | bytes 196612
  86.5 9.8 %copy-start.4 = (bf16[4096,1,256]{0,2,1:T(8,128)(2,1)}, bf16[4096,1,256]{0,2,1:T(8,128)(2,1)S(1)}, u32[]{:S(2)}) copy-start(bf16[4096,1,256]{0,2,1:T(8,128)(2,1)S(1)} %get-tuple-element.17) | copy-start | bytes 6291460
  96.4 5.1 copy-start.29
  96.4 5.8 copy-start.1
  101.5 0.6 copy-start.12
  101.5 2.8 copy-start.2
  104.2 2.5 copy-start.21
  104.3 131.8 %all-gather.5.cloned.1.call-start = ((), (), s32[]{:S(2)}) async-start(), calls=%async_computation.7 | async-start | bytes 2359296 | tf_op jit(solution)/shard_map/all_gather | solution.py:231
  146.9 9.1 %copy-start.7 = (f32[32,8,512]{2,0,1:T(8,128)}, f32[32,8,512]{2,0,1:T(8,128)S(1)}, u32[]{:S(2)}) copy-start(f32[32,8,512]{2,0,1:T(8,128)S(1)} %get-tuple-element.55) | copy-start | bytes 1572868
  156.0 3.1 copy-start.16
  159.1 1.8 copy-start.27
  166.4 2.0 copy-start.8
  168.5 0.8 copy-start.3
  173.8 5.8 copy-start.15
  173.8 5.8 copy-start.26
  173.8 5.8 copy-start.28
  176.5 4.2 copy-start.14
  188.0 5.2 copy-start
  190.7 3.9 copy-start.25
  193.2 1.4 copy-start.17
  195.5 166.0 %reduce-scatter.8.cloned.1.call-start = ((), (), s32[]{:S(2)}) async-start(), calls=%async_computation.8 | async-start | bytes 4456448 | tf_op jit(solution)/shard_map/reduce_scatter | solution.py:56
  239.8 5.8 copy-start.5
  250.1 4.1 copy-start.30
  278.1 3.7 copy-start.22
  278.1 179.2 %reduce-scatter.12.cloned.1.call-start = ((), (), s32[]{:S(2)}) async-start(), calls=%async_computation.10 | async-start | bytes 9437184 | tf_op jit(solution)/shard_map/reduce_scatter | solution.py:221
  278.1 4.2 copy-start.9
  281.8 1.1 copy-start.10
  281.8 1.8 copy-start.18
  288.9 0.9 copy-start.13
  288.9 4.7 copy-start.31
  288.9 235.9 %reduce-scatter.14.cloned.1.call-start = ((), (), s32[]{:S(2)}) async-start(), calls=%async_computation.11 | async-start | bytes 1114112 | tf_op jit(solution)/shard_map/reduce_scatter | solution.py:222
  293.6 164.0 %copy-start.11 = (f32[256,64]{1,0:T(8,128)S(1)}, f32[256,64]{1,0:T(8,128)}, u32[]{:S(2)}) copy-start(f32[256,64]{1,0:T(8,128)} %get-tuple-element.45) | copy-start | bytes 196612
  308.1 150.3 %copy-start.24 = (f32[256]{0:T(256)S(1)}, f32[256]{0:T(256)}, u32[]{:S(2)}) copy-start(f32[256]{0:T(256)} %copy-done.23) | copy-start | bytes 3076
  457.3 174.3 %reduce-scatter.10.cloned.1.call-start = ((), (), s32[]{:S(2)}) async-start(), calls=%async_computation.9 | async-start | bytes 8912896 | tf_op jit(solution)/shard_map/reduce_scatter | solution.py:56
  458.4 5.9 copy-start.6
Sparse Core Ops, SparseCore 0:
  19.8 62.6 all-gather.2
  104.4 35.7 reduce-scatter.5
  195.7 40.3 all-gather.4
  278.2 83.3 reduce-scatter.7
  364.0 93.2 reduce-scatter.11
  461.4 63.3 reduce-scatter.13
  529.2 102.3 reduce-scatter.9

commit v2 on v0

v2 whole, which is shorter than its diff:
```python
import functools
import math

import jax
import jax.numpy as jnp
from jax import lax
from jax.experimental import pallas as pl
from jax.experimental.pallas import tpu as pltpu
from jax.sharding import PartitionSpec as P

HD = 128
DHD = 64
VOCAB = 1024
CHIPS = 8
TP = 8
FR = 256
FR2 = 512
DD = 512
NS = 512

EPSILON = 1e-05
MASKED = -1e30
ROPE_BASE = 10000.0
MIB = 2**20
MESH = pl.DeviceIdType.MESH
F32 = jnp.float32
BF16 = jnp.bfloat16
ANY = pl.BlockSpec(memory_space=pl.ANY)
VMEM = pl.BlockSpec(memory_space=pltpu.VMEM)
TP_ORDER = (4, 1, 3, 5, 7, 2, 6)
CHIP_ORDER = (2, 6, 1, 4, 3, 7, 5)


def dot_nn(left, right):
    return jnp.dot(left, right, preferred_element_type=F32)


def dot_nt(left, right):
    return lax.dot_general(left, right, (((1,), (1,)), ((), ())), preferred_element_type=F32)


def dot_tn(left, right):
    return lax.dot_general(left, right, (((0,), (0,)), ((), ())), preferred_element_type=F32)


def rms_scale(values):
    return lax.rsqrt(jnp.mean(values * values, axis=-1, keepdims=True) + EPSILON)


def norm_back(values, scaling, gradient):
    inner_mean = jnp.mean(gradient * values, axis=-1, keepdims=True)
    return scaling * (gradient - values * (scaling * scaling) * inner_mean)


def angle_tables(first, count):
    half_width = HD // 2
    frequency = ROPE_BASE ** (-jnp.arange(half_width).astype(F32) / half_width)
    positions = (first + jnp.arange(count)).astype(F32)
    angles = positions[:, None] * frequency[None, :]
    return jnp.cos(angles), jnp.sin(angles)


def rotate(values, cosine, sine):
    half_width = HD // 2
    lower_half = values[..., :half_width]
    upper_half = values[..., half_width:]
    cosine = cosine[:, None, :]
    sine = sine[:, None, :]
    return jnp.concatenate(
        [lower_half * cosine - upper_half * sine, upper_half * cosine + lower_half * sine], axis=-1
    )


def place():
    seq = lax.axis_index("seq")
    tp = lax.axis_index("tp")
    return seq, seq // 2, seq % 2, tp


def run_exchange(peers, jobs, locals_, send_sems, recv_sems):
    barrier = pltpu.get_barrier_semaphore()
    for peer in peers:
        pl.semaphore_signal(barrier, inc=1, device_id=peer, device_id_type=MESH)
    pl.semaphore_wait(barrier, len(peers))
    copies = []
    for number, (source, target, device) in enumerate(jobs):
        copy = pltpu.make_async_remote_copy(
            src_ref=source,
            dst_ref=target,
            send_sem=send_sems.at[number],
            recv_sem=recv_sems.at[number],
            device_id=device,
            device_id_type=MESH,
        )
        copy.start()
        copies.append(copy)
    for source, bounce, target, sem in locals_:
        copy = pltpu.make_async_copy(source, bounce, sem)
        copy.start()
        copy.wait()
        copy = pltpu.make_async_copy(bounce, target, sem)
        copy.start()
        copy.wait()
    for copy in copies:
        copy.wait()


def exchange(kernel, name, collective_id, ins, outs, copies, bounces):
    return pl.pallas_call(
        kernel,
        name=name,
        out_shape=outs,
        in_specs=[ANY] * len(ins),
        out_specs=[ANY] * len(outs),
        scratch_shapes=[
            pltpu.SemaphoreType.DMA((copies,)),
            pltpu.SemaphoreType.DMA((copies,)),
            pltpu.SemaphoreType.DMA,
        ]
        + [pltpu.VMEM(shape, dtype) for shape, dtype in bounces],
        compiler_params=pltpu.CompilerParams(
            collective_id=collective_id, has_side_effects=True, vmem_limit_bytes=16 * MIB
        ),
    )(*ins)


def tp_peers(seq, tp, order=TP_ORDER):
    return [(seq, lax.rem(tp + hop, TP)) for hop in order]


def chip_peers(chip, core, tp, order=CHIP_ORDER):
    return [(lax.rem(chip + hop, CHIPS) * 2 + core, tp) for hop in order]


def keys_kernel(
    kv, query, normed, out_w, kv_all, query_two, normed_other, w_all,
    send_sems, recv_sems, sem, kv_bounce, query_bounce, w_bounce,
):
    seq, chip, core, tp = place()
    partner = (chip * 2 + 1 - core, tp)
    peers = [partner]
    jobs = [(query.at[1 - core], query_two.at[core], partner)]
    jobs.append((kv.at[1 - core], kv_all.at[seq], partner))
    for other in chip_peers(chip, core, tp):
        peers.append(other)
        jobs.append((kv.at[core], kv_all.at[seq], other))
    for other in chip_peers(chip, 1 - core, tp):
        peers.append(other)
        jobs.append((kv.at[1 - core], kv_all.at[seq], other))
    for other in tp_peers(seq, tp):
        peers.append(other)
        jobs.append((out_w.at[other[1]], w_all.at[tp], other))
    jobs.append((normed, normed_other, partner))
    run_exchange(
        peers,
        jobs,
        [
            (kv.at[core], kv_bounce, kv_all.at[seq], sem),
            (query.at[core], query_bounce, query_two.at[core], sem),
            (out_w.at[tp], w_bounce, w_all.at[tp], sem),
        ],
        send_sems,
        recv_sems,
    )


def exchange_keys(kv, query, normed, out_w):
    return exchange(
        keys_kernel,
        "exchange_keys",
        1,
        (kv, query, normed, out_w),
        [
            jax.ShapeDtypeStruct((2 * CHIPS, FR, 2 * HD), BF16),
            jax.ShapeDtypeStruct((2, FR, HD), BF16),
            jax.ShapeDtypeStruct(normed.shape, BF16),
            jax.ShapeDtypeStruct(out_w.shape, BF16),
        ],
        24,
        [((FR, 2 * HD), BF16), ((FR, HD), BF16), (out_w.shape[1:], BF16)],
    )


def attended_kernel(source, target, send_sems, recv_sems, sem, bounce):
    seq, chip, core, tp = place()
    slot = tp * 2 + core
    partner_seq = chip * 2 + 1 - core
    peers = [(partner_seq, tp)] + tp_peers(seq, tp) + tp_peers(partner_seq, tp)
    own = pl.ds(core * FR, FR)
    other = pl.ds((1 - core) * FR, FR)
    rows = [other] + [own] * (TP - 1) + [other] * (TP - 1)
    jobs = [(source.at[part], target.at[slot], peer) for part, peer in zip(rows, peers)]
    run_exchange(
        peers, jobs, [(source.at[own], bounce, target.at[slot], sem)], send_sems, recv_sems
    )


def exchange_attended(attended):
    return exchange(
        attended_kernel,
        "exchange_attended",
        2,
        (attended,),
        [jax.ShapeDtypeStruct((2 * TP, FR, HD), BF16)],
        15,
        [((FR, HD), BF16)],
    )[0]


def scatter_kernel(source, target, send_sems, recv_sems, sem, bounce):
    seq, chip, core, tp = place()
    peers = tp_peers(seq, tp)
    jobs = [(source.at[peer[1]], target.at[tp], peer) for peer in peers]
    run_exchange(
        peers, jobs, [(source.at[tp], bounce, target.at[tp], sem)], send_sems, recv_sems
    )


def gather_kernel(source, target, send_sems, recv_sems, sem, bounce):
    seq, chip, core, tp = place()
    peers = tp_peers(seq, tp)
    jobs = [(source, target.at[tp], peer) for peer in peers]
    run_exchange(peers, jobs, [(source, bounce, target.at[tp], sem)], send_sems, recv_sems)


def exchange_latent(parts):
    return exchange(
        scatter_kernel,
        "exchange_latent",
        3,
        (parts,),
        [jax.ShapeDtypeStruct(parts.shape, parts.dtype)],
        7,
        [(parts.shape[1:], parts.dtype)],
    )[0]


def exchange_message(message):
    return exchange(
        gather_kernel,
        "exchange_message",
        4,
        (message,),
        [jax.ShapeDtypeStruct((TP,) + message.shape, message.dtype)],
        7,
        [(message.shape, message.dtype)],
    )[0]


def cotangent_kernel(source, target, send_sems, recv_sems, sem, bounce):
    seq, chip, core, tp = place()
    partner_seq = chip * 2 + 1 - core
    peers = [(partner_seq, tp)] + tp_peers(seq, tp) + tp_peers(partner_seq, tp)
    heads = [1 - core] + [core] * (TP - 1) + [1 - core] * (TP - 1)
    jobs = [
        (source.at[peer[1] * 2 + head], target.at[core, tp], peer)
        for head, peer in zip(heads, peers)
    ]
    run_exchange(
        peers,
        jobs,
        [(source.at[tp * 2 + core], bounce, target.at[core, tp], sem)],
        send_sems,
        recv_sems,
    )


def exchange_cotangent(parts):
    return exchange(
        cotangent_kernel,
        "exchange_cotangent",
        5,
        (parts,),
        [jax.ShapeDtypeStruct((2, TP, FR, HD), BF16)],
        15,
        [((FR, HD), BF16)],
    )[0]


def key_grads_kernel(source, target, send_sems, recv_sems, sem, bounce):
    seq, chip, core, tp = place()
    peers = chip_peers(chip, core, tp)
    jobs = [(source.at[peer[0] // 2], target.at[chip], peer) for peer in peers]
    run_exchange(
        peers, jobs, [(source.at[chip], bounce, target.at[chip], sem)], send_sems, recv_sems
    )


def exchange_key_grads(parts):
    return exchange(
        key_grads_kernel,
        "exchange_key_grads",
        6,
        (parts,),
        [jax.ShapeDtypeStruct(parts.shape, parts.dtype)],
        7,
        [(parts.shape[1:], parts.dtype)],
    )[0]


def weights_kernel(source, target, send_sems, recv_sems, sem, bounce):
    seq, chip, core, tp = place()
    partner = (chip * 2 + 1 - core, tp)
    peers = [partner] + chip_peers(chip, core, tp) + chip_peers(chip, 1 - core, tp)
    jobs = [(source.at[peer[0]], target.at[core, chip], peer) for peer in peers]
    run_exchange(
        peers, jobs, [(source.at[seq], bounce, target.at[core, chip], sem)], send_sems, recv_sems
    )


def exchange_weights(parts):
    return exchange(
        weights_kernel,
        "exchange_weights",
        7,
        (parts,),
        [jax.ShapeDtypeStruct((2, CHIPS) + parts.shape[1:], parts.dtype)],
        15,
        [(parts.shape[1:], parts.dtype)],
    )[0]


def compute(kernel, name, ins, outs, scratch=(), limit=48):
    return pl.pallas_call(
        kernel,
        name=name,
        out_shape=outs,
        in_specs=[VMEM] * len(ins),
        out_specs=[VMEM] * len(outs),
        scratch_shapes=list(scratch),
        compiler_params=pltpu.CompilerParams(vmem_limit_bytes=limit * MIB),
    )(*ins)


def attend_kernel(kv_ref, query_ref, out_ref, prob_ref, out_t_ref, inverse_ref, score_ref):
    chip = lax.axis_index("seq") // 2
    blocks = 2 * chip + 2
    query = query_ref[...].reshape(FR2, HD)
    key_at = lax.broadcasted_iota(jnp.int32, (FR, FR2), 0)
    query_at = lax.broadcasted_iota(jnp.int32, (FR, FR2), 1) + chip * FR2

    def scores(block, top):
        score = dot_nt(kv_ref[block][:, :HD], query) * (1.0 / math.sqrt(HD))
        score = jnp.where(key_at + block * FR <= query_at, score, MASKED)
        score_ref[block] = score
        return jnp.maximum(top, jnp.max(score, axis=0, keepdims=True))

    top = lax.fori_loop(0, blocks, scores, jnp.full((1, FR2), MASKED, F32))

    def weigh(block, carry):
        total, mixed = carry
        prob = jnp.exp(score_ref[block] - top)
        total = total + jnp.sum(prob, axis=0, keepdims=True)
        prob = prob.astype(BF16)
        prob_ref[block] = prob
        return total, mixed + dot_tn(kv_ref[block][:, HD:], prob)

    total, mixed = lax.fori_loop(
        0, blocks, weigh, (jnp.zeros((1, FR2), F32), jnp.zeros((HD, FR2), F32))
    )
    inverse = 1.0 / total
    mixed = mixed * inverse
    out_t_ref[...] = mixed
    inverse_ref[...] = inverse
    out_ref[...] = mixed.T.astype(BF16)


def attend(kv_all, query_two):
    return compute(
        attend_kernel,
        "attend",
        (kv_all, query_two),
        [
            jax.ShapeDtypeStruct((FR2, HD), BF16),
            jax.ShapeDtypeStruct((2 * CHIPS, FR, FR2), BF16),
            jax.ShapeDtypeStruct((HD, FR2), F32),
            jax.ShapeDtypeStruct((1, FR2), F32),
        ],
        [pltpu.VMEM((2 * CHIPS, FR, FR2), F32)],
    )


def merge_kernel(att_ref, w_ref, hidden_ref, depth_in_ref, merged_ref, part_ref):
    merged = hidden_ref[...].astype(F32)
    for tp in range(TP):
        pair = jnp.concatenate([att_ref[2 * tp], att_ref[2 * tp + 1]], axis=1)
        merged = merged + dot_nt(pair, w_ref[tp])
    merged_ref[...] = merged
    squares = jnp.sum(merged * merged, axis=-1, keepdims=True)
    latent = dot_nn(merged.astype(BF16), depth_in_ref[...])
    part_ref[:, :, :DD] = latent.reshape(TP, FR // TP, DD)
    part_ref[:, :, DD:] = jnp.broadcast_to(squares, (FR, HD)).reshape(TP, FR // TP, HD)


def merge(att_all, w_all, hidden_slice, depth_in_slice):
    return compute(
        merge_kernel,
        "merge",
        (att_all, w_all, hidden_slice, depth_in_slice),
        [
            jax.ShapeDtypeStruct((FR, NS), F32),
            jax.ShapeDtypeStruct((TP, FR // TP, DD + HD), F32),
        ],
    )


def depth_kernel(width, loss_scale, part_ref, stack_ref, before_ref, code_ref, message_ref, grad_ref, prob_ref):
    frames = part_ref.shape[1]
    books = before_ref.shape[0] // frames
    tokens = frames * books
    qkv_rows = stack_ref[: 3 * DD]
    out_rows = stack_ref[3 * DD : 4 * DD]
    head_rows = stack_ref[4 * DD : 4 * DD + VOCAB]
    embed_rows = stack_ref[4 * DD + VOCAB :]
    total = jnp.sum(part_ref[...], axis=0)
    raw = total[:, :DD]
    scale_in = lax.rsqrt(total[:, DD : DD + 1] * (1.0 / width) + EPSILON)
    latent = raw * scale_in
    latent = jnp.broadcast_to(latent[:, None, :], (frames, books, DD)).reshape(tokens, DD)
    vocab_at = lax.broadcasted_iota(jnp.int32, (tokens, VOCAB), 1)
    hot = jnp.where(before_ref[...] == vocab_at, 1.0, 0.0).astype(BF16)
    stream = latent + dot_nn(hot, embed_rows)
    stream_scale = rms_scale(stream)
    stream_norm = (stream * stream_scale).astype(BF16)
    proj = dot_nt(stream_norm, qkv_rows).astype(BF16)
    row_at = lax.broadcasted_iota(jnp.int32, (tokens, tokens), 0)
    col_at = lax.broadcasted_iota(jnp.int32, (tokens, tokens), 1)
    allowed = (row_at // books == col_at // books) & (col_at <= row_at)
    depth_scale = 1.0 / math.sqrt(DHD)
    mixed = []
    for head in range(DD // DHD):
        low = head * DHD
        queries = proj[:, low : low + DHD]
        keys = proj[:, DD + low : DD + low + DHD]
        values = proj[:, 2 * DD + low : 2 * DD + low + DHD]
        scores = jnp.where(allowed, dot_nt(queries, keys) * depth_scale, MASKED)
        weights = jnp.exp(scores - jnp.max(scores, axis=-1, keepdims=True))
        probs = weights / jnp.sum(weights, axis=-1, keepdims=True)
        prob_ref[head] = probs
        mixed.append(dot_nn(probs.astype(BF16), values))
    mixed = jnp.concatenate(mixed, axis=1).astype(BF16)
    resid = stream + dot_nt(mixed, out_rows)
    resid_scale = rms_scale(resid)
    resid_norm = (resid * resid_scale).astype(BF16)
    logits = dot_nt(resid_norm, head_rows)
    weights = jnp.exp(logits - jnp.max(logits, axis=-1, keepdims=True))
    logit_probs = weights / jnp.sum(weights, axis=-1, keepdims=True)
    target = jnp.where(code_ref[...] == vocab_at, 1.0, 0.0)
    logit_grad = ((logit_probs - target) * loss_scale).astype(BF16)
    grad_ref[4 * DD : 4 * DD + VOCAB] = dot_tn(logit_grad, resid_norm).astype(BF16)
    resid_grad = norm_back(resid, resid_scale, dot_nn(logit_grad, head_rows))
    resid_round = resid_grad.astype(BF16)
    grad_ref[3 * DD : 4 * DD] = dot_tn(resid_round, mixed).astype(BF16)
    mixed_grad = dot_nn(resid_round, out_rows).astype(BF16)
    query_grad, key_grad, value_grad = [], [], []
    for head in range(DD // DHD):
        low = head * DHD
        queries = proj[:, low : low + DHD]
        keys = proj[:, DD + low : DD + low + DHD]
        values = proj[:, 2 * DD + low : 2 * DD + low + DHD]
        probs = prob_ref[head]
        mix_grad = mixed_grad[:, low : low + DHD]
        value_grad.append(dot_tn(probs.astype(BF16), mix_grad))
        prob_grad = dot_nt(mix_grad, values)
        inner = jnp.sum(probs * prob_grad, axis=-1, keepdims=True)
        score_grad = (probs * (prob_grad - inner) * depth_scale).astype(BF16)
        query_grad.append(dot_nn(score_grad, keys))
        key_grad.append(dot_tn(score_grad, queries))
    proj_grad = jnp.concatenate(query_grad + key_grad + value_grad, axis=1).astype(BF16)
    grad_ref[: 3 * DD] = dot_tn(proj_grad, stream_norm).astype(BF16)
    stream_grad = resid_grad + norm_back(stream, stream_scale, dot_nn(proj_grad, qkv_rows))
    grad_ref[4 * DD + VOCAB :] = dot_tn(hot, stream_grad.astype(BF16)).astype(BF16)
    latent_grad = jnp.sum(stream_grad.reshape(frames, books, DD), axis=1)
    latent_grad = latent_grad.astype(BF16).astype(F32)
    inner = jnp.sum(latent_grad * raw, axis=-1, keepdims=True) * (1.0 / width)
    pull = scale_in * scale_in * scale_in * inner
    coarse = pull.astype(BF16)
    fine = (pull - coarse.astype(F32)).astype(BF16)
    message_ref[:, :DD] = (latent_grad * scale_in).astype(BF16)
    message_ref[:, DD : DD + HD] = jnp.broadcast_to(coarse, (frames, HD))
    message_ref[:, DD + HD :] = jnp.broadcast_to(fine, (frames, HD))


def depth(parts, stack, before, codes, width, loss_scale):
    tokens = before.shape[0]
    return compute(
        functools.partial(depth_kernel, width, loss_scale),
        "depth",
        (parts, stack, before, codes),
        [
            jax.ShapeDtypeStruct((parts.shape[1], DD + 2 * HD), BF16),
            jax.ShapeDtypeStruct(stack.shape, BF16),
        ],
        [pltpu.VMEM((DD // DHD, tokens, tokens), F32)],
    )


def unmerge_kernel(message_ref, merged_ref, depth_in_ref, w_ref, merged_grad_ref, part_ref):
    message = message_ref[...].reshape(FR, DD + 2 * HD)
    pull = message[:, DD : DD + 1].astype(F32) + message[:, DD + HD : DD + HD + 1].astype(F32)
    gradient = dot_nt(message[:, :DD], depth_in_ref[...]) - merged_ref[...] * pull
    gradient = gradient.astype(BF16)
    merged_grad_ref[...] = gradient
    for tp in range(TP):
        pair = dot_nn(gradient, w_ref[tp]).astype(BF16)
        part_ref[2 * tp] = pair[:, :HD]
        part_ref[2 * tp + 1] = pair[:, HD:]


def unmerge(messages, merged, depth_in_slice, w_all):
    return compute(
        unmerge_kernel,
        "unmerge",
        (messages, merged, depth_in_slice, w_all),
        [
            jax.ShapeDtypeStruct((FR, NS), BF16),
            jax.ShapeDtypeStruct((2 * TP, FR, HD), BF16),
        ],
    )


def side_kernel(messages_ref, merged_ref, merged_grad_ref, att_ref, win_ref, out_ref):
    message = messages_ref[...].reshape(FR, DD + 2 * HD)
    win_ref[...] = dot_tn(merged_ref[...].astype(BF16), message[:, :DD]).astype(BF16)
    gradient = merged_grad_ref[...]
    for tp in range(TP):
        pair = jnp.concatenate([att_ref[2 * tp], att_ref[2 * tp + 1]], axis=1)
        out_ref[:, tp] = dot_tn(gradient, pair).astype(BF16)


def side_grads(messages, merged, merged_grad, att_all):
    return compute(
        side_kernel,
        "side_grads",
        (messages, merged, merged_grad, att_all),
        [
            jax.ShapeDtypeStruct((NS, DD), BF16),
            jax.ShapeDtypeStruct((NS, TP, 2 * HD), BF16),
        ],
    )


def attend_back_kernel(
    prob_ref, kv_ref, query_ref, part_ref, out_t_ref, inverse_ref, cos_ref, sin_ref, grad_ref, query_grad_ref
):
    chip = lax.axis_index("seq") // 2
    blocks = 2 * chip + 2
    grad_ref[...] = jnp.zeros_like(grad_ref)
    query = query_ref[...].reshape(FR2, HD)
    gradient = jnp.sum(part_ref[...].astype(F32), axis=1).reshape(FR2, HD)
    gradient = gradient.astype(BF16).astype(F32)
    gradient_t = (gradient.T * inverse_ref[...]).astype(BF16)
    wide_t = gradient_t.astype(F32)
    inner = jnp.sum(wide_t * out_t_ref[...], axis=0, keepdims=True)
    gradient = wide_t.T.astype(BF16)
    scale = 1.0 / math.sqrt(HD)

    def step(block, query_grad):
        prob = prob_ref[block]
        score_grad = prob.astype(F32) * (dot_nn(kv_ref[block, :, HD:], gradient_t) - inner)
        score_grad = score_grad.astype(BF16)
        grad_ref[block, :, :HD] = (dot_nn(score_grad, query) * scale).astype(BF16)
        grad_ref[block, :, HD:] = dot_nn(prob, gradient).astype(BF16)
        return query_grad + dot_tn(kv_ref[block, :, :HD], score_grad)

    query_grad = lax.fori_loop(0, blocks, step, jnp.zeros((HD, FR2), F32)) * scale

    query_grad = query_grad.T
    lower, upper = query_grad[:, : HD // 2], query_grad[:, HD // 2 :]
    cosine, sine = cos_ref[...], sin_ref[...]
    query_grad_ref[...] = jnp.concatenate(
        [lower * cosine + upper * sine, upper * cosine - lower * sine], axis=1
    ).astype(BF16)


def attend_back(probs, kv_all, query_two, parts, out_t, inverse, cosine, sine):
    return compute(
        attend_back_kernel,
        "attend_back",
        (probs, kv_all, query_two, parts, out_t, inverse, cosine, sine),
        [
            jax.ShapeDtypeStruct((2 * CHIPS, FR, 2 * HD), BF16),
            jax.ShapeDtypeStruct((FR2, HD), BF16),
        ],
    )


def weight_kernel(part_ref, query_grad_ref, cos_ref, sin_ref, normed_ref, other_ref, out_ref):
    core = lax.axis_index("seq") % 2
    total = jnp.sum(part_ref[...].astype(F32), axis=0)
    lower, upper = total[:, : HD // 2], total[:, HD // 2 : HD]
    cosine, sine = cos_ref[...], sin_ref[...]
    proj = jnp.concatenate(
        [
            query_grad_ref[...].astype(F32),
            lower * cosine + upper * sine,
            upper * cosine - lower * sine,
            total[:, HD:],
        ],
        axis=1,
    )
    proj_t = proj.T
    first, second = proj_t[:, :FR], proj_t[:, FR:]
    own = jnp.where(core == 0, first, second).astype(BF16)
    other = jnp.where(core == 0, second, first).astype(BF16)
    for piece in range(2 * CHIPS):
        low = piece * FR
        term = dot_nn(own, normed_ref[:, low : low + FR])
        term = term + dot_nn(other, other_ref[:, low : low + FR])
        out_ref[piece] = term.astype(BF16)


def weight_terms(parts, query_grad, cosine, sine, normed, normed_other):
    return compute(
        weight_kernel,
        "weight_terms",
        (parts, query_grad, cosine, sine, normed, normed_other),
        [jax.ShapeDtypeStruct((2 * CHIPS, 3 * HD, FR), BF16)],
    )[0]


def weight_sum_kernel(part_ref, out_ref):
    for head in range(2):
        total = jnp.sum(part_ref[head].astype(F32), axis=0).T
        for kind in range(3):
            out_ref[kind, :, head * HD : (head + 1) * HD] = total[:, kind * HD : (kind + 1) * HD]


def weight_sum(parts):
    return compute(
        weight_sum_kernel,
        "weight_sum",
        (parts,),
        [jax.ShapeDtypeStruct((3, FR, 2 * HD), F32)],
    )[0]


def per_device(hidden_in, temporal_weight_stack, depth_in, depth_stack, audio_codes):
    seq_index = lax.axis_index("seq")
    tp_index = lax.axis_index("tp")
    chip = seq_index // 2
    width = hidden_in.shape[1]
    depth_frames, book_count = audio_codes.shape
    seq_count = 2 * CHIPS
    total_frames = FR * seq_count
    loss_scale = 1.0 / math.sqrt(total_frames * book_count)

    hidden_full = hidden_in.astype(F32)
    normed = (hidden_full * rms_scale(hidden_full)).astype(BF16)
    projected = jnp.einsum(
        "wo,obu->wbu", normed, temporal_weight_stack[:, :3, :], preferred_element_type=F32
    )
    cosine, sine = angle_tables(seq_index * FR, FR)
    query = rotate(projected[:, 0].reshape(FR, 2, HD), cosine, sine).astype(BF16)
    key = rotate(projected[:, 1].reshape(FR, 2, HD), cosine, sine).astype(BF16)
    value = projected[:, 2].reshape(FR, 2, HD).astype(BF16)
    kv = jnp.concatenate([key, value], axis=-1).transpose(1, 0, 2)
    query = query.transpose(1, 0, 2)
    out_w = temporal_weight_stack[:, 3, :].reshape(seq_count, TP, -1, 2 * HD)
    out_w = out_w.transpose(1, 0, 2, 3).reshape(TP, NS, 2 * HD)
    kv_all, query_two, normed_other, w_all = exchange_keys(kv, query, normed, out_w)

    hidden_slice = lax.dynamic_index_in_dim(
        hidden_in.reshape(FR, seq_count, TP, -1), tp_index, 2, keepdims=False
    ).reshape(FR, NS)
    depth_in_slice = lax.dynamic_index_in_dim(
        depth_in.reshape(seq_count, TP, -1, DD), tp_index, 1, keepdims=False
    ).reshape(NS, DD)
    attended, probs, out_t, inverse = attend(kv_all, query_two)
    att_all = exchange_attended(attended)
    merged, latent_parts = merge(att_all, w_all, hidden_slice, depth_in_slice)
    latent_parts = exchange_latent(latent_parts)
    before = jnp.concatenate(
        [jnp.full((depth_frames, 1), -1, jnp.int32), audio_codes[:, :-1]], axis=1
    ).reshape(-1, 1)
    message, grad_depth = depth(
        latent_parts, depth_stack, before, audio_codes.reshape(-1, 1), width, loss_scale
    )
    messages = exchange_message(message)
    merged_grad, cotangent_parts = unmerge(messages, merged, depth_in_slice, w_all)
    cotangent_parts = exchange_cotangent(cotangent_parts)

    grad_depth = grad_depth.reshape(seq_count, TP, -1, DD).transpose(1, 0, 2, 3)
    grad_depth = lax.psum_scatter(grad_depth, "tp", scatter_dimension=0, tiled=True)[0]
    grad_depth = lax.psum_scatter(grad_depth, "seq", scatter_dimension=0, tiled=True)[0]
    grad_win, grad_out = side_grads(messages, merged, merged_grad, att_all)
    grad_win = lax.psum_scatter(grad_win, "seq", scatter_dimension=0, tiled=True)
    grad_out = lax.psum_scatter(grad_out, "seq", scatter_dimension=0, tiled=True)
    grad_out = lax.all_to_all(grad_out, "tp", 1, 0, tiled=True).reshape(FR, 1, 2 * HD)

    cosine, sine = angle_tables(chip * FR2, FR2)
    key_parts, query_grad = attend_back(
        probs, kv_all, query_two, cotangent_parts, out_t, inverse, cosine, sine
    )
    key_parts = exchange_key_grads(key_parts.reshape(CHIPS, FR2, 2 * HD))
    parts = weight_terms(key_parts, query_grad, cosine, sine, normed, normed_other)
    grad_in = weight_sum(exchange_weights(parts))
    grad_temporal = jnp.concatenate([grad_in.transpose(1, 0, 2), grad_out.astype(F32)], axis=1)
    return grad_temporal, grad_win.astype(F32), grad_depth.astype(F32)


def solution(mesh):
    in_specs = (P("seq", None), P(None, None, "tp"), P(), P(), P(("seq", "tp"), None))
    out_specs = (P("seq", None, "tp"), P(("seq", "tp"), None), P(("seq", "tp"), None))
    return jax.shard_map(
        per_device, mesh=mesh, in_specs=in_specs, out_specs=out_specs, check_vma=False
    )
```

time: 1170 us -> 442 us (0.38); the launches traced: 1150 us -> 440 us
  waiting for transfers between devices: 933 us -> 132 us
  Pallas kernels: 0 us -> 232 us
  matrix products: 115 us -> 6.23 us
  other arithmetic: 39.8 us -> 8.54 us
    reduce_scatter x4, waiting for transfers between devices: 839 us -> 131 us  [the longest x1 71.5 us: per_device(): lax.psum_scatter(grad_out, 'seq', scatter_dimension=0, tiled=True)]
    pallas_call x0 -> x15, Pallas kernels: none -> 232 us  [the longest x7 201 us: exchange(): pl.pallas_call(kernel, name=name, out_shape=outs, in_specs=[ANY] * len(in...]
    all_gather x2 -> x0, waiting for transfers between devices: 93.5 us -> none  [the longest x1 53.4 us: per_device(): all_pairs = lax.all_gather(local_pairs, 'seq', axis=0, tiled=True)]
    dot_general x28 -> x1, matrix products: 99.4 us -> 6.23 us  [per_device(): jnp.einsum('wo,obu->wbu', normed, temporal_weight_stack[:, :3, :], prefer...]
    unnamed x74 -> x59, local copies, waits for them, and re-layouts: 8.61 us -> 26.6 us
    concatenate x5 -> x1, other arithmetic: 16.1 us -> 0.08 us  [per_device(): jnp.concatenate([grad_in.transpose(1, 0, 2), grad_out.astype(F32)], axis=1)]
    sub x2 -> x0, matrix products: 13.5 us -> none  [masked_softmax(): weights = jnp.where(allowed, jnp.exp(scores - row_top), 0.0)]
  transfers between devices with their start and end apart: 6 -> 5, of which waited for: 6 -> 3; matrix products, arithmetic and copies ran while one was open for 4% -> 2% of each run, Pallas kernels for 0% -> 30%
where the time goes in v2:
time: 442 us; the launch traced here: 440 us
  Pallas kernels  232 us (52%)
  waiting for transfers between devices  132 us (30%)
  local copies, waits for them, and re-layouts  41.2 us (9%)
  between operations  14.3 us (3%)
  other arithmetic  8.54 us (2%)
  matrix products  6.23 us (1%)
  starting transfers between devices  4.89 us (1%)
    pallas_call x7, Pallas kernels, exchange(): pl.pallas_call(kernel, name=name, out_shape=outs, in_specs=[ANY] * len(in...  201 us
    reduce_scatter x1, waiting for transfers between devices, per_device(): lax.psum_scatter(grad_out, 'seq', scatter_dimension=0, tiled=True)  71.5 us
    reduce_scatter x1, waiting for transfers between devices, per_device(): lax.psum_scatter(grad_depth, 'tp', scatter_dimension=0, tiled=True)[0]  38.1 us
    pallas_call x8, Pallas kernels, compute(): pl.pallas_call(kernel, name=name, out_shape=outs, in_specs=[VMEM] * len(i...  31.4 us
    unnamed x59, local copies, waits for them, and re-layouts  26.6 us
    reduce_scatter x1, waiting for transfers between devices, per_device(): lax.psum_scatter(grad_depth, 'seq', scatter_dimension=0, tiled=True)[0]  21.8 us
  transfers between devices with their start and end apart: 5, of which 3 were waited for; matrix products, arithmetic and copies ran while one was open for 2% of the time, Pallas kernels for 30%

profile of v2, /device:TPU:1, one launch (start us, length us, event | category | flops | bytes accessed | tf_op | source)
XLA Modules:
  0.0 439.7 jit_solution(14257883453105249588)
XLA Ops:
  7.2 2.2 fusion.2
  10.1 6.2 %fusion = f32[256,3,256]{0,2,1:T(8,128)S(1)} fusion(bf16[4096,3,256]{2,1,0:T(4,128)(2,1)} %bitcast.47, bf16[256,4096]{1,0:T(8,128)(2,1)S(1)} %fusion.3.normed.normed_ref), kind=kOutput, calls=%fused_computation | convolution fusion | flops 1610612736 | bytes 9175040 | tf_op jit(solution)/shard_map/wo,obu->wbu/dot_general | solution.py:650
  16.4 5.4 %slice.39 = bf16[4096,1,256]{2,1,0:T(2,128)(2,1)} slice(bf16[4096,4,256]{2,1,0:T(4,128)(2,1)S(1)} %bitcast.49), slice={[0:4096], [3:4], [0:256]} | slice | bytes 4194304 | tf_op jit(solution)/shard_map/slice | solution.py:659
  21.9 4.1 copy.42
  26.7 2.5 copy.57
  30.4 56.9 %exchange_keys.1 = (bf16[16,256,256]{2,1,0:T(8,128)(2,1)S(1)}, bf16[2,256,128]{2,1,0:T(8,128)(2,1)S(1)}, bf16[256,4096]{1,0:T(8,128)(2,1)S(1)}, bf16[8,512,256]{2,1,0:T(8,128)(2,1)S(1)}) custom-call(bf16[2,256,256]{2,1,0:T(8,128)(2,1)S(1)} %maximum_bitcast_fusion.kv, bf16[2,256,128]{2,1,0:T(8,128)(2,1)S(1)} %maximum_bitcast_fusion.1.query, ...), custom_call_target="tpu_custom_call" | custom-call | tf_op jit(solution)/shard_map/exchange_keys/pallas_call | solution.py:109
  87.3 1.3 copy-done.2
  88.6 1.4 copy-done.9
  89.9 3.3 attend.1
  93.2 0.7 copy-done.17
  93.9 17.1 %exchange_attended.1.att_ref = bf16[16,256,128]{2,1,0:T(8,128)(2,1)S(1)} custom-call(bf16[512,128]{1,0:T(8,128)(2,1)S(1)} %get-tuple-element.24.source), custom_call_target="tpu_custom_call" | custom-call | tf_op jit(solution)/shard_map/exchange_attended/pallas_call | solution.py:109
  111.1 1.7 constant_dynamic-slice_fusion.1
  112.7 1.1 copy.44.hidden_ref
  113.9 1.1 constant_dynamic-slice_fusion
  115.0 1.8 copy-done.3
  116.7 0.9 merge.1
  117.7 0.8 copy-done.10
  118.5 11.6 %exchange_latent.1.part_ref = f32[8,32,640]{2,1,0:T(8,128)S(1)} custom-call(f32[8,32,640]{2,1,0:T(8,128)S(1)} %get-tuple-element.26.source), custom_call_target="tpu_custom_call" | custom-call | tf_op jit(solution)/shard_map/exchange_latent/pallas_call | solution.py:109
  130.2 0.8 copy-done.7
  131.9 0.8 reshape.140.code_ref
  132.8 1.1 copy-done.8
  133.8 12.2 %depth.1 = (bf16[32,768]{1,0:T(8,128)(2,1)S(1)}, bf16[4096,512]{1,0:T(8,128)(2,1)S(1)}) custom-call(f32[8,32,640]{2,1,0:T(8,128)S(1)} %copy-done.8, bf16[4096,512]{1,0:T(8,128)(2,1)} %stack_ref.1, s32[256,1]{1,0:T(8,128)S(1)} %reshape.139.before_ref, s32[256,1]{1,0:T(8,128)S(1)} %reshape.140.code_ref), custom_call_target="tpu_custom_call" | custom-call | tf_op jit(solution)/shard_map/depth/pallas_call | solution.py:324
  146.1 2.4 copy.63
  149.2 7.8 %exchange_message.1.message_ref.messages_ref = bf16[8,32,768]{2,1,0:T(8,128)(2,1)S(1)} custom-call(bf16[32,768]{1,0:T(8,128)(2,1)S(1)} %copy-done.20), custom_call_target="tpu_custom_call" | custom-call | tf_op jit(solution)/shard_map/exchange_message/pallas_call | solution.py:109
  157.1 1.6 copy-done.4
  158.7 1.0 copy-done.6
  159.7 1.0 copy-done.11
  160.8 1.0 unmerge.1
  161.7 1.0 copy-done.14
  162.7 3.3 side_grads.1
  166.0 1.3 copy-done.13
  167.3 0.8 copy-done.16
  168.9 38.1 %reduce-scatter.9.cloned.1.call-done = bf16[1,16,32,512]{3,2,1,0:T(8,128)(2,1)} async-done(((bf16[8,16,32,512]{3,2,1,0:T(8,128)(2,1)}), bf16[1,16,32,512]{3,2,1,0:T(8,128)(2,1)}) %reduce-scatter.9.cloned.1.call-update) | async-done | bytes 524304 | tf_op jit(solution)/shard_map/reduce_scatter | solution.py:684
  207.1 71.5 %reduce-scatter.5.cloned.1.call-done = bf16[32,8,256]{2,1,0:T(8,128)(2,1)} async-done(((bf16[512,8,256]{2,1,0:T(8,128)(2,1)}), bf16[32,8,256]{2,1,0:T(8,128)(2,1)}) %reduce-scatter.5.cloned.1.call-update) | async-done | bytes 131088 | tf_op jit(solution)/shard_map/reduce_scatter | solution.py:688
  278.6 1.6 copy.49
  280.1 4.5 %all-to-all-start = ((bf16[32,8,256]{2,0,1:T(8,128)(2,1)}), bf16[32,8,256]{2,0,1:T(8,128)(2,1)}, u32[]{:S(2)}, u32[]{:S(2)}) async-start(bf16[32,8,256]{2,0,1:T(8,128)(2,1)} %copy.49), calls=%async_computation.1 | async-start | bytes 262144 | tf_op jit(solution)/shard_map/all_to_all | solution.py:689
  284.7 1.0 multiply_sine_fusion
  285.7 20.3 %exchange_cotangent.1.part_ref = bf16[2,8,256,128]{3,2,1,0:T(8,128)(2,1)S(1)} custom-call(bf16[16,256,128]{2,1,0:T(8,128)(2,1)S(1)} %copy-done.15), custom_call_target="tpu_custom_call" | custom-call | tf_op jit(solution)/shard_map/exchange_cotangent/pallas_call | solution.py:109
  306.0 4.7 %attend_back.1 = (bf16[16,256,256]{2,1,0:T(8,128)(2,1)S(1)}, bf16[512,128]{1,0:T(8,128)(2,1)S(1)}) custom-call(bf16[16,256,512]{2,1,0:T(8,128)(2,1)} %get-tuple-element.23.prob_ref, bf16[16,256,256]{2,1,0:T(8,128)(2,1)} %copy-done.1, bf16[2,256,128]{2,1,0:T(8,128)(2,1)S(1)} %get-tuple-element.22.query_ref, ...), custom_call_target="tpu_custom_call" | custom-call | tf_op jit(solution)/shard_map/attend_back/pallas_call | solution.py:324
  310.7 40.0 %exchange_key_grads.1.part_ref = bf16[8,512,256]{2,1,0:T(8,128)(2,1)S(1)} custom-call(bf16[8,512,256]{2,1,0:T(8,128)(2,1)S(1)} %bitcast.43), custom_call_target="tpu_custom_call" | custom-call | tf_op jit(solution)/shard_map/exchange_key_grads/pallas_call | solution.py:109
  350.8 5.5 %weight_terms.1.source = bf16[16,384,256]{2,1,0:T(8,128)(2,1)} custom-call(bf16[8,512,256]{2,1,0:T(8,128)(2,1)S(1)} %exchange_key_grads.1.part_ref, bf16[512,128]{1,0:T(8,128)(2,1)S(1)} %get-tuple-element.33.query_grad_ref, f32[512,64]{1,0:T(8,128)S(1)} %get-tuple-element.61.cos_ref, f32[512,64]{1,0:T(8,128)S(1)} %get-tuple-element.60.sin_ref, ...), custom_call_target="tpu_custom_call" | custom-call | tf_op jit(solution)/shard_map/weight_terms/pallas_call | solution.py:324
  356.3 1.9 copy-done
  358.2 47.2 %exchange_weights.1.part_ref = bf16[2,8,384,256]{3,2,1,0:T(8,128)(2,1)S(1)} custom-call(bf16[16,384,256]{2,1,0:T(8,128)(2,1)S(1)} %copy-done), custom_call_target="tpu_custom_call" | custom-call | tf_op jit(solution)/shard_map/exchange_weights/pallas_call | solution.py:109
  405.9 1.4 convert_element_type.75
  407.3 0.9 bitcast_convert_fusion
  408.3 1.6 copy.51
  410.0 21.8 %reduce-scatter.11.cloned.1.call-done = bf16[1,32,512]{2,1,0:T(8,128)(2,1)} async-done(((bf16[16,32,512]{2,1,0:T(8,128)(2,1)}), bf16[1,32,512]{2,1,0:T(8,128)(2,1)}) %reduce-scatter.11.cloned.1.call-update) | async-done | bytes 32784 | tf_op jit(solution)/shard_map/reduce_scatter | solution.py:685
  431.7 1.4 bitcast_convert_fusion.1
  (72 shorter events, 5.6 us)
Async XLA Ops:
  7.2 199.9 %reduce-scatter.9.cloned.1.call-start = ((), (), s32[]{:S(2)}) async-start(), calls=%async_computation.7 | async-start | bytes 4718592 | tf_op jit(solution)/shard_map/reduce_scatter | solution.py:684
  7.2 2.3 copy-start.21
  9.5 6.9 %slice-start = ((s8[8388608]{0:T(1024)(128)(4,1)}), s8[4194304]{0:T(1024)(128)(4,1)S(1)}, s32[]{:S(2)}) async-start(s8[8388608]{0:T(1024)(128)(4,1)} %bitcast.48), calls=%async_computation.9 | async-start | bytes 8388608
  10.1 6.3 %slice-start.1 = ((s8[8388608]{0:T(1024)(128)(4,1)}), s8[4194304]{0:T(1024)(128)(4,1)S(1)}, s32[]{:S(2)}) async-start(s8[8388608]{0:T(1024)(128)(4,1)} %bitcast.48), calls=%async_computation.10 | async-start | bytes 8388608
  87.3 1.3 copy-start.2
  88.6 1.4 copy-start.9
  89.9 3.3 copy-start.1
  93.2 0.7 copy-start.17
  113.8 17.1 %copy-start.22 = (s32[32,8]{0,1:T(8,128)S(1)}, s32[32,8]{0,1:T(8,128)}, u32[]{:S(2)}) copy-start(s32[32,8]{0,1:T(8,128)} %param.9) | copy-start | bytes 3076
  115.0 2.7 copy-start.5
  115.0 1.8 copy-start.3
  117.7 0.8 copy-start.10
  130.1 0.8 copy-start.7
  132.7 1.1 copy-start.8
  146.1 2.4 copy-start.19
  148.4 0.8 copy-start.20
  148.5 130.1 %reduce-scatter.5.cloned.1.call-start = ((), (), s32[]{:S(2)}) async-start(), calls=%async_computation.5 | async-start | bytes 2228224 | tf_op jit(solution)/shard_map/reduce_scatter | solution.py:688
  157.1 1.6 copy-start.4
  158.7 1.0 copy-start.6
  159.7 1.0 copy-start.11
  160.8 1.9 copy-start.12
  161.7 1.0 copy-start.14
  166.0 1.3 copy-start.13
  167.3 0.8 copy-start.16
  168.1 117.5 %copy-start.15 = (bf16[16,256,128]{2,1,0:T(8,128)(2,1)S(1)}, bf16[16,256,128]{2,1,0:T(8,128)(2,1)}, u32[]{:S(2)}) copy-start(bf16[16,256,128]{2,1,0:T(8,128)(2,1)} %copy-done.14) | copy-start | bytes 3145732
  168.1 137.9 %copy-start.18 = (f32[128,512]{1,0:T(8,128)S(1)}, f32[128,512]{1,0:T(8,128)}, u32[]{:S(2)}) copy-start(f32[128,512]{1,0:T(8,128)} %copy-done.17) | copy-start | bytes 786436
  168.1 237.8 %reduce-scatter.7.cloned.1.call-start = ((), (), s32[]{:S(2)}) async-start(), calls=%async_computation.6 | async-start | bytes 557056 | tf_op jit(solution)/shard_map/reduce_scatter | solution.py:687
  168.9 262.9 %reduce-scatter.11.cloned.1.call-start = ((), (), s32[]{:S(2)}) async-start(), calls=%async_computation.8 | async-start | bytes 557056 | tf_op jit(solution)/shard_map/reduce_scatter | solution.py:685
  280.1 127.1 %all-to-all-start = ((bf16[32,8,256]{2,0,1:T(8,128)(2,1)}), bf16[32,8,256]{2,0,1:T(8,128)(2,1)}, u32[]{:S(2)}, u32[]{:S(2)}) async-start(bf16[32,8,256]{2,0,1:T(8,128)(2,1)} %copy.49), calls=%async_computation.1 | async-start | bytes 262144 | tf_op jit(solution)/shard_map/all_to_all | solution.py:689
  356.3 1.9 copy-start
Sparse Core Ops, SparseCore 0:
  148.6 58.4 reduce-scatter.8
  211.0 67.5 reduce-scatter.4
  282.3 76.0 reduce-scatter.6
  362.5 69.1 reduce-scatter.10

commit v3 on v2

--- a/solution.py
+++ b/solution.py
@@ -83,7 +83,7 @@
         pl.semaphore_signal(barrier, inc=1, device_id=peer, device_id_type=MESH)
     pl.semaphore_wait(barrier, len(peers))
     copies = []
-    for number, (source, target, device) in enumerate(jobs):
+    for number, (source, target, device, *when) in enumerate(jobs):
         copy = pltpu.make_async_remote_copy(
             src_ref=source,
             dst_ref=target,
@@ -92,8 +92,11 @@
             device_id=device,
             device_id_type=MESH,
         )
-        copy.start()
-        copies.append(copy)
+        if when:
+            pl.when(when[0])(copy.start)
+        else:
+            copy.start()
+        copies.append((copy, when))
     for source, bounce, target, sem in locals_:
         copy = pltpu.make_async_copy(source, bounce, sem)
         copy.start()
@@ -101,8 +104,12 @@
         copy = pltpu.make_async_copy(bounce, target, sem)
         copy.start()
         copy.wait()
-    for copy in copies:
-        copy.wait()
+    for copy, when in copies:
+        if when:
+            pl.when(when[0])(copy.wait_send)
+            pl.when(when[1])(copy.wait_recv)
+        else:
+            copy.wait()
 
 
 def exchange(kernel, name, collective_id, ins, outs, copies, bounces):
@@ -133,121 +140,151 @@
 
 
 def keys_kernel(
-    kv, query, normed, out_w, kv_all, query_two, normed_other, w_all,
-    send_sems, recv_sems, sem, kv_bounce, query_bounce, w_bounce,
+    kv, query, out_w, kv_all, query_two, w_half, send_sems, recv_sems, sem, kv_bounce, query_bounce, w_bounce
 ):
     seq, chip, core, tp = place()
     partner = (chip * 2 + 1 - core, tp)
+    half = pl.ds(core * FR, FR)
     peers = [partner]
-    jobs = [(query.at[1 - core], query_two.at[core], partner)]
-    jobs.append((kv.at[1 - core], kv_all.at[seq], partner))
-    for other in chip_peers(chip, core, tp):
-        peers.append(other)
-        jobs.append((kv.at[core], kv_all.at[seq], other))
-    for other in chip_peers(chip, 1 - core, tp):
-        peers.append(other)
-        jobs.append((kv.at[1 - core], kv_all.at[seq], other))
+    jobs = []
+    for hop in CHIP_ORDER:
+        there = lax.rem(chip + hop, CHIPS)
+        later = there > chip
+        earlier = lax.rem(chip - hop + CHIPS, CHIPS) < chip
+        for head in (core, 1 - core):
+            other = (there * 2 + head, tp)
+            peers.append(other)
+            jobs.append((kv.at[head], kv_all.at[seq], other, later, earlier))
     for other in tp_peers(seq, tp):
         peers.append(other)
-        jobs.append((out_w.at[other[1]], w_all.at[tp], other))
-    jobs.append((normed, normed_other, partner))
+        jobs.append((out_w.at[other[1], half], w_half.at[tp], other))
+    jobs.append((query.at[1 - core], query_two.at[core], partner))
+    jobs.append((kv.at[1 - core], kv_all.at[seq], partner))
     run_exchange(
         peers,
         jobs,
         [
             (kv.at[core], kv_bounce, kv_all.at[seq], sem),
             (query.at[core], query_bounce, query_two.at[core], sem),
-            (out_w.at[tp], w_bounce, w_all.at[tp], sem),
+            (out_w.at[tp, half], w_bounce, w_half.at[tp], sem),
         ],
         send_sems,
         recv_sems,
     )
 
 
-def exchange_keys(kv, query, normed, out_w):
+def exchange_keys(kv, query, out_w):
     return exchange(
         keys_kernel,
         "exchange_keys",
         1,
-        (kv, query, normed, out_w),
+        (kv, query, out_w),
         [
             jax.ShapeDtypeStruct((2 * CHIPS, FR, 2 * HD), BF16),
             jax.ShapeDtypeStruct((2, FR, HD), BF16),
-            jax.ShapeDtypeStruct(normed.shape, BF16),
-            jax.ShapeDtypeStruct(out_w.shape, BF16),
-        ],
-        24,
-        [((FR, 2 * HD), BF16), ((FR, HD), BF16), (out_w.shape[1:], BF16)],
-    )
-
-
-def attended_kernel(source, target, send_sems, recv_sems, sem, bounce):
+            jax.ShapeDtypeStruct((TP, FR, 2 * HD), BF16),
+        ],
+        23,
+        [((FR, 2 * HD), BF16), ((FR, HD), BF16), ((FR, 2 * HD), BF16)],
+    )
+
+
+def attended_kernel(
+    source, w_half, normed, target, w_other, normed_other, send_sems, recv_sems, sem, bounce
+):
     seq, chip, core, tp = place()
     slot = tp * 2 + core
     partner_seq = chip * 2 + 1 - core
-    peers = [(partner_seq, tp)] + tp_peers(seq, tp) + tp_peers(partner_seq, tp)
+    partner = (partner_seq, tp)
+    peers = [partner] + tp_peers(seq, tp) + tp_peers(partner_seq, tp)
     own = pl.ds(core * FR, FR)
     other = pl.ds((1 - core) * FR, FR)
     rows = [other] + [own] * (TP - 1) + [other] * (TP - 1)
     jobs = [(source.at[part], target.at[slot], peer) for part, peer in zip(rows, peers)]
+    jobs.append((w_half, w_other, partner))
+    jobs.append((normed, normed_other, partner))
     run_exchange(
         peers, jobs, [(source.at[own], bounce, target.at[slot], sem)], send_sems, recv_sems
     )
 
 
-def exchange_attended(attended):
+def exchange_attended(attended, w_half, normed):
     return exchange(
         attended_kernel,
         "exchange_attended",
         2,
-        (attended,),
-        [jax.ShapeDtypeStruct((2 * TP, FR, HD), BF16)],
-        15,
+        (attended, w_half, normed),
+        [
+            jax.ShapeDtypeStruct((2 * TP, FR, HD), BF16),
+            jax.ShapeDtypeStruct(w_half.shape, BF16),
+            jax.ShapeDtypeStruct(normed.shape, BF16),
+        ],
+        17,
         [((FR, HD), BF16)],
-    )[0]
-
-
-def scatter_kernel(source, target, send_sems, recv_sems, sem, bounce):
+    )
+
+
+def latent_kernel(
+    source, att_all, merged, target, att_other, merged_other, send_sems, recv_sems, sem, bounce
+):
     seq, chip, core, tp = place()
+    partner = (chip * 2 + 1 - core, tp)
     peers = tp_peers(seq, tp)
     jobs = [(source.at[peer[1]], target.at[tp], peer) for peer in peers]
+    jobs.append((att_all, att_other, partner))
+    jobs.append((merged, merged_other, partner))
     run_exchange(
-        peers, jobs, [(source.at[tp], bounce, target.at[tp], sem)], send_sems, recv_sems
-    )
-
-
-def gather_kernel(source, target, send_sems, recv_sems, sem, bounce):
-    seq, chip, core, tp = place()
-    peers = tp_peers(seq, tp)
-    jobs = [(source, target.at[tp], peer) for peer in peers]
-    run_exchange(peers, jobs, [(source, bounce, target.at[tp], sem)], send_sems, recv_sems)
-
-
-def exchange_latent(parts):
+        peers + [partner],
+        jobs,
+        [(source.at[tp], bounce, target.at[tp], sem)],
+        send_sems,
+        recv_sems,
+    )
+
+
+def exchange_latent(parts, att_all, merged):
     return exchange(
-        scatter_kernel,
+        latent_kernel,
         "exchange_latent",
         3,
-        (parts,),
-        [jax.ShapeDtypeStruct(parts.shape, parts.dtype)],
-        7,
+        (parts, att_all, merged),
+        [
+            jax.ShapeDtypeStruct(parts.shape, parts.dtype),
+            jax.ShapeDtypeStruct(att_all.shape, BF16),
+            jax.ShapeDtypeStruct(merged.shape, BF16),
+        ],
+        9,
         [(parts.shape[1:], parts.dtype)],
-    )[0]
-
-
-def exchange_message(message):
+    )
+
+
+def message_kernel(source, grads, target, grads_other, send_sems, recv_sems, sem, bounce):
+    seq, chip, core, tp = place()
+    partner_seq = chip * 2 + 1 - core
+    peers = tp_peers(seq, tp) + tp_peers(partner_seq, tp) + [(partner_seq, tp)]
+    jobs = [(source, target.at[core, tp], peer) for peer in peers]
+    jobs.append((grads.at[:, 1 - core], grads_other, peers[-1]))
+    run_exchange(peers, jobs, [(source, bounce, target.at[core, tp], sem)], send_sems, recv_sems)
+
+
+def exchange_message(message, grads):
     return exchange(
-        gather_kernel,
+        message_kernel,
         "exchange_message",
         4,
-        (message,),
-        [jax.ShapeDtypeStruct((TP,) + message.shape, message.dtype)],
-        7,
+        (message, grads),
+        [
+            jax.ShapeDtypeStruct((2, TP) + message.shape, message.dtype),
+            jax.ShapeDtypeStruct((CHIPS, TP) + grads.shape[3:], BF16),
+        ],
+        16,
         [(message.shape, message.dtype)],
-    )[0]
-
-
-def cotangent_kernel(source, target, send_sems, recv_sems, sem, bounce):
+    )
+
+
+def cotangent_kernel(
+    source, side, target, side_all, send_sems, recv_sems, sem, bounce, side_bounce
+):
     seq, chip, core, tp = place()
     partner_seq = chip * 2 + 1 - core
     peers = [(partner_seq, tp)] + tp_peers(seq, tp) + tp_peers(partner_seq, tp)
@@ -256,76 +293,136 @@
         (source.at[peer[1] * 2 + head], target.at[core, tp], peer)
         for head, peer in zip(heads, peers)
     ]
+    for other in chip_peers(chip, core, tp):
+        peers.append(other)
+        jobs.append((side.at[other[0] // 2], side_all.at[chip], other))
     run_exchange(
         peers,
         jobs,
-        [(source.at[tp * 2 + core], bounce, target.at[core, tp], sem)],
+        [
+            (source.at[tp * 2 + core], bounce, target.at[core, tp], sem),
+            (side.at[chip], side_bounce, side_all.at[chip], sem),
+        ],
         send_sems,
         recv_sems,
     )
 
 
-def exchange_cotangent(parts):
+def exchange_cotangent(parts, side):
     return exchange(
         cotangent_kernel,
         "exchange_cotangent",
         5,
-        (parts,),
-        [jax.ShapeDtypeStruct((2, TP, FR, HD), BF16)],
-        15,
-        [((FR, HD), BF16)],
-    )[0]
-
-
-def key_grads_kernel(source, target, send_sems, recv_sems, sem, bounce):
+        (parts, side),
+        [
+            jax.ShapeDtypeStruct((2, TP, FR, HD), BF16),
+            jax.ShapeDtypeStruct(side.shape, BF16),
+        ],
+        22,
+        [((FR, HD), BF16), (side.shape[1:], BF16)],
+    )
+
+
+def key_grads_kernel(source, grads, target, grads_z, send_sems, recv_sems, sem, bounce, grads_bounce):
     seq, chip, core, tp = place()
-    peers = chip_peers(chip, core, tp)
-    jobs = [(source.at[peer[0] // 2], target.at[chip], peer) for peer in peers]
+    row, depth_at = tp // 4, tp % 4
+    peers = []
+    jobs = []
+    for hop in CHIP_ORDER:
+        there = lax.rem(chip + hop, CHIPS)
+        here = lax.rem(chip - hop + CHIPS, CHIPS)
+        other = (there * 2 + core, tp)
+        peers.append(other)
+        jobs.append((source.at[there], target.at[chip], other, there < chip, here > chip))
+    for hop in (1, 3, 2):
+        there = lax.rem(depth_at + hop, 4)
+        other = (seq, row * 4 + there)
+        peers.append(other)
+        jobs.append((grads.at[:, :, there], grads_z.at[depth_at], other))
     run_exchange(
-        peers, jobs, [(source.at[chip], bounce, target.at[chip], sem)], send_sems, recv_sems
-    )
-
-
-def exchange_key_grads(parts):
+        peers,
+        jobs,
+        [
+            (source.at[chip], bounce, target.at[chip], sem),
+            (grads.at[:, :, depth_at], grads_bounce, grads_z.at[depth_at], sem),
+        ],
+        send_sems,
+        recv_sems,
+    )
+
+
+def exchange_key_grads(parts, grads):
+    slab = (CHIPS, 2) + grads.shape[3:]
     return exchange(
         key_grads_kernel,
         "exchange_key_grads",
         6,
-        (parts,),
-        [jax.ShapeDtypeStruct(parts.shape, parts.dtype)],
-        7,
-        [(parts.shape[1:], parts.dtype)],
-    )[0]
-
-
-def weights_kernel(source, target, send_sems, recv_sems, sem, bounce):
+        (parts, grads),
+        [
+            jax.ShapeDtypeStruct(parts.shape, parts.dtype),
+            jax.ShapeDtypeStruct((4,) + slab, BF16),
+        ],
+        10,
+        [(parts.shape[1:], parts.dtype), (slab, BF16)],
+    )
+
+
+def weights_kernel(
+    source, grads, out, target, grads_all, out_all, send_sems, recv_sems, sem, bounce, grads_bounce, out_bounce
+):
     seq, chip, core, tp = place()
+    row, depth_at = tp // 4, tp % 4
     partner = (chip * 2 + 1 - core, tp)
     peers = [partner] + chip_peers(chip, core, tp) + chip_peers(chip, 1 - core, tp)
     jobs = [(source.at[peer[0]], target.at[core, chip], peer) for peer in peers]
+    for hop in CHIP_ORDER:
+        there = lax.rem(chip + hop, CHIPS)
+        jobs.append((grads.at[there, row], grads_all.at[chip, row], (there * 2 + core, tp)))
+    across = (1 - row) * 4 + depth_at
+    for hop in (0,) + CHIP_ORDER:
+        there = lax.rem(chip + hop, CHIPS)
+        other = (there * 2 + core, across)
+        if hop:
+            peers.append(other)
+        jobs.append((grads.at[there, 1 - row], grads_all.at[chip, row], other))
+    for other in tp_peers(seq, tp):
+        peers.append(other)
+        jobs.append((out.at[other[1]], out_all.at[tp], other))
     run_exchange(
-        peers, jobs, [(source.at[seq], bounce, target.at[core, chip], sem)], send_sems, recv_sems
-    )
-
-
-def exchange_weights(parts):
+        peers,
+        jobs,
+        [
+            (source.at[seq], bounce, target.at[core, chip], sem),
+            (grads.at[chip, row], grads_bounce, grads_all.at[chip, row], sem),
+            (out.at[tp], out_bounce, out_all.at[tp], sem),
+        ],
+        send_sems,
+        recv_sems,
+    )
+
+
+def exchange_weights(parts, grads, out):
     return exchange(
         weights_kernel,
         "exchange_weights",
         7,
-        (parts,),
-        [jax.ShapeDtypeStruct((2, CHIPS) + parts.shape[1:], parts.dtype)],
-        15,
-        [(parts.shape[1:], parts.dtype)],
-    )[0]
-
-
-def compute(kernel, name, ins, outs, scratch=(), limit=48):
+        (parts, grads, out),
+        [
+            jax.ShapeDtypeStruct((2, CHIPS) + parts.shape[1:], parts.dtype),
+            jax.ShapeDtypeStruct(grads.shape, BF16),
+            jax.ShapeDtypeStruct(out.shape, BF16),
+        ],
+        37,
+        [(parts.shape[1:], BF16), (grads.shape[2:], BF16), (out.shape[1:], BF16)],
+    )
+
+
+def compute(kernel, name, ins, outs, scratch=(), limit=48, hbm=0):
     return pl.pallas_call(
         kernel,
         name=name,
         out_shape=outs,
-        in_specs=[VMEM] * len(ins),
+        in_specs=[VMEM] * (len(ins) - hbm) + [ANY] * hbm,
         out_specs=[VMEM] * len(outs),
         scratch_shapes=list(scratch),
         compiler_params=pltpu.CompilerParams(vmem_limit_bytes=limit * MIB),
@@ -380,27 +477,59 @@
     )
 
 
-def merge_kernel(att_ref, w_ref, hidden_ref, depth_in_ref, merged_ref, part_ref):
-    merged = hidden_ref[...].astype(F32)
-    for tp in range(TP):
-        pair = jnp.concatenate([att_ref[2 * tp], att_ref[2 * tp + 1]], axis=1)
-        merged = merged + dot_nt(pair, w_ref[tp])
+def fetch(source, target, sem):
+    copy = pltpu.make_async_copy(source, target, sem)
+    copy.start()
+    return copy
+
+
+def order_halves(core, mine, other):
+    return jnp.where(core == 0, mine, other), jnp.where(core == 0, other, mine)
+
+
+def merge_kernel(
+    att_ref, half_ref, other_ref, hidden_ref, depth_in_hbm, merged_ref, round_ref, part_ref, depth_in_ref, sem
+):
+    seq, chip, core, tp = place()
+    copy = fetch(depth_in_hbm.at[:, tp], depth_in_ref, sem)
+    width = hidden_ref.shape[1]
+    group = width // 2
+    row_at = lax.broadcasted_iota(jnp.int32, (group, FR), 0)
+    col_at = lax.broadcasted_iota(jnp.int32, (group, FR), 1)
+    wanted = (col_at // 32) * 256 + tp * 32 + col_at % 32
+    pick = jnp.where(row_at == wanted, 1.0, 0.0).astype(BF16)
+    merged = jnp.concatenate(
+        [dot_nn(hidden_ref[:, :group], pick), dot_nn(hidden_ref[:, group:], pick)], axis=1
+    )
+    mine = jnp.zeros((FR, FR), F32)
+    other = jnp.zeros((FR, FR), F32)
+    for at in range(TP):
+        pair = jnp.concatenate([att_ref[2 * at], att_ref[2 * at + 1]], axis=1)
+        mine = mine + dot_nt(pair, half_ref[at])
+        other = other + dot_nt(pair, other_ref[at])
+    merged = merged + jnp.concatenate(order_halves(core, mine, other), axis=1)
+    rounded = merged.astype(BF16)
     merged_ref[...] = merged
+    round_ref[...] = rounded
     squares = jnp.sum(merged * merged, axis=-1, keepdims=True)
-    latent = dot_nn(merged.astype(BF16), depth_in_ref[...])
+    copy.wait()
+    latent = dot_nn(rounded, depth_in_ref[...].reshape(NS, DD))
     part_ref[:, :, :DD] = latent.reshape(TP, FR // TP, DD)
     part_ref[:, :, DD:] = jnp.broadcast_to(squares, (FR, HD)).reshape(TP, FR // TP, HD)
 
 
-def merge(att_all, w_all, hidden_slice, depth_in_slice):
+def merge(att_all, w_half, w_other, hidden, depth_in):
     return compute(
         merge_kernel,
         "merge",
-        (att_all, w_all, hidden_slice, depth_in_slice),
+        (att_all, w_half, w_other, hidden, depth_in),
         [
             jax.ShapeDtypeStruct((FR, NS), F32),
+            jax.ShapeDtypeStruct((FR, NS), BF16),
             jax.ShapeDtypeStruct((TP, FR // TP, DD + HD), F32),
         ],
+        [pltpu.VMEM((2 * CHIPS, 32, DD), BF16), pltpu.SemaphoreType.DMA],
+        hbm=1,
     )
 
 
@@ -495,48 +624,100 @@
     )
 
 
-def unmerge_kernel(message_ref, merged_ref, depth_in_ref, w_ref, merged_grad_ref, part_ref):
-    message = message_ref[...].reshape(FR, DD + 2 * HD)
+def merged_gradient(message, merged, depth_in):
     pull = message[:, DD : DD + 1].astype(F32) + message[:, DD + HD : DD + HD + 1].astype(F32)
-    gradient = dot_nt(message[:, :DD], depth_in_ref[...]) - merged_ref[...] * pull
-    gradient = gradient.astype(BF16)
-    merged_grad_ref[...] = gradient
-    for tp in range(TP):
-        pair = dot_nn(gradient, w_ref[tp]).astype(BF16)
-        part_ref[2 * tp] = pair[:, :HD]
-        part_ref[2 * tp + 1] = pair[:, HD:]
-
-
-def unmerge(messages, merged, depth_in_slice, w_all):
+    return dot_nt(message[:, :DD], depth_in) - merged * pull
+
+
+def unmerge_kernel(
+    message_ref,
+    merged_ref,
+    round_ref,
+    round_other_ref,
+    att_ref,
+    att_other_ref,
+    half_ref,
+    other_ref,
+    grads_other_ref,
+    grads_hbm,
+    depth_in_hbm,
+    part_ref,
+    side_ref,
+    grads_ref,
+    depth_in_ref,
+    grads_own_ref,
+    sems,
+):
+    seq, chip, core, tp = place()
+    copy = fetch(depth_in_hbm.at[:, tp], depth_in_ref, sems.at[0])
+    grads_copy = fetch(grads_hbm.at[:, core], grads_own_ref, sems.at[1])
+    copy.wait()
+    depth_in = depth_in_ref[...].reshape(NS, DD)
+    message = message_ref[core].reshape(FR, DD + 2 * HD)
+    message_other = message_ref[1 - core].reshape(FR, DD + 2 * HD)
+    gradient = merged_gradient(message, merged_ref[...], depth_in)
+    lower, upper = gradient[:, :FR], gradient[:, FR:]
+    mine, other = order_halves(core, lower, upper)
+    mine, other = mine.astype(BF16), other.astype(BF16)
+    for at in range(TP):
+        pair = (dot_nn(mine, half_ref[at]) + dot_nn(other, other_ref[at])).astype(BF16)
+        part_ref[2 * at] = pair[:, :HD]
+        part_ref[2 * at + 1] = pair[:, HD:]
+    gradient_other = merged_gradient(
+        message_other, round_other_ref[...].astype(F32), depth_in
+    )
+
+    def pick_rows(own, others):
+        both = jnp.concatenate([own.T, others.T], axis=1).reshape(CHIPS, 2, 32, FR2)
+        both = jnp.where(core == 0, both[:, 0], both[:, 1])
+        return both.reshape(FR, FR2).astype(BF16)
+
+    rows = pick_rows(gradient, gradient_other)
+    for at in range(TP):
+        pair = jnp.concatenate([att_ref[2 * at], att_ref[2 * at + 1]], axis=1)
+        pair_other = jnp.concatenate([att_other_ref[2 * at], att_other_ref[2 * at + 1]], axis=1)
+        term = dot_nn(rows, jnp.concatenate([pair, pair_other], axis=0)).astype(BF16)
+        side_ref[:, :, at * FR : (at + 1) * FR] = term.reshape(CHIPS, 32, FR)
+    rows = pick_rows(round_ref[...].astype(F32), round_other_ref[...].astype(F32))
+    both = jnp.concatenate([message[:, :DD], message_other[:, :DD]], axis=0)
+    side_ref[:, :, TP * FR :] = dot_nn(rows, both).astype(BF16).reshape(CHIPS, 32, DD)
+    grads_copy.wait()
+    for at in range(CHIPS):
+        grads_ref[at] = (
+            grads_own_ref[at].astype(F32) + grads_other_ref[at].astype(F32)
+        ).astype(BF16)
+
+
+def unmerge(
+    messages, merged, rounded, rounded_other, att_all, att_other, w_half, w_other, grads_other, grads, depth_in
+):
     return compute(
         unmerge_kernel,
         "unmerge",
-        (messages, merged, depth_in_slice, w_all),
-        [
-            jax.ShapeDtypeStruct((FR, NS), BF16),
+        (
+            messages,
+            merged,
+            rounded,
+            rounded_other,
+            att_all,
+            att_other,
+            w_half,
+            w_other,
+            grads_other,
+            grads,
+            depth_in,
+        ),
+        [
             jax.ShapeDtypeStruct((2 * TP, FR, HD), BF16),
-        ],
-    )
-
-
-def side_kernel(messages_ref, merged_ref, merged_grad_ref, att_ref, win_ref, out_ref):
-    message = messages_ref[...].reshape(FR, DD + 2 * HD)
-    win_ref[...] = dot_tn(merged_ref[...].astype(BF16), message[:, :DD]).astype(BF16)
-    gradient = merged_grad_ref[...]
-    for tp in range(TP):
-        pair = jnp.concatenate([att_ref[2 * tp], att_ref[2 * tp + 1]], axis=1)
-        out_ref[:, tp] = dot_tn(gradient, pair).astype(BF16)
-
-
-def side_grads(messages, merged, merged_grad, att_all):
-    return compute(
-        side_kernel,
-        "side_grads",
-        (messages, merged, merged_grad, att_all),
-        [
-            jax.ShapeDtypeStruct((NS, DD), BF16),
-            jax.ShapeDtypeStruct((NS, TP, 2 * HD), BF16),
-        ],
+            jax.ShapeDtypeStruct((CHIPS, 32, TP * FR + DD), BF16),
+            jax.ShapeDtypeStruct(grads_other.shape, BF16),
+        ],
+        [
+            pltpu.VMEM((2 * CHIPS, 32, DD), BF16),
+            pltpu.VMEM(grads_other.shape, BF16),
+            pltpu.SemaphoreType.DMA((2,)),
+        ],
+        hbm=2,
     )
 
 
@@ -545,7 +726,6 @@
 ):
     chip = lax.axis_index("seq") // 2
     blocks = 2 * chip + 2
-    grad_ref[...] = jnp.zeros_like(grad_ref)
     query = query_ref[...].reshape(FR2, HD)
     gradient = jnp.sum(part_ref[...].astype(F32), axis=1).reshape(FR2, HD)
     gradient = gradient.astype(BF16).astype(F32)
@@ -585,9 +765,18 @@
     )
 
 
-def weight_kernel(part_ref, query_grad_ref, cos_ref, sin_ref, normed_ref, other_ref, out_ref):
+def weight_kernel(
+    part_ref, query_grad_ref, cos_ref, sin_ref, normed_ref, other_ref, grads_z_ref, side_ref,
+    out_ref, grads_ref, win_ref, out_w_ref,
+):
+    chip = lax.axis_index("seq") // 2
     core = lax.axis_index("seq") % 2
-    total = jnp.sum(part_ref[...].astype(F32), axis=0)
+    total = lax.fori_loop(
+        chip,
+        CHIPS,
+        lambda at, carry: carry + part_ref[at].astype(F32),
+        jnp.zeros((FR2, 2 * HD), F32),
+    )
     lower, upper = total[:, : HD // 2], total[:, HD // 2 : HD]
     cosine, sine = cos_ref[...], sin_ref[...]
     proj = jnp.concatenate(
@@ -600,39 +789,54 @@
         axis=1,
     )
     proj_t = proj.T
-    first, second = proj_t[:, :FR], proj_t[:, FR:]
-    own = jnp.where(core == 0, first, second).astype(BF16)
-    other = jnp.where(core == 0, second, first).astype(BF16)
+    own, other = order_halves(core, proj_t[:, :FR], proj_t[:, FR:])
+    own, other = own.astype(BF16), other.astype(BF16)
     for piece in range(2 * CHIPS):
         low = piece * FR
         term = dot_nn(own, normed_ref[:, low : low + FR])
         term = term + dot_nn(other, other_ref[:, low : low + FR])
         out_ref[piece] = term.astype(BF16)
-
-
-def weight_terms(parts, query_grad, cosine, sine, normed, normed_other):
+    for at in range(CHIPS):
+        grads_ref[at] = jnp.sum(grads_z_ref[:, at].astype(F32), axis=0).astype(BF16)
+    side = jnp.sum(side_ref[...].astype(F32), axis=0)
+    win_ref[...] = side[:, TP * FR :]
+    for at in range(TP):
+        out_w_ref[at] = side[:, at * FR : (at + 1) * FR].astype(BF16)
+
+
+def weight_terms(parts, query_grad, cosine, sine, normed, normed_other, grads_z, side_all):
     return compute(
         weight_kernel,
         "weight_terms",
-        (parts, query_grad, cosine, sine, normed, normed_other),
-        [jax.ShapeDtypeStruct((2 * CHIPS, 3 * HD, FR), BF16)],
-    )[0]
-
-
-def weight_sum_kernel(part_ref, out_ref):
+        (parts, query_grad, cosine, sine, normed, normed_other, grads_z, side_all),
+        [
+            jax.ShapeDtypeStruct((2 * CHIPS, 3 * HD, FR), BF16),
+            jax.ShapeDtypeStruct(grads_z.shape[1:], BF16),
+            jax.ShapeDtypeStruct((32, DD), F32),
+            jax.ShapeDtypeStruct((TP, 32, FR), BF16),
+        ],
+    )
+
+
+def weight_sum_kernel(part_ref, grads_ref, out_w_ref, out_ref, depth_ref):
     for head in range(2):
         total = jnp.sum(part_ref[head].astype(F32), axis=0).T
         for kind in range(3):
             out_ref[kind, :, head * HD : (head + 1) * HD] = total[:, kind * HD : (kind + 1) * HD]
-
-
-def weight_sum(parts):
+    out_ref[3] = out_w_ref[...].astype(F32).reshape(FR, 2 * HD)
+    depth_ref[...] = jnp.sum(jnp.sum(grads_ref[...].astype(F32), axis=0), axis=0)
+
+
+def weight_sum(parts, grads_all, out_all):
     return compute(
         weight_sum_kernel,
         "weight_sum",
-        (parts,),
-        [jax.ShapeDtypeStruct((3, FR, 2 * HD), F32)],
-    )[0]
+        (parts, grads_all, out_all),
+        [
+            jax.ShapeDtypeStruct((4, FR, 2 * HD), F32),
+            jax.ShapeDtypeStruct(grads_all.shape[2:], F32),
+        ],
+    )
 
 
 def per_device(hidden_in, temporal_weight_stack, depth_in, depth_stack, audio_codes):
@@ -658,45 +862,48 @@
     query = query.transpose(1, 0, 2)
     out_w = temporal_weight_stack[:, 3, :].reshape(seq_count, TP, -1, 2 * HD)
     out_w = out_w.transpose(1, 0, 2, 3).reshape(TP, NS, 2 * HD)
-    kv_all, query_two, normed_other, w_all = exchange_keys(kv, query, normed, out_w)
-
-    hidden_slice = lax.dynamic_index_in_dim(
-        hidden_in.reshape(FR, seq_count, TP, -1), tp_index, 2, keepdims=False
-    ).reshape(FR, NS)
-    depth_in_slice = lax.dynamic_index_in_dim(
-        depth_in.reshape(seq_count, TP, -1, DD), tp_index, 1, keepdims=False
-    ).reshape(NS, DD)
+    kv_all, query_two, w_half = exchange_keys(kv, query, out_w)
+
+    depth_in = depth_in.reshape(seq_count, TP, -1, DD)
     attended, probs, out_t, inverse = attend(kv_all, query_two)
-    att_all = exchange_attended(attended)
-    merged, latent_parts = merge(att_all, w_all, hidden_slice, depth_in_slice)
-    latent_parts = exchange_latent(latent_parts)
+    att_all, w_other, normed_other = exchange_attended(attended, w_half, normed)
+    merged, rounded, latent_parts = merge(att_all, w_half, w_other, hidden_in, depth_in)
+    latent_parts, att_other, rounded_other = exchange_latent(latent_parts, att_all, rounded)
     before = jnp.concatenate(
         [jnp.full((depth_frames, 1), -1, jnp.int32), audio_codes[:, :-1]], axis=1
     ).reshape(-1, 1)
-    message, grad_depth = depth(
+    message, grads = depth(
         latent_parts, depth_stack, before, audio_codes.reshape(-1, 1), width, loss_scale
     )
-    messages = exchange_message(message)
-    merged_grad, cotangent_parts = unmerge(messages, merged, depth_in_slice, w_all)
-    cotangent_parts = exchange_cotangent(cotangent_parts)
-
-    grad_depth = grad_depth.reshape(seq_count, TP, -1, DD).transpose(1, 0, 2, 3)
-    grad_depth = lax.psum_scatter(grad_depth, "tp", scatter_dimension=0, tiled=True)[0]
-    grad_depth = lax.psum_scatter(grad_depth, "seq", scatter_dimension=0, tiled=True)[0]
-    grad_win, grad_out = side_grads(messages, merged, merged_grad, att_all)
-    grad_win = lax.psum_scatter(grad_win, "seq", scatter_dimension=0, tiled=True)
-    grad_out = lax.psum_scatter(grad_out, "seq", scatter_dimension=0, tiled=True)
-    grad_out = lax.all_to_all(grad_out, "tp", 1, 0, tiled=True).reshape(FR, 1, 2 * HD)
+    grads = grads.reshape(CHIPS, 2, TP, -1, DD)
+    messages, grads_other = exchange_message(message, grads)
+    cotangent_parts, side, grads = unmerge(
+        messages,
+        merged,
+        rounded,
+        rounded_other,
+        att_all,
+        att_other,
+        w_half,
+        w_other,
+        grads_other,
+        grads,
+        depth_in,
+    )
+    cotangent_parts, side_all = exchange_cotangent(cotangent_parts, side)
 
     cosine, sine = angle_tables(chip * FR2, FR2)
     key_parts, query_grad = attend_back(
         probs, kv_all, query_two, cotangent_parts, out_t, inverse, cosine, sine
     )
-    key_parts = exchange_key_grads(key_parts.reshape(CHIPS, FR2, 2 * HD))
-    parts = weight_terms(key_parts, query_grad, cosine, sine, normed, normed_other)
-    grad_in = weight_sum(exchange_weights(parts))
-    grad_temporal = jnp.concatenate([grad_in.transpose(1, 0, 2), grad_out.astype(F32)], axis=1)
-    return grad_temporal, grad_win.astype(F32), grad_depth.astype(F32)
+    key_parts, grads_z = exchange_key_grads(
+        key_parts.reshape(CHIPS, FR2, 2 * HD), grads.reshape(CHIPS, 2, 4, -1, DD)
+    )
+    parts, grads, grad_win, out_parts = weight_terms(
+        key_parts, query_grad, cosine, sine, normed, normed_other, grads_z, side_all
+    )
+    grad_temporal, grad_depth = weight_sum(*exchange_weights(parts, grads, out_parts))
+    return grad_temporal.transpose(1, 0, 2), grad_win, grad_depth
 
 
 def solution(mesh):

time: 442 us -> 287 us (0.65)
  waiting for transfers between devices: 132 us -> 0 us
  local copies, waits for them, and re-layouts: 41.2 us -> 20.7 us
  Pallas kernels: 232 us -> 250 us
  between operations: 14.3 us -> 1.07 us
  starting transfers between devices: 4.89 us -> 0 us
    reduce_scatter x4 -> x0, waiting for transfers between devices: 131 us -> none  [the longest x1 71.5 us: per_device(): lax.psum_scatter(grad_out, 'seq', scatter_dimension=0, tiled=True)]
    unnamed x59 -> x50, local copies, waits for them, and re-layouts: 26.6 us -> 12.9 us
    pallas_call x8 -> x7, Pallas kernels: 31.4 us -> 40.6 us  [compute(): pl.pallas_call(kernel, name=name, out_shape=outs, in_specs=[VMEM] * (len(...]
    pallas_call x7, Pallas kernels: 201 us -> 210 us  [exchange(): pl.pallas_call(kernel, name=name, out_shape=outs, in_specs=[ANY] * len(in...]
    all_to_all x1 -> x0, starting transfers between devices: 4.51 us -> none  [per_device(): lax.all_to_all(grad_out, 'tp', 1, 0, tiled=True).reshape(FR, 1, 2 * HD)]
  transfers between devices with their start and end apart: 5 -> 0, of which waited for: 3 -> 0; matrix products, arithmetic and copies ran while one was open for 2% -> 0% of each run, Pallas kernels for 30% -> 0%
where the time goes in v3:
time: 287 us
  Pallas kernels  250 us (87%)
  local copies, waits for them, and re-layouts  20.7 us (7%)
  other arithmetic  7.85 us (3%)
  matrix products  6.69 us (2%)
    pallas_call x7, Pallas kernels, exchange(): pl.pallas_call(kernel, name=name, out_shape=outs, in_specs=[ANY] * len(in...  210 us
    pallas_call x7, Pallas kernels, compute(): pl.pallas_call(kernel, name=name, out_shape=outs, in_specs=[VMEM] * (len(...  40.6 us
    unnamed x50, local copies, waits for them, and re-layouts  12.9 us
    dot_general x1, matrix products, per_device(): jnp.einsum('wo,obu->wbu', normed, temporal_weight_stack[:, :3, :], prefer...  6.69 us
    slice x1, local copies, waits for them, and re-layouts, per_device(): out_w = temporal_weight_stack[:, 3, :].reshape(seq_count, TP, -1, 2 * HD)  6.13 us

profile of v3, /device:TPU:1, one launch (start us, length us, event | category | flops | bytes accessed | tf_op | source)
XLA Modules:
  0.0 286.6 jit_solution(2661553001180529511)
XLA Ops:
  0.6 0.0 copy-start.18
  0.7 1.2 multiply_cosine_fusion.1
  1.9 2.1 fusion.2
  4.0 0.6 fusion.3.normed.normed_ref
  4.6 6.7 %fusion = f32[256,3,256]{0,2,1:T(8,128)S(1)} fusion(bf16[4096,3,256]{2,1,0:T(4,128)(2,1)} %bitcast.30, bf16[256,4096]{1,0:T(8,128)(2,1)S(1)} %fusion.3.normed.normed_ref), kind=kOutput, calls=%fused_computation | convolution fusion | flops 1610612736 | bytes 9175040 | tf_op jit(solution)/shard_map/wo,obu->wbu/dot_general | solution.py:854
  11.3 0.0 copy-start.19
  11.4 0.8 copy-done.19
  12.2 0.1 copy.27
  12.3 0.1 copy.28
  12.5 0.1 copy.29
  12.6 0.1 copy.30
  12.7 1.8 subtract_convert_fusion
  14.5 1.0 slice.49
  15.5 0.1 copy.16
  15.6 1.1 maximum_bitcast_fusion.kv
  16.7 0.1 maximum_bitcast_fusion.1.query
  16.8 6.1 %slice.39 = bf16[4096,1,256]{2,1,0:T(2,128)(2,1)S(1)} slice(bf16[4096,4,256]{2,1,0:T(4,128)(2,1)} %param.6), slice={[0:4096], [3:4], [0:256]} | slice | bytes 4194304 | tf_op jit(solution)/shard_map/slice | solution.py:863
  22.9 0.3 copy.31
  23.3 0.2 copy.20
  23.5 30.3 %exchange_keys.1 = (bf16[16,256,256]{2,1,0:T(8,128)(2,1)S(1)}, bf16[2,256,128]{2,1,0:T(8,128)(2,1)S(1)}, bf16[8,256,256]{2,1,0:T(8,128)(2,1)S(1)}) custom-call(bf16[2,256,256]{2,1,0:T(8,128)(2,1)S(1)} %maximum_bitcast_fusion.kv, bf16[2,256,128]{2,1,0:T(8,128)(2,1)S(1)} %maximum_bitcast_fusion.1.query, bf16[8,512,256]{2,1,0:T(8,128)(2,1)S(1)} %bitcast.23), custom_call_target="tpu_custom_call" | custom-call | tf_op jit(solution)/shard_map/exchange_keys/pallas_call | solution.py:116
  53.9 3.3 %attend.1 = (bf16[512,128]{1,0:T(8,128)(2,1)S(1)}, bf16[16,256,512]{2,1,0:T(8,128)(2,1)}, f32[128,512]{1,0:T(8,128)S(1)}, f32[1,512]{1,0:T(1,128)S(1)}) custom-call(bf16[16,256,256]{2,1,0:T(8,128)(2,1)S(1)} %get-tuple-element.41.kv_ref, bf16[2,256,128]{2,1,0:T(8,128)(2,1)S(1)} %get-tuple-element.42.query_ref), custom_call_target="tpu_custom_call" | custom-call | tf_op jit(solution)/shard_map/attend/pallas_call | solution.py:421
  57.1 0.7 copy-done.16
  57.8 18.9 %exchange_attended.1 = (bf16[16,256,128]{2,1,0:T(8,128)(2,1)S(1)}, bf16[8,256,256]{2,1,0:T(8,128)(2,1)S(1)}, bf16[256,4096]{1,0:T(8,128)(2,1)S(1)}) custom-call(bf16[512,128]{1,0:T(8,128)(2,1)S(1)} %get-tuple-element.44.source, bf16[8,256,256]{2,1,0:T(8,128)(2,1)S(1)} %get-tuple-element.45.w_half.half_ref, bf16[256,4096]{1,0:T(8,128)(2,1)S(1)} %fusion.3.normed.normed_ref), custom_call_target="tpu_custom_call" | custom-call | tf_op jit(solution)/shard_map/exchange_attended/pallas_call | solution.py:116
  76.8 1.3 copy-done.7
  78.1 5.0 %merge.1 = (f32[256,512]{1,0:T(8,128)S(1)}, bf16[256,512]{1,0:T(8,128)(2,1)S(1)}, f32[8,32,640]{2,1,0:T(8,128)S(1)}) custom-call(bf16[16,256,128]{2,1,0:T(8,128)(2,1)S(1)} %get-tuple-element.46.att_ref.att_all, bf16[8,256,256]{2,1,0:T(8,128)(2,1)S(1)} %get-tuple-element.45.w_half.half_ref, bf16[8,256,256]{2,1,0:T(8,128)(2,1)S(1)} %get-tuple-element.47.other_ref, ...), custom_call_target="tpu_custom_call" | custom-call | tf_op jit(solution)/shard_map/merge/pallas_call | solution.py:421
  83.1 0.8 copy-done.12
  84.0 11.7 %exchange_latent.1 = (f32[8,32,640]{2,1,0:T(8,128)S(1)}, bf16[16,256,128]{2,1,0:T(8,128)(2,1)S(1)}, bf16[256,512]{1,0:T(8,128)(2,1)S(1)}) custom-call(f32[8,32,640]{2,1,0:T(8,128)S(1)} %get-tuple-element.48.source, bf16[16,256,128]{2,1,0:T(8,128)(2,1)S(1)} %get-tuple-element.46.att_ref.att_all, bf16[256,512]{1,0:T(8,128)(2,1)S(1)} %get-tuple-element.49.merged.round_ref), custom_call_target="tpu_custom_call" | custom-call | tf_op jit(solution)/shard_map/exchange_latent/pallas_call | solution.py:116
  95.7 0.7 copy-done.14
  96.4 0.1 copy.32
  96.5 0.1 concatenate.15.clone
  96.6 0.1 reshape.108.before_ref
  96.7 0.1 copy.22
  96.7 0.1 reshape.109.code_ref
  96.8 12.2 %depth.1 = (bf16[32,768]{1,0:T(8,128)(2,1)S(1)}, bf16[4096,512]{1,0:T(8,128)(2,1)S(1)}) custom-call(f32[8,32,640]{2,1,0:T(8,128)S(1)} %get-tuple-element.50.part_ref, bf16[4096,512]{1,0:T(8,128)(2,1)} %stack_ref.1, s32[256,1]{1,0:T(8,128)S(1)} %reshape.108.before_ref, s32[256,1]{1,0:T(8,128)S(1)} %reshape.109.code_ref), custom_call_target="tpu_custom_call" | custom-call | tf_op jit(solution)/shard_map/depth/pallas_call | solution.py:421
  109.1 15.7 %exchange_message.1 = (bf16[2,8,32,768]{3,2,1,0:T(8,128)(2,1)S(1)}, bf16[8,8,32,512]{3,2,1,0:T(8,128)(2,1)S(1)}) custom-call(bf16[32,768]{1,0:T(8,128)(2,1)S(1)} %get-tuple-element.51.source, bf16[8,2,8,32,512]{4,3,2,1,0:T(8,128)(2,1)S(1)} %bitcast.21), custom_call_target="tpu_custom_call" | custom-call | tf_op jit(solution)/shard_map/exchange_message/pallas_call | solution.py:116
  124.8 1.4 copy-done.10
  126.2 6.8 %unmerge.1 = (bf16[16,256,128]{2,1,0:T(8,128)(2,1)S(1)}, bf16[8,32,2560]{2,1,0:T(8,128)(2,1)}, bf16[8,8,32,512]{3,2,1,0:T(8,128)(2,1)}) custom-call(bf16[2,8,32,768]{3,2,1,0:T(8,128)(2,1)S(1)} %get-tuple-element.53.message_ref, f32[256,512]{1,0:T(8,128)S(1)} %copy-done.13, bf16[256,512]{1,0:T(8,128)(2,1)S(1)} %get-tuple-element.49.merged.round_ref, ...), custom_call_target="tpu_custom_call" | custom-call | tf_op jit(solution)/shard_map/unmerge/pallas_call | solution.py:421
  133.0 1.3 copy-done.11
  134.3 48.7 %exchange_cotangent.1 = (bf16[2,8,256,128]{3,2,1,0:T(8,128)(2,1)S(1)}, bf16[8,32,2560]{2,1,0:T(8,128)(2,1)S(1)}) custom-call(bf16[16,256,128]{2,1,0:T(8,128)(2,1)S(1)} %get-tuple-element.58.source, bf16[8,32,2560]{2,1,0:T(8,128)(2,1)S(1)} %copy-done.11), custom_call_target="tpu_custom_call" | custom-call | tf_op jit(solution)/shard_map/exchange_cotangent/pallas_call | solution.py:116
  183.1 1.0 multiply_sine_fusion
  184.1 4.7 %attend_back.1 = (bf16[16,256,256]{2,1,0:T(8,128)(2,1)S(1)}, bf16[512,128]{1,0:T(8,128)(2,1)S(1)}) custom-call(bf16[16,256,512]{2,1,0:T(8,128)(2,1)} %get-tuple-element.43.prob_ref, bf16[16,256,256]{2,1,0:T(8,128)(2,1)} %copy-done.4, bf16[2,256,128]{2,1,0:T(8,128)(2,1)S(1)} %get-tuple-element.42.query_ref, ...), custom_call_target="tpu_custom_call" | custom-call | tf_op jit(solution)/shard_map/attend_back/pallas_call | solution.py:421
  188.8 34.3 %exchange_key_grads.1 = (bf16[8,512,256]{2,1,0:T(8,128)(2,1)S(1)}, bf16[4,8,2,32,512]{4,3,2,1,0:T(8,128)(2,1)S(1)}) custom-call(bf16[8,512,256]{2,1,0:T(8,128)(2,1)S(1)} %bitcast.25, bf16[8,2,4,32,512]{4,3,2,1,0:T(8,128)(2,1)S(1)} %bitcast.24), custom_call_target="tpu_custom_call" | custom-call | tf_op jit(solution)/shard_map/exchange_key_grads/pallas_call | solution.py:116
  223.1 1.3 copy-done.8
  224.4 7.6 %weight_terms.1 = (bf16[16,384,256]{2,1,0:T(8,128)(2,1)}, bf16[8,2,32,512]{3,2,1,0:T(8,128)(2,1)S(1)}, f32[32,512]{1,0:T(8,128)}, bf16[8,32,256]{2,1,0:T(8,128)(2,1)S(1)}) custom-call(bf16[8,512,256]{2,1,0:T(8,128)(2,1)S(1)} %get-tuple-element.65.part_ref, bf16[512,128]{1,0:T(8,128)(2,1)S(1)} %get-tuple-element.66.query_grad_ref, ...), custom_call_target="tpu_custom_call" | custom-call | tf_op jit(solution)/shard_map/weight_terms/pallas_call | solution.py:421
  232.0 1.9 copy-done.6
  233.9 50.0 %exchange_weights.1 = (bf16[2,8,384,256]{3,2,1,0:T(8,128)(2,1)S(1)}, bf16[8,2,32,512]{3,2,1,0:T(8,128)(2,1)S(1)}, bf16[8,32,256]{2,1,0:T(8,128)(2,1)S(1)}) custom-call(bf16[16,384,256]{2,1,0:T(8,128)(2,1)S(1)} %copy-done.6, bf16[8,2,32,512]{3,2,1,0:T(8,128)(2,1)S(1)} %get-tuple-element.71.grads, bf16[8,32,256]{2,1,0:T(8,128)(2,1)S(1)} %get-tuple-element.72.out), custom_call_target="tpu_custom_call" | custom-call | tf_op jit(solution)/shard_map/exchange_weights/pallas_call | solution.py:116
  283.9 1.1 weight_sum.1
  285.0 1.6 copy.25
  (38 shorter events, 0.2 us)
Async XLA Ops:
  0.6 3.4 %copy-start.18 = (bf16[256,4096]{1,0:T(8,128)(2,1)S(1)}, bf16[256,4096]{1,0:T(8,128)(2,1)}, u32[]{:S(2)}) copy-start(bf16[256,4096]{1,0:T(8,128)(2,1)} %hidden_ref.1) | copy-start | bytes 6291460
  4.6 53.2 %copy-start = (bf16[256,4096]{1,0:T(8,128)(2,1)}, bf16[256,4096]{1,0:T(8,128)(2,1)S(1)}, u32[]{:S(2)}) copy-start(bf16[256,4096]{1,0:T(8,128)(2,1)S(1)} %fusion.3.normed.normed_ref) | copy-start | bytes 6291460
  11.3 0.9 copy-start.19
  53.9 4.0 %copy-start.4 = (bf16[16,256,256]{2,1,0:T(8,128)(2,1)}, bf16[16,256,256]{2,1,0:T(8,128)(2,1)S(1)}, u32[]{:S(2)}) copy-start(bf16[16,256,256]{2,1,0:T(8,128)(2,1)S(1)} %get-tuple-element.41.kv_ref) | copy-start | bytes 6291460
  57.1 0.7 copy-start.16
  76.7 1.4 copy-start.7
  78.1 5.0 %copy-start.5 = (bf16[8,256,256]{2,1,0:T(8,128)(2,1)}, bf16[8,256,256]{2,1,0:T(8,128)(2,1)S(1)}, u32[]{:S(2)}) copy-start(bf16[8,256,256]{2,1,0:T(8,128)(2,1)S(1)} %get-tuple-element.47.other_ref) | copy-start | bytes 3145732
  78.1 5.8 %copy-start.2 = (bf16[16,256,128]{2,1,0:T(8,128)(2,1)}, bf16[16,256,128]{2,1,0:T(8,128)(2,1)S(1)}, u32[]{:S(2)}) copy-start(bf16[16,256,128]{2,1,0:T(8,128)(2,1)S(1)} %get-tuple-element.46.att_ref.att_all) | copy-start | bytes 3145732
  78.1 18.3 %copy-start.20 = (s32[32,8]{0,1:T(8,128)S(1)}, s32[32,8]{0,1:T(8,128)}, u32[]{:S(2)}) copy-start(s32[32,8]{0,1:T(8,128)} %param.9) | copy-start | bytes 3076
  83.1 0.8 copy-start.12
  95.7 0.7 copy-start.14
  109.1 15.8 %copy-start.1 = (bf16[4096,512]{1,0:T(8,128)(2,1)}, bf16[4096,512]{1,0:T(8,128)(2,1)S(1)}, u32[]{:S(2)}) copy-start(bf16[4096,512]{1,0:T(8,128)(2,1)S(1)} %get-tuple-element.52) | copy-start | bytes 12582916
  109.1 17.1 %copy-start.3 = (bf16[16,256,128]{2,1,0:T(8,128)(2,1)S(1)}, bf16[16,256,128]{2,1,0:T(8,128)(2,1)}, u32[]{:S(2)}) copy-start(bf16[16,256,128]{2,1,0:T(8,128)(2,1)} %copy-done.2) | copy-start | bytes 3145732
  109.1 17.1 %copy-start.13 = (f32[256,512]{1,0:T(8,128)S(1)}, f32[256,512]{1,0:T(8,128)}, u32[]{:S(2)}) copy-start(f32[256,512]{1,0:T(8,128)} %copy-done.12) | copy-start | bytes 1572868
  109.1 17.1 %copy-start.15 = (bf16[256,512]{1,0:T(8,128)(2,1)S(1)}, bf16[256,512]{1,0:T(8,128)(2,1)}, u32[]{:S(2)}) copy-start(bf16[256,512]{1,0:T(8,128)(2,1)} %copy-done.14) | copy-start | bytes 786436
  124.8 1.4 copy-start.10
  126.2 57.9 %copy-start.17 = (f32[128,512]{1,0:T(8,128)S(1)}, f32[128,512]{1,0:T(8,128)}, u32[]{:S(2)}) copy-start(f32[128,512]{1,0:T(8,128)} %copy-done.16) | copy-start | bytes 786436
  133.0 1.3 copy-start.11
  184.1 4.7 %copy-start.9 = (bf16[8,8,32,512]{3,2,1,0:T(8,128)(2,1)S(1)}, bf16[8,8,32,512]{3,2,1,0:T(8,128)(2,1)}, u32[]{:S(2)}) copy-start(bf16[8,8,32,512]{3,2,1,0:T(8,128)(2,1)} %get-tuple-element.64) | copy-start | bytes 6291460
  223.1 1.3 copy-start.8
  232.0 1.9 copy-start.6

commit v4 on v3

--- a/solution.py
+++ b/solution.py
@@ -60,30 +60,21 @@
     return jnp.cos(angles), jnp.sin(angles)
 
 
-def rotate(values, cosine, sine):
-    half_width = HD // 2
-    lower_half = values[..., :half_width]
-    upper_half = values[..., half_width:]
-    cosine = cosine[:, None, :]
-    sine = sine[:, None, :]
-    return jnp.concatenate(
-        [lower_half * cosine - upper_half * sine, upper_half * cosine + lower_half * sine], axis=-1
-    )
-
-
 def place():
     seq = lax.axis_index("seq")
     tp = lax.axis_index("tp")
     return seq, seq // 2, seq % 2, tp
 
 
-def run_exchange(peers, jobs, locals_, send_sems, recv_sems):
+def run_exchange(peers, jobs, locals_, send_sems, recv_sems, forwards=()):
     barrier = pltpu.get_barrier_semaphore()
     for peer in peers:
         pl.semaphore_signal(barrier, inc=1, device_id=peer, device_id_type=MESH)
     pl.semaphore_wait(barrier, len(peers))
     copies = []
-    for number, (source, target, device, *when) in enumerate(jobs):
+
+    def begin(source, target, device, *when):
+        number = len(copies)
         copy = pltpu.make_async_remote_copy(
             src_ref=source,
             dst_ref=target,
@@ -97,6 +88,9 @@
         else:
             copy.start()
         copies.append((copy, when))
+
+    for job in jobs:
+        begin(*job)
     for source, bounce, target, sem in locals_:
         copy = pltpu.make_async_copy(source, bounce, sem)
         copy.start()
@@ -104,12 +98,19 @@
         copy = pltpu.make_async_copy(bounce, target, sem)
         copy.start()
         copy.wait()
-    for copy, when in copies:
+    arrived = set()
+    for number, job in forwards:
+        copies[number][0].wait_recv()
+        arrived.add(number)
+        begin(*job)
+    for number, (copy, when) in enumerate(copies):
         if when:
             pl.when(when[0])(copy.wait_send)
             pl.when(when[1])(copy.wait_recv)
         else:
-            copy.wait()
+            copy.wait_send()
+            if number not in arrived:
+                copy.wait_recv()
 
 
 def exchange(kernel, name, collective_id, ins, outs, copies, bounces):
@@ -126,7 +127,7 @@
         ]
         + [pltpu.VMEM(shape, dtype) for shape, dtype in bounces],
         compiler_params=pltpu.CompilerParams(
-            collective_id=collective_id, has_side_effects=True, vmem_limit_bytes=16 * MIB
+            collective_id=collective_id, has_side_effects=True, vmem_limit_bytes=4 * MIB
         ),
     )(*ins)
 
@@ -189,9 +190,7 @@
     )
 
 
-def attended_kernel(
-    source, w_half, normed, target, w_other, normed_other, send_sems, recv_sems, sem, bounce
-):
+def attended_kernel(source, w_half, target, w_other, send_sems, recv_sems, sem, bounce):
     seq, chip, core, tp = place()
     slot = tp * 2 + core
     partner_seq = chip * 2 + 1 - core
@@ -202,24 +201,22 @@
     rows = [other] + [own] * (TP - 1) + [other] * (TP - 1)
     jobs = [(source.at[part], target.at[slot], peer) for part, peer in zip(rows, peers)]
     jobs.append((w_half, w_other, partner))
-    jobs.append((normed, normed_other, partner))
     run_exchange(
         peers, jobs, [(source.at[own], bounce, target.at[slot], sem)], send_sems, recv_sems
     )
 
 
-def exchange_attended(attended, w_half, normed):
+def exchange_attended(attended, w_half):
     return exchange(
         attended_kernel,
         "exchange_attended",
         2,
-        (attended, w_half, normed),
+        (attended, w_half),
         [
             jax.ShapeDtypeStruct((2 * TP, FR, HD), BF16),
             jax.ShapeDtypeStruct(w_half.shape, BF16),
-            jax.ShapeDtypeStruct(normed.shape, BF16),
-        ],
-        17,
+        ],
+        16,
         [((FR, HD), BF16)],
     )
 
@@ -260,11 +257,23 @@
 
 def message_kernel(source, grads, target, grads_other, send_sems, recv_sems, sem, bounce):
     seq, chip, core, tp = place()
-    partner_seq = chip * 2 + 1 - core
-    peers = tp_peers(seq, tp) + tp_peers(partner_seq, tp) + [(partner_seq, tp)]
+    partner = (chip * 2 + 1 - core, tp)
+    peers = tp_peers(seq, tp)
     jobs = [(source, target.at[core, tp], peer) for peer in peers]
-    jobs.append((grads.at[:, 1 - core], grads_other, peers[-1]))
-    run_exchange(peers, jobs, [(source, bounce, target.at[core, tp], sem)], send_sems, recv_sems)
+    forwards = []
+    for number, hop in enumerate(TP_ORDER):
+        slot = target.at[core, lax.rem(tp - hop + TP, TP)]
+        forwards.append((number, (slot, slot, partner)))
+    jobs.append((source, target.at[core, tp], partner))
+    jobs.append((grads.at[:, 1 - core], grads_other, partner))
+    run_exchange(
+        peers + [partner],
+        jobs,
+        [(source, bounce, target.at[core, tp], sem)],
+        send_sems,
+        recv_sems,
+        forwards,
+    )
 
 
 def exchange_message(message, grads):
@@ -282,26 +291,27 @@
     )
 
 
-def cotangent_kernel(
-    source, side, target, side_all, send_sems, recv_sems, sem, bounce, side_bounce
-):
+def cotangent_kernel(source, side, target, side_x, send_sems, recv_sems, sem, bounce, side_bounce):
     seq, chip, core, tp = place()
     partner_seq = chip * 2 + 1 - core
+    at_x, at_y = chip // 2, chip % 2
     peers = [(partner_seq, tp)] + tp_peers(seq, tp) + tp_peers(partner_seq, tp)
     heads = [1 - core] + [core] * (TP - 1) + [1 - core] * (TP - 1)
     jobs = [
         (source.at[peer[1] * 2 + head], target.at[core, tp], peer)
         for head, peer in zip(heads, peers)
     ]
-    for other in chip_peers(chip, core, tp):
+    for hop in (2, 1, 3):
+        there = lax.rem(at_x + hop, 4)
+        other = (there * 4 + at_y * 2 + core, tp)
         peers.append(other)
-        jobs.append((side.at[other[0] // 2], side_all.at[chip], other))
+        jobs.append((side.at[there], side_x.at[at_x], other))
     run_exchange(
         peers,
         jobs,
         [
             (source.at[tp * 2 + core], bounce, target.at[core, tp], sem),
-            (side.at[chip], side_bounce, side_all.at[chip], sem),
+            (side.at[at_x], side_bounce, side_x.at[at_x], sem),
         ],
         send_sems,
         recv_sems,
@@ -318,14 +328,18 @@
             jax.ShapeDtypeStruct((2, TP, FR, HD), BF16),
             jax.ShapeDtypeStruct(side.shape, BF16),
         ],
-        22,
+        18,
         [((FR, HD), BF16), (side.shape[1:], BF16)],
     )
 
 
-def key_grads_kernel(source, grads, target, grads_z, send_sems, recv_sems, sem, bounce, grads_bounce):
+def key_grads_kernel(
+    source, grads, side, normed, target, grads_z, side_in, normed_other,
+    send_sems, recv_sems, sem, bounce, grads_bounce,
+):
     seq, chip, core, tp = place()
     row, depth_at = tp // 4, tp % 4
+    at_x, at_y = chip // 2, chip % 2
     peers = []
     jobs = []
     for hop in CHIP_ORDER:
@@ -339,6 +353,10 @@
         other = (seq, row * 4 + there)
         peers.append(other)
         jobs.append((grads.at[:, :, there], grads_z.at[depth_at], other))
+    jobs.append((side.at[1 - at_y], side_in, (at_x * 4 + (1 - at_y) * 2 + core, tp)))
+    partner = (chip * 2 + 1 - core, tp)
+    jobs.append((normed, normed_other, partner))
+    peers.append(partner)
     run_exchange(
         peers,
         jobs,
@@ -351,18 +369,20 @@
     )
 
 
-def exchange_key_grads(parts, grads):
+def exchange_key_grads(parts, grads, side, normed):
     slab = (CHIPS, 2) + grads.shape[3:]
     return exchange(
         key_grads_kernel,
         "exchange_key_grads",
         6,
-        (parts, grads),
+        (parts, grads, side, normed),
         [
             jax.ShapeDtypeStruct(parts.shape, parts.dtype),
             jax.ShapeDtypeStruct((4,) + slab, BF16),
-        ],
-        10,
+            jax.ShapeDtypeStruct(side.shape[1:], BF16),
+            jax.ShapeDtypeStruct(normed.shape, BF16),
+        ],
+        12,
         [(parts.shape[1:], parts.dtype), (slab, BF16)],
     )
 
@@ -429,31 +449,105 @@
     )(*ins)
 
 
+def start_kernel(
+    hidden_ref, w_ref, cos_ref, sin_ref, normed_ref, kv_ref, query_ref, out_w_ref, total_ref
+):
+    step = pl.program_id(0)
+    depth_rows = w_ref.shape[0]
+
+    @pl.when(step == 0)
+    def _():
+        hidden = hidden_ref[...].astype(F32)
+        normed_ref[...] = (hidden * rms_scale(hidden)).astype(BF16)
+        total_ref[...] = jnp.zeros_like(total_ref)
+
+    normed = normed_ref[:, pl.ds(pl.multiple_of(step * depth_rows, depth_rows), depth_rows)]
+    weights = w_ref[...].reshape(depth_rows, 8 * HD)
+    total_ref[...] += dot_nn(normed, weights[:, : 6 * HD])
+    out_w = weights[:, 6 * HD :].reshape(-1, TP, 32, 2 * HD)
+    for at in range(TP):
+        for piece in range(out_w.shape[0]):
+            out_w_ref[at, piece * 32 : (piece + 1) * 32] = out_w[piece, at]
+
+    @pl.when(step == pl.num_programs(0) - 1)
+    def _():
+        cosine, sine = cos_ref[...], sin_ref[...]
+
+        def turned(at):
+            lower = total_ref[:, at : at + HD // 2]
+            upper = total_ref[:, at + HD // 2 : at + HD]
+            return jnp.concatenate(
+                [lower * cosine - upper * sine, upper * cosine + lower * sine], axis=1
+            ).astype(BF16)
+
+        for head in range(2):
+            query_ref[head] = turned(head * HD)
+            kv_ref[head, :, :HD] = turned((2 + head) * HD)
+            at = (4 + head) * HD
+            kv_ref[head, :, HD:] = total_ref[:, at : at + HD].astype(BF16)
+
+
+def start(hidden, weights, cosine, sine):
+    steps = 8
+    depth_rows = weights.shape[0] // steps
+
+    def whole(*shape):
+        return pl.BlockSpec(shape, lambda step: (0,) * len(shape))
+
+    return pl.pallas_call(
+        start_kernel,
+        name="start",
+        grid=(steps,),
+        out_shape=[
+            jax.ShapeDtypeStruct(hidden.shape, BF16),
+            jax.ShapeDtypeStruct((2, FR, 2 * HD), BF16),
+            jax.ShapeDtypeStruct((2, FR, HD), BF16),
+            jax.ShapeDtypeStruct((TP, NS, 2 * HD), BF16),
+        ],
+        in_specs=[
+            whole(*hidden.shape),
+            pl.BlockSpec((depth_rows, 4, 2 * HD), lambda step: (step, 0, 0)),
+            whole(*cosine.shape),
+            whole(*sine.shape),
+        ],
+        out_specs=[
+            whole(*hidden.shape),
+            whole(2, FR, 2 * HD),
+            whole(2, FR, HD),
+            pl.BlockSpec((TP, depth_rows // TP, 2 * HD), lambda step: (0, step, 0)),
+        ],
+        scratch_shapes=[pltpu.VMEM((FR, 6 * HD), F32)],
+        compiler_params=pltpu.CompilerParams(vmem_limit_bytes=24 * MIB),
+    )(hidden, weights, cosine, sine)
+
+
 def attend_kernel(kv_ref, query_ref, out_ref, prob_ref, out_t_ref, inverse_ref, score_ref):
     chip = lax.axis_index("seq") // 2
-    blocks = 2 * chip + 2
     query = query_ref[...].reshape(FR2, HD)
-    key_at = lax.broadcasted_iota(jnp.int32, (FR, FR2), 0)
-    query_at = lax.broadcasted_iota(jnp.int32, (FR, FR2), 1) + chip * FR2
+    scale = math.log2(math.e) / math.sqrt(HD)
+    key_at = lax.broadcasted_iota(jnp.int32, (FR2, FR2), 0)
+    query_at = lax.broadcasted_iota(jnp.int32, (FR2, FR2), 1)
 
     def scores(block, top):
-        score = dot_nt(kv_ref[block][:, :HD], query) * (1.0 / math.sqrt(HD))
-        score = jnp.where(key_at + block * FR <= query_at, score, MASKED)
+        score = dot_nt(kv_ref[block, :, :HD], query) * scale
         score_ref[block] = score
         return jnp.maximum(top, jnp.max(score, axis=0, keepdims=True))
 
-    top = lax.fori_loop(0, blocks, scores, jnp.full((1, FR2), MASKED, F32))
+    score = dot_nt(kv_ref[chip, :, :HD], query) * scale
+    score = jnp.where(key_at <= query_at, score, MASKED)
+    score_ref[chip] = score
+    top = lax.fori_loop(0, chip, scores, jnp.max(score, axis=0, keepdims=True))
 
     def weigh(block, carry):
         total, mixed = carry
-        prob = jnp.exp(score_ref[block] - top)
+        prob = jnp.exp2(score_ref[block] - top)
         total = total + jnp.sum(prob, axis=0, keepdims=True)
         prob = prob.astype(BF16)
         prob_ref[block] = prob
-        return total, mixed + dot_tn(kv_ref[block][:, HD:], prob)
+        return total, mixed + dot_tn(kv_ref[block, :, HD:], prob)
 
     total, mixed = lax.fori_loop(
-        0, blocks, weigh, (jnp.zeros((1, FR2), F32), jnp.zeros((HD, FR2), F32))
+        0, chip + 1, weigh, (jnp.zeros((1, FR2), F32), jnp.zeros((HD, FR2), F32))
     )
     inverse = 1.0 / total
     mixed = mixed * inverse
@@ -469,11 +563,12 @@
         (kv_all, query_two),
         [
             jax.ShapeDtypeStruct((FR2, HD), BF16),
-            jax.ShapeDtypeStruct((2 * CHIPS, FR, FR2), BF16),
+            jax.ShapeDtypeStruct((CHIPS, FR2, FR2), BF16),
             jax.ShapeDtypeStruct((HD, FR2), F32),
             jax.ShapeDtypeStruct((1, FR2), F32),
         ],
-        [pltpu.VMEM((2 * CHIPS, FR, FR2), F32)],
+        [pltpu.VMEM((CHIPS, FR2, FR2), F32)],
+        limit=24,
     )
 
 
@@ -514,8 +609,11 @@
     squares = jnp.sum(merged * merged, axis=-1, keepdims=True)
     copy.wait()
     latent = dot_nn(rounded, depth_in_ref[...].reshape(NS, DD))
-    part_ref[:, :, :DD] = latent.reshape(TP, FR // TP, DD)
-    part_ref[:, :, DD:] = jnp.broadcast_to(squares, (FR, HD)).reshape(TP, FR // TP, HD)
+    coarse = squares.astype(BF16)
+    fine = (squares - coarse.astype(F32)).astype(BF16)
+    part_ref[:, :, :DD] = latent.astype(BF16).reshape(TP, FR // TP, DD)
+    part_ref[:, :, DD : DD + HD] = jnp.broadcast_to(coarse, (FR, HD)).reshape(TP, FR // TP, HD)
+    part_ref[:, :, DD + HD :] = jnp.broadcast_to(fine, (FR, HD)).reshape(TP, FR // TP, HD)
 
 
 def merge(att_all, w_half, w_other, hidden, depth_in):
@@ -526,10 +624,11 @@
         [
             jax.ShapeDtypeStruct((FR, NS), F32),
             jax.ShapeDtypeStruct((FR, NS), BF16),
-            jax.ShapeDtypeStruct((TP, FR // TP, DD + HD), F32),
+            jax.ShapeDtypeStruct((TP, FR // TP, DD + 2 * HD), BF16),
         ],
         [pltpu.VMEM((2 * CHIPS, 32, DD), BF16), pltpu.SemaphoreType.DMA],
         hbm=1,
+        limit=24,
     )
 
 
@@ -541,9 +640,10 @@
     out_rows = stack_ref[3 * DD : 4 * DD]
     head_rows = stack_ref[4 * DD : 4 * DD + VOCAB]
     embed_rows = stack_ref[4 * DD + VOCAB :]
-    total = jnp.sum(part_ref[...], axis=0)
+    total = jnp.sum(part_ref[...].astype(F32), axis=0)
     raw = total[:, :DD]
-    scale_in = lax.rsqrt(total[:, DD : DD + 1] * (1.0 / width) + EPSILON)
+    squares = total[:, DD : DD + 1] + total[:, DD + HD : DD + HD + 1]
+    scale_in = lax.rsqrt(squares * (1.0 / width) + EPSILON)
     latent = raw * scale_in
     latent = jnp.broadcast_to(latent[:, None, :], (frames, books, DD)).reshape(tokens, DD)
     vocab_at = lax.broadcasted_iota(jnp.int32, (tokens, VOCAB), 1)
@@ -621,6 +721,7 @@
             jax.ShapeDtypeStruct(stack.shape, BF16),
         ],
         [pltpu.VMEM((DD // DHD, tokens, tokens), F32)],
+        limit=32,
     )
 
 
@@ -718,14 +819,15 @@
             pltpu.SemaphoreType.DMA((2,)),
         ],
         hbm=2,
+        limit=28,
     )
 
 
 def attend_back_kernel(
-    prob_ref, kv_ref, query_ref, part_ref, out_t_ref, inverse_ref, cos_ref, sin_ref, grad_ref, query_grad_ref
+    prob_ref, kv_ref, query_ref, part_ref, out_t_ref, inverse_ref, cos_ref, sin_ref, side_x_ref,
+    grad_ref, query_grad_ref, side_ref,
 ):
     chip = lax.axis_index("seq") // 2
-    blocks = 2 * chip + 2
     query = query_ref[...].reshape(FR2, HD)
     gradient = jnp.sum(part_ref[...].astype(F32), axis=1).reshape(FR2, HD)
     gradient = gradient.astype(BF16).astype(F32)
@@ -743,31 +845,33 @@
         grad_ref[block, :, HD:] = dot_nn(prob, gradient).astype(BF16)
         return query_grad + dot_tn(kv_ref[block, :, :HD], score_grad)
 
-    query_grad = lax.fori_loop(0, blocks, step, jnp.zeros((HD, FR2), F32)) * scale
-
+    query_grad = lax.fori_loop(0, chip + 1, step, jnp.zeros((HD, FR2), F32)) * scale
     query_grad = query_grad.T
     lower, upper = query_grad[:, : HD // 2], query_grad[:, HD // 2 :]
     cosine, sine = cos_ref[...], sin_ref[...]
     query_grad_ref[...] = jnp.concatenate(
         [lower * cosine + upper * sine, upper * cosine - lower * sine], axis=1
     ).astype(BF16)
-
-
-def attend_back(probs, kv_all, query_two, parts, out_t, inverse, cosine, sine):
+    side_ref[...] = jnp.sum(side_x_ref[...].astype(F32), axis=0).astype(BF16)
+
+
+def attend_back(probs, kv_all, query_two, parts, out_t, inverse, cosine, sine, side_x):
     return compute(
         attend_back_kernel,
         "attend_back",
-        (probs, kv_all, query_two, parts, out_t, inverse, cosine, sine),
-        [
-            jax.ShapeDtypeStruct((2 * CHIPS, FR, 2 * HD), BF16),
+        (probs, kv_all, query_two, parts, out_t, inverse, cosine, sine, side_x),
+        [
+            jax.ShapeDtypeStruct((CHIPS, FR2, 2 * HD), BF16),
             jax.ShapeDtypeStruct((FR2, HD), BF16),
-        ],
+            jax.ShapeDtypeStruct(side_x.shape[1:], BF16),
+        ],
+        limit=28,
     )
 
 
 def weight_kernel(
     part_ref, query_grad_ref, cos_ref, sin_ref, normed_ref, other_ref, grads_z_ref, side_ref,
-    out_ref, grads_ref, win_ref, out_w_ref,
+    side_in_ref, out_ref, grads_ref, win_ref, out_w_ref,
 ):
     chip = lax.axis_index("seq") // 2
     core = lax.axis_index("seq") % 2
@@ -798,23 +902,24 @@
         out_ref[piece] = term.astype(BF16)
     for at in range(CHIPS):
         grads_ref[at] = jnp.sum(grads_z_ref[:, at].astype(F32), axis=0).astype(BF16)
-    side = jnp.sum(side_ref[...].astype(F32), axis=0)
+    side = side_ref[chip % 2].astype(F32) + side_in_ref[...].astype(F32)
     win_ref[...] = side[:, TP * FR :]
     for at in range(TP):
         out_w_ref[at] = side[:, at * FR : (at + 1) * FR].astype(BF16)
 
 
-def weight_terms(parts, query_grad, cosine, sine, normed, normed_other, grads_z, side_all):
+def weight_terms(parts, query_grad, cosine, sine, normed, normed_other, grads_z, side, side_in):
     return compute(
         weight_kernel,
         "weight_terms",
-        (parts, query_grad, cosine, sine, normed, normed_other, grads_z, side_all),
+        (parts, query_grad, cosine, sine, normed, normed_other, grads_z, side, side_in),
         [
             jax.ShapeDtypeStruct((2 * CHIPS, 3 * HD, FR), BF16),
             jax.ShapeDtypeStruct(grads_z.shape[1:], BF16),
             jax.ShapeDtypeStruct((32, DD), F32),
             jax.ShapeDtypeStruct((TP, 32, FR), BF16),
         ],
+        limit=28,
     )
 
 
@@ -836,6 +941,7 @@
             jax.ShapeDtypeStruct((4, FR, 2 * HD), F32),
             jax.ShapeDtypeStruct(grads_all.shape[2:], F32),
         ],
+        limit=16,
     )
 
 
@@ -849,24 +955,14 @@
     total_frames = FR * seq_count
     loss_scale = 1.0 / math.sqrt(total_frames * book_count)
 
-    hidden_full = hidden_in.astype(F32)
-    normed = (hidden_full * rms_scale(hidden_full)).astype(BF16)
-    projected = jnp.einsum(
-        "wo,obu->wbu", normed, temporal_weight_stack[:, :3, :], preferred_element_type=F32
-    )
     cosine, sine = angle_tables(seq_index * FR, FR)
-    query = rotate(projected[:, 0].reshape(FR, 2, HD), cosine, sine).astype(BF16)
-    key = rotate(projected[:, 1].reshape(FR, 2, HD), cosine, sine).astype(BF16)
-    value = projected[:, 2].reshape(FR, 2, HD).astype(BF16)
-    kv = jnp.concatenate([key, value], axis=-1).transpose(1, 0, 2)
-    query = query.transpose(1, 0, 2)
-    out_w = temporal_weight_stack[:, 3, :].reshape(seq_count, TP, -1, 2 * HD)
-    out_w = out_w.transpose(1, 0, 2, 3).reshape(TP, NS, 2 * HD)
+    normed, kv, query, out_w = start(hidden_in, temporal_weight_stack, cosine, sine)
     kv_all, query_two, w_half = exchange_keys(kv, query, out_w)
+    kv_all = kv_all.reshape(CHIPS, FR2, 2 * HD)
 
     depth_in = depth_in.reshape(seq_count, TP, -1, DD)
     attended, probs, out_t, inverse = attend(kv_all, query_two)
-    att_all, w_other, normed_other = exchange_attended(attended, w_half, normed)
+    att_all, w_other = exchange_attended(attended, w_half)
     merged, rounded, latent_parts = merge(att_all, w_half, w_other, hidden_in, depth_in)
     latent_parts, att_other, rounded_other = exchange_latent(latent_parts, att_all, rounded)
     before = jnp.concatenate(
@@ -890,17 +986,17 @@
         grads,
         depth_in,
     )
-    cotangent_parts, side_all = exchange_cotangent(cotangent_parts, side)
+    cotangent_parts, side = exchange_cotangent(cotangent_parts, side.reshape(4, 2, 32, -1))
 
     cosine, sine = angle_tables(chip * FR2, FR2)
-    key_parts, query_grad = attend_back(
-        probs, kv_all, query_two, cotangent_parts, out_t, inverse, cosine, sine
-    )
-    key_parts, grads_z = exchange_key_grads(
-        key_parts.reshape(CHIPS, FR2, 2 * HD), grads.reshape(CHIPS, 2, 4, -1, DD)
+    key_parts, query_grad, side = attend_back(
+        probs, kv_all, query_two, cotangent_parts, out_t, inverse, cosine, sine, side
+    )
+    key_parts, grads_z, side_in, normed_other = exchange_key_grads(
+        key_parts, grads.reshape(CHIPS, 2, 4, -1, DD), side, normed
     )
     parts, grads, grad_win, out_parts = weight_terms(
-        key_parts, query_grad, cosine, sine, normed, normed_other, grads_z, side_all
+        key_parts, query_grad, cosine, sine, normed, normed_other, grads_z, side, side_in
     )
     grad_temporal, grad_depth = weight_sum(*exchange_weights(parts, grads, out_parts))
     return grad_temporal.transpose(1, 0, 2), grad_win, grad_depth

time: 287 us -> 246 us (0.86)
  Pallas kernels: 250 us -> 216 us
  matrix products: 6.69 us -> 0 us
  other arithmetic: 7.85 us -> 1.53 us
  local copies, waits for them, and re-layouts: 20.7 us -> 25.8 us
    pallas_call x7, Pallas kernels: 210 us -> 188 us  [exchange(): pl.pallas_call(kernel, name=name, out_shape=outs, in_specs=[ANY] * len(in...]
    pallas_call x7, Pallas kernels: 40.6 us -> 22.3 us  [compute(): pl.pallas_call(kernel, name=name, out_shape=outs, in_specs=[VMEM] * (len(...]
    unnamed x50 -> x63, local copies, waits for them, and re-layouts: 12.9 us -> 22.9 us
    slice x5 -> x0, local copies, waits for them, and re-layouts: 7.17 us -> none  [the longest x1 6.13 us: per_device(): out_w = temporal_weight_stack[:, 3, :].reshape(seq_count, TP, -1, 2 * HD)]
    dot_general x1 -> x0, matrix products: 6.69 us -> none  [per_device(): jnp.einsum('wo,obu->wbu', normed, temporal_weight_stack[:, :3, :], prefer...]
    pallas_call x0 -> x1, Pallas kernels: none -> 6.07 us  [start(): pl.pallas_call(start_kernel, name='start', grid=(steps,), out_shape=[jax....]
where the time goes in v4:
time: 246 us; the launch traced here: 245 us
  Pallas kernels  216 us (88%)
  local copies, waits for them, and re-layouts  25.8 us (10%)
    pallas_call x7, Pallas kernels, exchange(): pl.pallas_call(kernel, name=name, out_shape=outs, in_specs=[ANY] * len(in...  188 us
    unnamed x63, local copies, waits for them, and re-layouts  22.9 us
    pallas_call x7, Pallas kernels, compute(): pl.pallas_call(kernel, name=name, out_shape=outs, in_specs=[VMEM] * (len(...  22.3 us
    pallas_call x1, Pallas kernels, start(): pl.pallas_call(start_kernel, name='start', grid=(steps,), out_shape=[jax....  6.07 us

profile of v4, /device:TPU:1, one launch (start us, length us, event | category | flops | bytes accessed | tf_op | source)
XLA Modules:
  0.0 244.6 jit_solution(6959149411914007595)
XLA Ops:
  0.7 0.5 multiply_sine_fusion.1
  1.2 0.0 copy-start.2
  1.2 3.4 %copy-done.2 = bf16[4096,4,256]{2,1,0:T(4,128)(2,1)S(1)} copy-done((bf16[4096,4,256]{2,1,0:T(4,128)(2,1)S(1)}, bf16[4096,4,256]{2,1,0:T(4,128)(2,1)}, u32[]{:S(2)}) %copy-start.2) | copy-done | bytes 8388632
  4.6 1.6 copy-done.7
  6.2 6.1 %start.1 = (bf16[256,4096]{1,0:T(8,128)(2,1)S(1)}, bf16[2,256,256]{2,1,0:T(8,128)(2,1)S(1)}, bf16[2,256,128]{2,1,0:T(8,128)(2,1)S(1)}, bf16[8,512,256]{2,1,0:T(8,128)(2,1)S(1)}) custom-call(bf16[256,4096]{1,0:T(8,128)(2,1)S(1)} %copy-done.7, bf16[4096,4,256]{2,1,0:T(4,128)(2,1)S(1)} %copy-done.2, f32[256,64]{1,0:T(8,128)S(1)} %get-tuple-element.100.cos_ref, ...), custom_call_target="tpu_custom_call" | custom-call | tf_op jit(solution)/shard_map/start/pallas_call | solution.py:497
  12.3 1.4 copy-done.3
  13.6 30.1 %exchange_keys.1 = (bf16[16,256,256]{2,1,0:T(8,128)(2,1)S(1)}, bf16[2,256,128]{2,1,0:T(8,128)(2,1)S(1)}, bf16[8,256,256]{2,1,0:T(8,128)(2,1)S(1)}) custom-call(bf16[2,256,256]{2,1,0:T(8,128)(2,1)S(1)} %get-tuple-element.47.kv, bf16[2,256,128]{2,1,0:T(8,128)(2,1)S(1)} %get-tuple-element.48.query, bf16[8,512,256]{2,1,0:T(8,128)(2,1)S(1)} %get-tuple-element.49.out_w), custom_call_target="tpu_custom_call" | custom-call | tf_op jit(solution)/shard_map/exchange_keys/pallas_call | solution.py:117
  43.8 1.0 attend.1
  44.8 0.0 copy-start.10
  44.8 0.0 copy-start.27
  44.8 0.4 copy-done.5
  45.2 18.9 %exchange_attended.1 = (bf16[16,256,128]{2,1,0:T(8,128)(2,1)S(1)}, bf16[8,256,256]{2,1,0:T(8,128)(2,1)S(1)}) custom-call(bf16[512,128]{1,0:T(8,128)(2,1)S(1)} %get-tuple-element.53.source, bf16[8,256,256]{2,1,0:T(8,128)(2,1)S(1)} %get-tuple-element.54.w_half.half_ref), custom_call_target="tpu_custom_call" | custom-call | tf_op jit(solution)/shard_map/exchange_attended/pallas_call | solution.py:117
  64.0 0.0 copy-done.8
  64.0 0.0 copy-done
  64.1 0.0 copy-start.29
  64.1 1.7 merge.1
  65.8 8.7 %exchange_latent.1 = (bf16[8,32,768]{2,1,0:T(8,128)(2,1)S(1)}, bf16[16,256,128]{2,1,0:T(8,128)(2,1)S(1)}, bf16[256,512]{1,0:T(8,128)(2,1)S(1)}) custom-call(bf16[8,32,768]{2,1,0:T(8,128)(2,1)S(1)} %get-tuple-element.57.source, bf16[16,256,128]{2,1,0:T(8,128)(2,1)S(1)} %get-tuple-element.55.att_ref.att_all, ...), custom_call_target="tpu_custom_call" | custom-call | tf_op jit(solution)/shard_map/exchange_latent/pallas_call | solution.py:117
  74.6 0.0 copy-start.14
  74.6 1.0 copy-done.14
  75.6 0.8 copy-done.23
  76.3 0.7 copy-done.25
  77.0 0.1 copy.16
  77.1 0.7 concatenate.3.clone
  77.8 0.8 reshape.51.before_ref
  78.6 0.7 copy.12
  79.3 1.5 reshape.52.code_ref
  80.8 2.2 copy-done.9
  82.9 0.9 copy-done.20
  83.8 1.0 copy-done.24
  84.9 10.1 %depth.1 = (bf16[32,768]{1,0:T(8,128)(2,1)S(1)}, bf16[4096,512]{1,0:T(8,128)(2,1)S(1)}) custom-call(bf16[8,32,768]{2,1,0:T(8,128)(2,1)S(1)} %copy-done.24, bf16[4096,512]{1,0:T(8,128)(2,1)S(1)} %copy-done.9, s32[256,1]{1,0:T(8,128)S(1)} %reshape.51.before_ref, s32[256,1]{1,0:T(8,128)S(1)} %copy-done.20), custom_call_target="tpu_custom_call" | custom-call | tf_op jit(solution)/shard_map/depth/pallas_call | solution.py:441
  94.9 0.0 copy-start.1
  94.9 11.6 %exchange_message.1 = (bf16[2,8,32,768]{3,2,1,0:T(8,128)(2,1)S(1)}, bf16[8,8,32,512]{3,2,1,0:T(8,128)(2,1)S(1)}) custom-call(bf16[32,768]{1,0:T(8,128)(2,1)S(1)} %get-tuple-element.60.source, bf16[8,2,8,32,512]{4,3,2,1,0:T(8,128)(2,1)S(1)} %bitcast.9), custom_call_target="tpu_custom_call" | custom-call | tf_op jit(solution)/shard_map/exchange_message/pallas_call | solution.py:117
  106.6 2.9 %unmerge.1 = (bf16[16,256,128]{2,1,0:T(8,128)(2,1)S(1)}, bf16[8,32,2560]{2,1,0:T(8,128)(2,1)S(1)}, bf16[8,8,32,512]{3,2,1,0:T(8,128)(2,1)S(1)}) custom-call(bf16[2,8,32,768]{3,2,1,0:T(8,128)(2,1)S(1)} %get-tuple-element.62.message_ref, f32[256,512]{1,0:T(8,128)S(1)} %copy-done.19, bf16[256,512]{1,0:T(8,128)(2,1)S(1)} %get-tuple-element.58.merged.round_ref, ...), custom_call_target="tpu_custom_call" | custom-call | tf_op jit(solution)/shard_map/unmerge/pallas_call | solution.py:441
  109.5 1.3 copy-done.12
  110.8 34.6 %exchange_cotangent.1 = (bf16[2,8,256,128]{3,2,1,0:T(8,128)(2,1)S(1)}, bf16[4,2,32,2560]{3,2,1,0:T(8,128)(2,1)S(1)}) custom-call(bf16[16,256,128]{2,1,0:T(8,128)(2,1)S(1)} %get-tuple-element.67.source, bf16[4,2,32,2560]{3,2,1,0:T(8,128)(2,1)S(1)} %bitcast.14), custom_call_target="tpu_custom_call" | custom-call | tf_op jit(solution)/shard_map/exchange_cotangent/pallas_call | solution.py:117
  145.4 0.0 copy-start.16
  145.4 1.0 copy-done.16
  146.4 1.0 multiply_sine_fusion
  147.4 2.2 copy-done.11
  149.6 1.2 copy-done.17
  150.8 0.9 copy-done.28
  151.7 1.6 attend_back.1
  153.4 0.6 copy-done.13
  153.9 33.5 %exchange_key_grads.1 = (bf16[8,512,256]{2,1,0:T(8,128)(2,1)S(1)}, bf16[4,8,2,32,512]{4,3,2,1,0:T(8,128)(2,1)S(1)}, bf16[32,2560]{1,0:T(8,128)(2,1)S(1)}, bf16[256,4096]{1,0:T(8,128)(2,1)S(1)}) custom-call(bf16[8,512,256]{2,1,0:T(8,128)(2,1)S(1)} %get-tuple-element.73.source, bf16[8,2,4,32,512]{4,3,2,1,0:T(8,128)(2,1)S(1)} %bitcast.13, ...), custom_call_target="tpu_custom_call" | custom-call | tf_op jit(solution)/shard_map/exchange_key_grads/pallas_call | solution.py:117
  187.5 3.9 %weight_terms.1 = (bf16[16,384,256]{2,1,0:T(8,128)(2,1)S(1)}, bf16[8,2,32,512]{3,2,1,0:T(8,128)(2,1)S(1)}, f32[32,512]{1,0:T(8,128)}, bf16[8,32,256]{2,1,0:T(8,128)(2,1)S(1)}) custom-call(bf16[8,512,256]{2,1,0:T(8,128)(2,1)S(1)} %get-tuple-element.77.part_ref, bf16[512,128]{1,0:T(8,128)(2,1)S(1)} %get-tuple-element.78.query_grad_ref, ...), custom_call_target="tpu_custom_call" | custom-call | tf_op jit(solution)/shard_map/weight_terms/pallas_call | solution.py:441
  191.4 50.4 %exchange_weights.1 = (bf16[2,8,384,256]{3,2,1,0:T(8,128)(2,1)S(1)}, bf16[8,2,32,512]{3,2,1,0:T(8,128)(2,1)S(1)}, bf16[8,32,256]{2,1,0:T(8,128)(2,1)S(1)}) custom-call(bf16[16,384,256]{2,1,0:T(8,128)(2,1)S(1)} %get-tuple-element.82.source, bf16[8,2,32,512]{3,2,1,0:T(8,128)(2,1)S(1)} %get-tuple-element.83.grads, bf16[8,32,256]{2,1,0:T(8,128)(2,1)S(1)} %get-tuple-element.84.out), custom_call_target="tpu_custom_call" | custom-call | tf_op jit(solution)/shard_map/exchange_weights/pallas_call | solution.py:117
  241.8 1.1 weight_sum.1
  243.0 1.6 copy.15
  (38 shorter events, 0.1 us)
Async XLA Ops:
  1.2 3.4 %copy-start.2 = (bf16[4096,4,256]{2,1,0:T(4,128)(2,1)S(1)}, bf16[4096,4,256]{2,1,0:T(4,128)(2,1)}, u32[]{:S(2)}) copy-start(bf16[4096,4,256]{2,1,0:T(4,128)(2,1)} %w_ref.1) | copy-start | bytes 25165828
  4.6 1.6 copy-start.7
  6.2 57.9 %copy-start.8 = (bf16[256,4096]{1,0:T(8,128)(2,1)S(1)}, bf16[256,4096]{1,0:T(8,128)(2,1)}, u32[]{:S(2)}) copy-start(bf16[256,4096]{1,0:T(8,128)(2,1)} %hidden_ref.3) | copy-start | bytes 6291460
  12.2 1.4 copy-start.3
  13.6 50.4 %copy-start = (bf16[4096,512]{1,0:T(8,128)(2,1)S(1)}, bf16[4096,512]{1,0:T(8,128)(2,1)}, u32[]{:S(2)}) copy-start(bf16[4096,512]{1,0:T(8,128)(2,1)} %param.7) | copy-start | bytes 12582916
  43.8 1.4 copy-start.5
  43.8 22.0 %copy-start.21 = (bf16[2,256,128]{2,1,0:T(8,128)(2,1)}, bf16[2,256,128]{2,1,0:T(8,128)(2,1)S(1)}, u32[]{:S(2)}) copy-start(bf16[2,256,128]{2,1,0:T(8,128)(2,1)S(1)} %get-tuple-element.51.query_ref) | copy-start | bytes 393220
  44.8 21.1 %copy-start.10 = (bf16[8,512,512]{2,1,0:T(8,128)(2,1)}, bf16[8,512,512]{2,1,0:T(8,128)(2,1)S(1)}, u32[]{:S(2)}) copy-start(bf16[8,512,512]{2,1,0:T(8,128)(2,1)S(1)} %get-tuple-element.52.prob_ref) | copy-start | bytes 12582916
  44.8 21.1 %copy-start.27 = (f32[128,512]{1,0:T(8,128)}, f32[128,512]{1,0:T(8,128)S(1)}, u32[]{:S(2)}) copy-start(f32[128,512]{1,0:T(8,128)S(1)} %get-tuple-element.70.out_t_ref) | copy-start | bytes 786436
  64.1 13.0 %copy-start.29 = (s32[32,8]{0,1:T(8,128)S(1)}, s32[32,8]{0,1:T(8,128)}, u32[]{:S(2)}) copy-start(s32[32,8]{0,1:T(8,128)} %param.9) | copy-start | bytes 3076
  65.8 8.7 %copy-start.18 = (f32[256,512]{1,0:T(8,128)}, f32[256,512]{1,0:T(8,128)S(1)}, u32[]{:S(2)}) copy-start(f32[256,512]{1,0:T(8,128)S(1)} %get-tuple-element.63.merged_ref) | copy-start | bytes 1572868
  74.6 1.0 copy-start.14
  75.6 0.8 copy-start.23
  76.3 0.7 copy-start.25
  80.8 2.2 copy-start.9
  82.9 0.9 copy-start.20
  83.8 1.0 copy-start.24
  84.8 21.7 %copy-start.15 = (bf16[16,256,128]{2,1,0:T(8,128)(2,1)S(1)}, bf16[16,256,128]{2,1,0:T(8,128)(2,1)}, u32[]{:S(2)}) copy-start(bf16[16,256,128]{2,1,0:T(8,128)(2,1)} %copy-done.14) | copy-start | bytes 3145732
  84.8 21.7 %copy-start.19 = (f32[256,512]{1,0:T(8,128)S(1)}, f32[256,512]{1,0:T(8,128)}, u32[]{:S(2)}) copy-start(f32[256,512]{1,0:T(8,128)} %copy-done.18) | copy-start | bytes 1572868
  84.8 21.7 %copy-start.26 = (bf16[256,512]{1,0:T(8,128)(2,1)S(1)}, bf16[256,512]{1,0:T(8,128)(2,1)}, u32[]{:S(2)}) copy-start(bf16[256,512]{1,0:T(8,128)(2,1)} %copy-done.25) | copy-start | bytes 786436
  94.9 11.6 %copy-start.1 = (bf16[4096,512]{1,0:T(8,128)(2,1)S(1)}, bf16[4096,512]{1,0:T(8,128)(2,1)}, u32[]{:S(2)}) copy-start(bf16[4096,512]{1,0:T(8,128)(2,1)} %param.7) | copy-start | bytes 12582916
  109.4 1.3 copy-start.12
  110.8 36.6 %copy-start.6 = (bf16[16,256,256]{2,1,0:T(8,128)(2,1)S(1)}, bf16[16,256,256]{2,1,0:T(8,128)(2,1)}, u32[]{:S(2)}) copy-start(bf16[16,256,256]{2,1,0:T(8,128)(2,1)} %copy-done.5) | copy-start | bytes 6291460
  110.8 36.6 %copy-start.22 = (bf16[2,256,128]{2,1,0:T(8,128)(2,1)S(1)}, bf16[2,256,128]{2,1,0:T(8,128)(2,1)}, u32[]{:S(2)}) copy-start(bf16[2,256,128]{2,1,0:T(8,128)(2,1)} %copy-done.21) | copy-start | bytes 393220
  145.4 1.0 copy-start.16
  147.4 2.2 copy-start.11
  149.6 1.2 copy-start.17
  150.8 0.9 copy-start.28
  151.7 1.6 copy-start.4
  151.7 2.2 copy-start.13

commit v5 on v4

--- a/solution.py
+++ b/solution.py
@@ -27,8 +27,14 @@
 BF16 = jnp.bfloat16
 ANY = pl.BlockSpec(memory_space=pl.ANY)
 VMEM = pl.BlockSpec(memory_space=pltpu.VMEM)
+HBM = pl.BlockSpec(memory_space=pltpu.HBM)
 TP_ORDER = (4, 1, 3, 5, 7, 2, 6)
 CHIP_ORDER = (2, 6, 1, 4, 3, 7, 5)
+LOG_SCALE = math.log2(math.e) / math.sqrt(HD)
+Z_EARLY = 3
+Z_LATE = CHIPS - Z_EARLY
+X_ROWS = 160
+Y_ROWS = 224
 
 
 def dot_nn(left, right):
@@ -66,7 +72,9 @@
     return seq, seq // 2, seq % 2, tp
 
 
-def run_exchange(peers, jobs, locals_, send_sems, recv_sems, forwards=()):
+def run_exchange(
+    peers, jobs, locals_, send_sems, recv_sems, forwards=(), relay=None, relay_after=()
+):
     barrier = pltpu.get_barrier_semaphore()
     for peer in peers:
         pl.semaphore_signal(barrier, inc=1, device_id=peer, device_id_type=MESH)
@@ -103,6 +111,11 @@
         copies[number][0].wait_recv()
         arrived.add(number)
         begin(*job)
+    if relay is not None:
+        for number in relay_after:
+            copies[number][0].wait_recv()
+            arrived.add(number)
+        relay(len(copies), send_sems, recv_sems)
     for number, (copy, when) in enumerate(copies):
         if when:
             pl.when(when[0])(copy.wait_send)
@@ -132,6 +145,122 @@
     )(*ins)
 
 
+RELAY_COPIES = 23
+
+
+def relay_blocks(own, slot, mirrored, base, send_sems, recv_sems):
+    seq, chip, core, tp = place()
+    at_x, at_y = chip // 2, chip % 2
+    column = 3 - at_x if mirrored else at_x
+    line = 1 - at_y if mirrored else at_y
+
+    def real(x):
+        return 3 - x if mirrored else x
+
+    def block(source, item):
+        row = 1 - at_y if item == 2 else at_y
+        return slot(real(source) * 2 + row, 0 if item == 0 else 1)
+
+    def copy(number, source, target, x, y):
+        return pltpu.make_async_remote_copy(
+            src_ref=source,
+            dst_ref=target,
+            send_sem=send_sems.at[base + number],
+            recv_sem=recv_sems.at[base + number],
+            device_id=(x * 4 + y * 2 + core, tp),
+            device_id_type=MESH,
+        )
+
+    paths = ((0, 1), (0, 3), (0, 2), (1, 2), (1, 3), (2, 3))
+    hops = {}
+    for at, (source, target) in enumerate(paths):
+        relayed = (source, target) in ((0, 2), (1, 3))
+        for item in range(3):
+            there = block(source, item)
+            here = there if relayed or item == 2 else own(item)
+            hops[source, target, item] = copy(at * 3 + item, here, there, real(target), at_y)
+    across_a = copy(18, own(0), slot(chip, 0), at_x, 1 - at_y)
+    across_b = copy(19, own(1), slot(chip, 1), at_x, 1 - at_y)
+    across = [
+        copy(20 + source, block(source, 0), block(source, 0), at_x, 1 - at_y)
+        for source in range(3)
+    ]
+    sends_b = (line == 0) | (column < 3)
+    gets_b = (line == 1) | (column < 3)
+    pl.when(line == 0)(across_a.start)
+    pl.when(sends_b)(across_b.start)
+
+    def begin(items):
+        for at in range(3):
+
+            @pl.when(column == at)
+            def _():
+                for item in items:
+                    hops[at, at + 1, item].start()
+                    if at == 0:
+                        hops[0, 3, item].start()
+
+    begin((0, 1))
+    pl.when(gets_b)(across_b.wait_recv)
+    begin((2,))
+
+    @pl.when(column == 1)
+    def _():
+        for item in range(3):
+            hops[0, 1, item].wait_recv()
+            if item == 0:
+                across[0].start()
+
+    @pl.when(column == 2)
+    def _():
+        for item in range(3):
+            hops[1, 2, item].wait_recv()
+            hops[1, 3, item].start()
+            if item == 0:
+                across[1].start()
+        for item in range(3):
+            hops[0, 2, item].wait_recv()
+            if item == 0:
+                across[0].start()
+
+    @pl.when(column == 3)
+    def _():
+        for item in range(3):
+            hops[0, 3, item].wait_recv()
+            hops[0, 2, item].start()
+            if item == 0:
+                across[0].start()
+        for source in (2, 1):
+            for item in range(3):
+                hops[source, 3, item].wait_recv()
+                if item == 0:
+                    across[source].start()
+
+    pl.when(line == 0)(across_a.wait_send)
+    pl.when(line == 1)(across_a.wait_recv)
+    pl.when(sends_b)(across_b.wait_send)
+    sent = (((0, 1), (0, 3)), ((1, 2),), ((2, 3), (1, 3)), ((0, 2),))
+    for at in range(4):
+
+        @pl.when(column == at)
+        def _():
+            for source, target in sent[at]:
+                for item in range(3):
+                    hops[source, target, item].wait_send()
+            for source in range(at):
+                across[source].wait()
+
+
+def near_peers(seq, chip, core, tp):
+    x, y = chip // 2, chip % 2
+    return [
+        (lax.rem(x + 1, 4) * 4 + y * 2 + core, tp),
+        (lax.rem(x + 3, 4) * 4 + y * 2 + core, tp),
+        (x * 4 + (1 - y) * 2 + core, tp),
+        (x * 4 + y * 2 + 1 - core, tp),
+    ]
+
+
 def tp_peers(seq, tp, order=TP_ORDER):
     return [(seq, lax.rem(tp + hop, TP)) for hop in order]
 
@@ -144,33 +273,37 @@
     kv, query, out_w, kv_all, query_two, w_half, send_sems, recv_sems, sem, kv_bounce, query_bounce, w_bounce
 ):
     seq, chip, core, tp = place()
-    partner = (chip * 2 + 1 - core, tp)
+    peers = near_peers(seq, chip, core, tp)
+    partner = peers[-1]
     half = pl.ds(core * FR, FR)
-    peers = [partner]
-    jobs = []
-    for hop in CHIP_ORDER:
-        there = lax.rem(chip + hop, CHIPS)
-        later = there > chip
-        earlier = lax.rem(chip - hop + CHIPS, CHIPS) < chip
-        for head in (core, 1 - core):
-            other = (there * 2 + head, tp)
-            peers.append(other)
-            jobs.append((kv.at[head], kv_all.at[seq], other, later, earlier))
+    jobs = [(kv.at[1 - core], kv_all.at[chip, core], partner)]
+    jobs.append((query.at[1 - core], query_two.at[core], partner))
     for other in tp_peers(seq, tp):
         peers.append(other)
         jobs.append((out_w.at[other[1], half], w_half.at[tp], other))
-    jobs.append((query.at[1 - core], query_two.at[core], partner))
-    jobs.append((kv.at[1 - core], kv_all.at[seq], partner))
+
+    def relay(base, send_sems, recv_sems):
+        relay_blocks(
+            lambda part: kv_all.at[chip, part],
+            lambda source, part: kv_all.at[source, part],
+            False,
+            base,
+            send_sems,
+            recv_sems,
+        )
+
     run_exchange(
         peers,
         jobs,
         [
-            (kv.at[core], kv_bounce, kv_all.at[seq], sem),
+            (kv.at[core], kv_bounce, kv_all.at[chip, core], sem),
             (query.at[core], query_bounce, query_two.at[core], sem),
             (out_w.at[tp, half], w_bounce, w_half.at[tp], sem),
         ],
         send_sems,
         recv_sems,
+        relay=relay,
+        relay_after=(0,),
     )
 
 
@@ -181,11 +314,11 @@
         1,
         (kv, query, out_w),
         [
-            jax.ShapeDtypeStruct((2 * CHIPS, FR, 2 * HD), BF16),
+            jax.ShapeDtypeStruct((CHIPS, 2, FR, 2 * HD), BF16),
             jax.ShapeDtypeStruct((2, FR, HD), BF16),
             jax.ShapeDtypeStruct((TP, FR, 2 * HD), BF16),
         ],
-        23,
+        9 + RELAY_COPIES,
         [((FR, 2 * HD), BF16), ((FR, HD), BF16), ((FR, 2 * HD), BF16)],
     )
 
@@ -291,10 +424,13 @@
     )
 
 
-def cotangent_kernel(source, side, target, side_x, send_sems, recv_sems, sem, bounce, side_bounce):
+def cotangent_kernel(
+    source, side, grads, target, side_x, grads_z, send_sems, recv_sems, sem, bounce, side_bounce, grads_bounce
+):
     seq, chip, core, tp = place()
     partner_seq = chip * 2 + 1 - core
     at_x, at_y = chip // 2, chip % 2
+    row, depth_at = tp // 4, tp % 4
     peers = [(partner_seq, tp)] + tp_peers(seq, tp) + tp_peers(partner_seq, tp)
     heads = [1 - core] + [core] * (TP - 1) + [1 - core] * (TP - 1)
     jobs = [
@@ -306,36 +442,44 @@
         other = (there * 4 + at_y * 2 + core, tp)
         peers.append(other)
         jobs.append((side.at[there], side_x.at[at_x], other))
+    early = pl.ds(0, Z_EARLY)
+    for hop in (2, 1, 3):
+        there = lax.rem(depth_at + hop, 4)
+        other = (seq, row * 4 + there)
+        jobs.append((grads.at[early, :, there], grads_z.at[depth_at], other))
     run_exchange(
         peers,
         jobs,
         [
             (source.at[tp * 2 + core], bounce, target.at[core, tp], sem),
             (side.at[at_x], side_bounce, side_x.at[at_x], sem),
+            (grads.at[early, :, depth_at], grads_bounce, grads_z.at[depth_at], sem),
         ],
         send_sems,
         recv_sems,
     )
 
 
-def exchange_cotangent(parts, side):
+def exchange_cotangent(parts, side, grads):
+    slab = (Z_EARLY, 2) + grads.shape[3:]
     return exchange(
         cotangent_kernel,
         "exchange_cotangent",
         5,
-        (parts, side),
+        (parts, side, grads),
         [
             jax.ShapeDtypeStruct((2, TP, FR, HD), BF16),
             jax.ShapeDtypeStruct(side.shape, BF16),
-        ],
-        18,
-        [((FR, HD), BF16), (side.shape[1:], BF16)],
-    )
-
-
-def key_grads_kernel(
-    source, grads, side, normed, target, grads_z, side_in, normed_other,
-    send_sems, recv_sems, sem, bounce, grads_bounce,
+            jax.ShapeDtypeStruct((4,) + slab, BF16),
+        ],
+        21,
+        [((FR, HD), BF16), (side.shape[1:], BF16), (slab, BF16)],
+    )
+
+
+def grads_kernel(
+    pair, stats, grads, side, normed, pair_all, stats_all, grads_z, side_in, normed_other,
+    send_sems, recv_sems, sem, bounce, stats_bounce, grads_bounce,
 ):
     seq, chip, core, tp = place()
     row, depth_at = tp // 4, tp % 4
@@ -347,73 +491,101 @@
         here = lax.rem(chip - hop + CHIPS, CHIPS)
         other = (there * 2 + core, tp)
         peers.append(other)
-        jobs.append((source.at[there], target.at[chip], other, there < chip, here > chip))
-    for hop in (1, 3, 2):
+        jobs.append((stats, stats_all.at[chip], other, there < chip, here > chip))
+    for hop in (2, 1, 3):
         there = lax.rem(depth_at + hop, 4)
         other = (seq, row * 4 + there)
         peers.append(other)
-        jobs.append((grads.at[:, :, there], grads_z.at[depth_at], other))
+        jobs.append((grads.at[pl.ds(Z_EARLY, Z_LATE), :, there], grads_z.at[depth_at], other))
     jobs.append((side.at[1 - at_y], side_in, (at_x * 4 + (1 - at_y) * 2 + core, tp)))
     partner = (chip * 2 + 1 - core, tp)
     jobs.append((normed, normed_other, partner))
     peers.append(partner)
+
+    def relay(base, send_sems, recv_sems):
+        relay_blocks(
+            lambda part: pair.at[part],
+            lambda source, part: pair_all.at[source, part],
+            True,
+            base,
+            send_sems,
+            recv_sems,
+        )
+
     run_exchange(
         peers,
         jobs,
         [
-            (source.at[chip], bounce, target.at[chip], sem),
-            (grads.at[:, :, depth_at], grads_bounce, grads_z.at[depth_at], sem),
+            (pair, bounce, pair_all.at[chip], sem),
+            (stats, stats_bounce, stats_all.at[chip], sem),
+            (
+                grads.at[pl.ds(Z_EARLY, Z_LATE), :, depth_at],
+                grads_bounce,
+                grads_z.at[depth_at],
+                sem,
+            ),
         ],
         send_sems,
         recv_sems,
-    )
-
-
-def exchange_key_grads(parts, grads, side, normed):
-    slab = (CHIPS, 2) + grads.shape[3:]
+        relay=relay,
+    )
+
+
+def exchange_grads(pair, stats, grads, side, normed):
+    slab = (Z_LATE, 2) + grads.shape[3:]
     return exchange(
-        key_grads_kernel,
-        "exchange_key_grads",
+        grads_kernel,
+        "exchange_grads",
         6,
-        (parts, grads, side, normed),
-        [
-            jax.ShapeDtypeStruct(parts.shape, parts.dtype),
+        (pair, stats, grads, side, normed),
+        [
+            jax.ShapeDtypeStruct((CHIPS,) + pair.shape, BF16),
+            jax.ShapeDtypeStruct((CHIPS,) + stats.shape, F32),
             jax.ShapeDtypeStruct((4,) + slab, BF16),
             jax.ShapeDtypeStruct(side.shape[1:], BF16),
             jax.ShapeDtypeStruct(normed.shape, BF16),
         ],
-        12,
-        [(parts.shape[1:], parts.dtype), (slab, BF16)],
-    )
-
-
-def weights_kernel(
-    source, grads, out, target, grads_all, out_all, send_sems, recv_sems, sem, bounce, grads_bounce, out_bounce
+        12 + RELAY_COPIES,
+        [(pair.shape, BF16), (stats.shape, F32), (slab, BF16)],
+    )
+
+
+def first_kernel(
+    x_first, y_first, grads, out, x_in, y_in, grads_x, out_all,
+    send_sems, recv_sems, sem, x_bounce, y_bounce, grads_bounce, out_bounce,
 ):
     seq, chip, core, tp = place()
-    row, depth_at = tp // 4, tp % 4
-    partner = (chip * 2 + 1 - core, tp)
-    peers = [partner] + chip_peers(chip, core, tp) + chip_peers(chip, 1 - core, tp)
-    jobs = [(source.at[peer[0]], target.at[core, chip], peer) for peer in peers]
-    for hop in CHIP_ORDER:
-        there = lax.rem(chip + hop, CHIPS)
-        jobs.append((grads.at[there, row], grads_all.at[chip, row], (there * 2 + core, tp)))
-    across = (1 - row) * 4 + depth_at
-    for hop in (0,) + CHIP_ORDER:
-        there = lax.rem(chip + hop, CHIPS)
-        other = (there * 2 + core, across)
-        if hop:
-            peers.append(other)
-        jobs.append((grads.at[there, 1 - row], grads_all.at[chip, row], other))
+    at_x, at_y = chip // 2, chip % 2
+
+    def device(x, y, c):
+        return x * 4 + y * 2 + c, tp
+
+    peers = []
+    jobs = []
+    for hop in (2, 1, 3):
+        x = lax.rem(at_x + hop, 4)
+        for c in (core, 1 - core):
+            peers.append(device(x, at_y, c))
+            jobs.append((x_first.at[x, c], x_in.at[at_x, core], peers[-1]))
+    for c in (core, 1 - core):
+        peers.append(device(at_x, 1 - at_y, c))
+        jobs.append((y_first.at[1 - at_y, c], y_in.at[at_y, core], peers[-1]))
+    for hop in (2, 1, 3):
+        x = lax.rem(at_x + hop, 4)
+        jobs.append((grads.at[x], grads_x.at[at_x], device(x, at_y, core)))
     for other in tp_peers(seq, tp):
         peers.append(other)
         jobs.append((out.at[other[1]], out_all.at[tp], other))
+    peers.append(device(at_x, at_y, 1 - core))
+    jobs.append((x_first.at[at_x, 1 - core], x_in.at[at_x, core], peers[-1]))
+    jobs.append((y_first.at[at_y, 1 - core], y_in.at[at_y, core], peers[-1]))
     run_exchange(
         peers,
         jobs,
         [
-            (source.at[seq], bounce, target.at[core, chip], sem),
-            (grads.at[chip, row], grads_bounce, grads_all.at[chip, row], sem),
+            (x_first.at[at_x, core], x_bounce, x_in.at[at_x, core], sem),
+            (y_first.at[at_y, core], y_bounce, y_in.at[at_y, core], sem),
+            (grads.at[at_x], grads_bounce, grads_x.at[at_x], sem),
             (out.at[tp], out_bounce, out_all.at[tp], sem),
         ],
         send_sems,
@@ -421,19 +593,63 @@
     )
 
 
-def exchange_weights(parts, grads, out):
+def exchange_first(x_first, y_first, grads, out):
+    arrays = (x_first, y_first, grads, out)
+    tails = (x_first.shape[2:], y_first.shape[2:], grads.shape[1:], out.shape[1:])
     return exchange(
-        weights_kernel,
-        "exchange_weights",
+        first_kernel,
+        "exchange_first",
         7,
-        (parts, grads, out),
-        [
-            jax.ShapeDtypeStruct((2, CHIPS) + parts.shape[1:], parts.dtype),
+        arrays,
+        [jax.ShapeDtypeStruct(array.shape, BF16) for array in arrays],
+        20,
+        [(tail, BF16) for tail in tails],
+    )
+
+
+def second_kernel(
+    x_sum, y_sum, grads, x_in, y_in, grads_in, send_sems, recv_sems, sem, y_bounce, grads_bounce
+):
+    seq, chip, core, tp = place()
+    at_x, at_y = chip // 2, chip % 2
+    row, depth_at = tp // 4, tp % 4
+    peers = []
+    jobs = []
+    for hop in (2, 1, 3):
+        x = lax.rem(at_x + hop, 4)
+        peers.append((x * 4 + at_y * 2 + core, tp))
+        jobs.append((y_sum.at[x], y_in.at[at_x], peers[-1]))
+    peers.append((at_x * 4 + (1 - at_y) * 2 + core, tp))
+    jobs.append((x_sum.at[1 - at_y], x_in, peers[-1]))
+    jobs.append((grads.at[1 - at_y, row], grads_in.at[at_y, row], peers[-1]))
+    for y in (at_y, 1 - at_y):
+        peers.append((at_x * 4 + y * 2 + core, (1 - row) * 4 + depth_at))
+        jobs.append((grads.at[y, 1 - row], grads_in.at[at_y, row], peers[-1]))
+    run_exchange(
+        peers,
+        jobs,
+        [
+            (y_sum.at[at_x], y_bounce, y_in.at[at_x], sem),
+            (grads.at[at_y, row], grads_bounce, grads_in.at[at_y, row], sem),
+        ],
+        send_sems,
+        recv_sems,
+    )
+
+
+def exchange_second(x_sum, y_sum, grads):
+    return exchange(
+        second_kernel,
+        "exchange_second",
+        8,
+        (x_sum, y_sum, grads),
+        [
+            jax.ShapeDtypeStruct(x_sum.shape[1:], BF16),
+            jax.ShapeDtypeStruct(y_sum.shape, BF16),
             jax.ShapeDtypeStruct(grads.shape, BF16),
-            jax.ShapeDtypeStruct(out.shape, BF16),
-        ],
-        37,
-        [(parts.shape[1:], BF16), (grads.shape[2:], BF16), (out.shape[1:], BF16)],
+        ],
+        7,
+        [(y_sum.shape[1:], BF16), (grads.shape[2:], BF16)],
     )
 
 
@@ -442,7 +658,7 @@
         kernel,
         name=name,
         out_shape=outs,
-        in_specs=[VMEM] * (len(ins) - hbm) + [ANY] * hbm,
+        in_specs=[VMEM] * (len(ins) - hbm) + [HBM] * hbm,
         out_specs=[VMEM] * len(outs),
         scratch_shapes=list(scratch),
         compiler_params=pltpu.CompilerParams(vmem_limit_bytes=limit * MIB),
@@ -453,6 +669,7 @@
     hidden_ref, w_ref, cos_ref, sin_ref, normed_ref, kv_ref, query_ref, out_w_ref, total_ref
 ):
     step = pl.program_id(0)
+    own = pl.ds(pl.multiple_of(lax.axis_index("seq") % 2 * FR, FR), FR)
     depth_rows = w_ref.shape[0]
 
     @pl.when(step == 0)
@@ -471,7 +688,7 @@
 
     @pl.when(step == pl.num_programs(0) - 1)
     def _():
-        cosine, sine = cos_ref[...], sin_ref[...]
+        cosine, sine = cos_ref[own], sin_ref[own]
 
         def turned(at):
             lower = total_ref[:, at : at + HD // 2]
@@ -521,19 +738,18 @@
     )(hidden, weights, cosine, sine)
 
 
-def attend_kernel(kv_ref, query_ref, out_ref, prob_ref, out_t_ref, inverse_ref, score_ref):
+def attend_kernel(kv_ref, query_ref, out_ref, out_t_ref, level_ref, score_ref):
     chip = lax.axis_index("seq") // 2
-    query = query_ref[...].reshape(FR2, HD)
-    scale = math.log2(math.e) / math.sqrt(HD)
+    query = query_ref[...]
     key_at = lax.broadcasted_iota(jnp.int32, (FR2, FR2), 0)
     query_at = lax.broadcasted_iota(jnp.int32, (FR2, FR2), 1)
 
     def scores(block, top):
-        score = dot_nt(kv_ref[block, :, :HD], query) * scale
+        score = dot_nt(kv_ref[block, :, :HD], query) * LOG_SCALE
         score_ref[block] = score
         return jnp.maximum(top, jnp.max(score, axis=0, keepdims=True))
 
-    score = dot_nt(kv_ref[chip, :, :HD], query) * scale
+    score = dot_nt(kv_ref[chip, :, :HD], query) * LOG_SCALE
     score = jnp.where(key_at <= query_at, score, MASKED)
     score_ref[chip] = score
     top = lax.fori_loop(0, chip, scores, jnp.max(score, axis=0, keepdims=True))
@@ -542,33 +758,29 @@
         total, mixed = carry
         prob = jnp.exp2(score_ref[block] - top)
         total = total + jnp.sum(prob, axis=0, keepdims=True)
-        prob = prob.astype(BF16)
-        prob_ref[block] = prob
-        return total, mixed + dot_tn(kv_ref[block, :, HD:], prob)
+        return total, mixed + dot_tn(kv_ref[block, :, HD:], prob.astype(BF16))
 
     total, mixed = lax.fori_loop(
         0, chip + 1, weigh, (jnp.zeros((1, FR2), F32), jnp.zeros((HD, FR2), F32))
     )
-    inverse = 1.0 / total
-    mixed = mixed * inverse
+    mixed = mixed * (1.0 / total)
     out_t_ref[...] = mixed
-    inverse_ref[...] = inverse
+    level_ref[...] = top + jnp.log2(total)
     out_ref[...] = mixed.T.astype(BF16)
 
 
-def attend(kv_all, query_two):
+def attend(kv_all, query):
     return compute(
         attend_kernel,
         "attend",
-        (kv_all, query_two),
+        (kv_all, query),
         [
             jax.ShapeDtypeStruct((FR2, HD), BF16),
-            jax.ShapeDtypeStruct((CHIPS, FR2, FR2), BF16),
             jax.ShapeDtypeStruct((HD, FR2), F32),
             jax.ShapeDtypeStruct((1, FR2), F32),
         ],
         [pltpu.VMEM((CHIPS, FR2, FR2), F32)],
-        limit=24,
+        limit=20,
     )
 
 
@@ -632,25 +844,42 @@
     )
 
 
-def depth_kernel(width, loss_scale, part_ref, stack_ref, before_ref, code_ref, message_ref, grad_ref, prob_ref):
-    frames = part_ref.shape[1]
-    books = before_ref.shape[0] // frames
+def depth_kernel(
+    width, loss_scale, part_ref, code_ref, stack_hbm, message_ref, grad_ref, prob_ref, stack_ref, sems
+):
+    frames, books = code_ref.shape
+    pieces = ((3072, 1024), (0, 1536), (1536, 512), (2048, 1024))
+    copies = [
+        fetch(stack_hbm.at[pl.ds(low, rows)], stack_ref.at[pl.ds(low, rows)], sems.at[at])
+        for at, (low, rows) in enumerate(pieces)
+    ]
+    grid = (frames, books, books)
+    row_at = lax.broadcasted_iota(jnp.int32, grid, 1)
+    col_at = lax.broadcasted_iota(jnp.int32, grid, 2)
+    spread = jnp.broadcast_to(code_ref[...][:, None, :], grid)
+
+    def column(wanted):
+        picked = jnp.where(wanted, spread + 1, 0).astype(F32)
+        picked = jnp.sum(picked, axis=-1, keepdims=True).reshape(frames * books, 1)
+        return picked - 1.0
+
+    codes = column(col_at == row_at)
+    before = column(col_at == row_at - 1)
     tokens = frames * books
-    qkv_rows = stack_ref[: 3 * DD]
-    out_rows = stack_ref[3 * DD : 4 * DD]
-    head_rows = stack_ref[4 * DD : 4 * DD + VOCAB]
-    embed_rows = stack_ref[4 * DD + VOCAB :]
     total = jnp.sum(part_ref[...].astype(F32), axis=0)
     raw = total[:, :DD]
     squares = total[:, DD : DD + 1] + total[:, DD + HD : DD + HD + 1]
     scale_in = lax.rsqrt(squares * (1.0 / width) + EPSILON)
     latent = raw * scale_in
     latent = jnp.broadcast_to(latent[:, None, :], (frames, books, DD)).reshape(tokens, DD)
-    vocab_at = lax.broadcasted_iota(jnp.int32, (tokens, VOCAB), 1)
-    hot = jnp.where(before_ref[...] == vocab_at, 1.0, 0.0).astype(BF16)
-    stream = latent + dot_nn(hot, embed_rows)
+    vocab_at = lax.broadcasted_iota(jnp.int32, (tokens, VOCAB), 1).astype(F32)
+    hot = jnp.where(before == vocab_at, 1.0, 0.0).astype(BF16)
+    copies[0].wait()
+    stream = latent + dot_nn(hot, stack_ref[4 * DD + VOCAB :])
     stream_scale = rms_scale(stream)
     stream_norm = (stream * stream_scale).astype(BF16)
+    copies[1].wait()
+    qkv_rows = stack_ref[: 3 * DD]
     proj = dot_nt(stream_norm, qkv_rows).astype(BF16)
     row_at = lax.broadcasted_iota(jnp.int32, (tokens, tokens), 0)
     col_at = lax.broadcasted_iota(jnp.int32, (tokens, tokens), 1)
@@ -668,13 +897,17 @@
         prob_ref[head] = probs
         mixed.append(dot_nn(probs.astype(BF16), values))
     mixed = jnp.concatenate(mixed, axis=1).astype(BF16)
+    copies[2].wait()
+    out_rows = stack_ref[3 * DD : 4 * DD]
     resid = stream + dot_nt(mixed, out_rows)
     resid_scale = rms_scale(resid)
     resid_norm = (resid * resid_scale).astype(BF16)
+    copies[3].wait()
+    head_rows = stack_ref[4 * DD : 4 * DD + VOCAB]
     logits = dot_nt(resid_norm, head_rows)
     weights = jnp.exp(logits - jnp.max(logits, axis=-1, keepdims=True))
     logit_probs = weights / jnp.sum(weights, axis=-1, keepdims=True)
-    target = jnp.where(code_ref[...] == vocab_at, 1.0, 0.0)
+    target = jnp.where(codes == vocab_at, 1.0, 0.0)
     logit_grad = ((logit_probs - target) * loss_scale).astype(BF16)
     grad_ref[4 * DD : 4 * DD + VOCAB] = dot_tn(logit_grad, resid_norm).astype(BF16)
     resid_grad = norm_back(resid, resid_scale, dot_nn(logit_grad, head_rows))
@@ -710,17 +943,22 @@
     message_ref[:, DD + HD :] = jnp.broadcast_to(fine, (frames, HD))
 
 
-def depth(parts, stack, before, codes, width, loss_scale):
-    tokens = before.shape[0]
+def depth(parts, codes, stack, width, loss_scale):
+    tokens = codes.shape[0] * codes.shape[1]
     return compute(
         functools.partial(depth_kernel, width, loss_scale),
         "depth",
-        (parts, stack, before, codes),
+        (parts, codes, stack),
         [
             jax.ShapeDtypeStruct((parts.shape[1], DD + 2 * HD), BF16),
             jax.ShapeDtypeStruct(stack.shape, BF16),
         ],
-        [pltpu.VMEM((DD // DHD, tokens, tokens), F32)],
+        [
+            pltpu.VMEM((DD // DHD, tokens, tokens), F32),
+            pltpu.VMEM(stack.shape, BF16),
+            pltpu.SemaphoreType.DMA((4,)),
+        ],
+        hbm=1,
         limit=32,
     )
 
@@ -823,123 +1061,180 @@
     )
 
 
+def prepare_kernel(
+    part_ref, query_ref, out_t_ref, level_ref, side_x_ref, pair_ref, stats_ref, side_ref
+):
+    gradient = jnp.sum(part_ref[...].astype(F32), axis=1).reshape(FR2, HD).astype(BF16)
+    pair_ref[:, :, :HD] = query_ref[...].reshape(2, FR, HD)
+    pair_ref[:, :, HD:] = gradient.reshape(2, FR, HD)
+    inner = jnp.sum(gradient.astype(F32).T * out_t_ref[...], axis=0, keepdims=True)
+    stats_ref[...] = jnp.concatenate(
+        [level_ref[...], inner, jnp.zeros((6, FR2), F32)], axis=0
+    )
+    side_ref[...] = jnp.sum(side_x_ref[...].astype(F32), axis=0).astype(BF16)
+
+
+def prepare(parts, query, out_t, level, side_x):
+    return compute(
+        prepare_kernel,
+        "prepare",
+        (parts, query, out_t, level, side_x),
+        [
+            jax.ShapeDtypeStruct((2, FR, 2 * HD), BF16),
+            jax.ShapeDtypeStruct((8, FR2), F32),
+            jax.ShapeDtypeStruct(side_x.shape[1:], BF16),
+        ],
+        limit=16,
+    )
+
+
 def attend_back_kernel(
-    prob_ref, kv_ref, query_ref, part_ref, out_t_ref, inverse_ref, cos_ref, sin_ref, side_x_ref,
-    grad_ref, query_grad_ref, side_ref,
-):
-    chip = lax.axis_index("seq") // 2
-    query = query_ref[...].reshape(FR2, HD)
-    gradient = jnp.sum(part_ref[...].astype(F32), axis=1).reshape(FR2, HD)
-    gradient = gradient.astype(BF16).astype(F32)
-    gradient_t = (gradient.T * inverse_ref[...]).astype(BF16)
-    wide_t = gradient_t.astype(F32)
-    inner = jnp.sum(wide_t * out_t_ref[...], axis=0, keepdims=True)
-    gradient = wide_t.T.astype(BF16)
-    scale = 1.0 / math.sqrt(HD)
-
-    def step(block, query_grad):
-        prob = prob_ref[block]
-        score_grad = prob.astype(F32) * (dot_nn(kv_ref[block, :, HD:], gradient_t) - inner)
-        score_grad = score_grad.astype(BF16)
-        grad_ref[block, :, :HD] = (dot_nn(score_grad, query) * scale).astype(BF16)
-        grad_ref[block, :, HD:] = dot_nn(prob, gradient).astype(BF16)
-        return query_grad + dot_tn(kv_ref[block, :, :HD], score_grad)
-
-    query_grad = lax.fori_loop(0, chip + 1, step, jnp.zeros((HD, FR2), F32)) * scale
-    query_grad = query_grad.T
-    lower, upper = query_grad[:, : HD // 2], query_grad[:, HD // 2 :]
-    cosine, sine = cos_ref[...], sin_ref[...]
-    query_grad_ref[...] = jnp.concatenate(
-        [lower * cosine + upper * sine, upper * cosine - lower * sine], axis=1
-    ).astype(BF16)
-    side_ref[...] = jnp.sum(side_x_ref[...].astype(F32), axis=0).astype(BF16)
-
-
-def attend_back(probs, kv_all, query_two, parts, out_t, inverse, cosine, sine, side_x):
-    return compute(
-        attend_back_kernel,
-        "attend_back",
-        (probs, kv_all, query_two, parts, out_t, inverse, cosine, sine, side_x),
-        [
-            jax.ShapeDtypeStruct((CHIPS, FR2, 2 * HD), BF16),
-            jax.ShapeDtypeStruct((FR2, HD), BF16),
-            jax.ShapeDtypeStruct(side_x.shape[1:], BF16),
-        ],
-        limit=28,
-    )
-
-
-def weight_kernel(
-    part_ref, query_grad_ref, cos_ref, sin_ref, normed_ref, other_ref, grads_z_ref, side_ref,
-    side_in_ref, out_ref, grads_ref, win_ref, out_w_ref,
+    stats_ref, cos_ref, sin_ref, side_ref, side_in_ref, kv_hbm, pair_hbm, early_hbm, late_hbm,
+    normed_hbm, other_hbm, x_ref, y_ref, grads_ref, win_ref, out_w_ref,
+    kv_ref, pair_ref, early_ref, late_ref, normed_ref, other_ref, sems,
 ):
     chip = lax.axis_index("seq") // 2
     core = lax.axis_index("seq") % 2
-    total = lax.fori_loop(
-        chip,
-        CHIPS,
-        lambda at, carry: carry + part_ref[at].astype(F32),
-        jnp.zeros((FR2, 2 * HD), F32),
-    )
-    lower, upper = total[:, : HD // 2], total[:, HD // 2 : HD]
-    cosine, sine = cos_ref[...], sin_ref[...]
-    proj = jnp.concatenate(
-        [
-            query_grad_ref[...].astype(F32),
-            lower * cosine + upper * sine,
-            upper * cosine - lower * sine,
-            total[:, HD:],
-        ],
-        axis=1,
-    )
+    places = (
+        (kv_hbm, kv_ref),
+        (pair_hbm, pair_ref),
+        (normed_hbm, normed_ref),
+        (other_hbm, other_ref),
+        (early_hbm, early_ref),
+        (late_hbm, late_ref),
+    )
+    copies = [fetch(source, target, sems.at[at]) for at, (source, target) in enumerate(places)]
+    copies[0].wait()
+    copies[1].wait()
+    scale = 1.0 / math.sqrt(HD)
+
+    def pair(queries, keys, diagonal):
+        query = pair_ref[queries, :, :HD]
+        gradient = pair_ref[queries, :, HD:]
+        score = dot_nt(kv_ref[keys, :, :HD], query) * LOG_SCALE
+        if diagonal:
+            key_at = lax.broadcasted_iota(jnp.int32, (FR2, FR2), 0)
+            query_at = lax.broadcasted_iota(jnp.int32, (FR2, FR2), 1)
+            score = jnp.where(key_at <= query_at, score, MASKED)
+        prob = jnp.exp2(score - stats_ref[queries, 0:1])
+        prob_grad = dot_nt(kv_ref[keys, :, HD:], gradient)
+        score_grad = (prob * (prob_grad - stats_ref[queries, 1:2])).astype(BF16)
+        return query, gradient, prob.astype(BF16), score_grad
+
+    def own_queries(block, total):
+        score_grad = pair(chip, block, False)[3]
+        return total + dot_tn(kv_ref[block, :, :HD], score_grad)
+
+    def own_keys(block, totals):
+        query, gradient, prob, score_grad = pair(block, chip, False)
+        return totals[0] + dot_nn(score_grad, query), totals[1] + dot_nn(prob, gradient)
+
+    query, gradient, prob, score_grad = pair(chip, chip, True)
+    query_grad = dot_tn(kv_ref[chip, :, :HD], score_grad)
+    key_grad = dot_nn(score_grad, query)
+    value_grad = dot_nn(prob, gradient)
+    query_grad = lax.fori_loop(0, chip, own_queries, query_grad)
+    key_grad, value_grad = lax.fori_loop(chip + 1, CHIPS, own_keys, (key_grad, value_grad))
+    query_grad = query_grad.T
+    cosine, sine = cos_ref[...] * scale, sin_ref[...] * scale
+
+    def turned(total):
+        lower, upper = total[:, : HD // 2], total[:, HD // 2 :]
+        return [lower * cosine + upper * sine, upper * cosine - lower * sine]
+
+    proj = jnp.concatenate(turned(query_grad) + turned(key_grad) + [value_grad], axis=1)
     proj_t = proj.T
     own, other = order_halves(core, proj_t[:, :FR], proj_t[:, FR:])
     own, other = own.astype(BF16), other.astype(BF16)
+    copies[2].wait()
+    copies[3].wait()
     for piece in range(2 * CHIPS):
         low = piece * FR
         term = dot_nn(own, normed_ref[:, low : low + FR])
-        term = term + dot_nn(other, other_ref[:, low : low + FR])
-        out_ref[piece] = term.astype(BF16)
+        term = (term + dot_nn(other, other_ref[:, low : low + FR])).astype(BF16)
+        x, y, c = piece // 4, piece // 2 % 2, piece % 2
+        x_ref[x, c, y] = term[:X_ROWS]
+        y_ref[y, c, x] = term[X_ROWS:]
+    copies[4].wait()
+    copies[5].wait()
     for at in range(CHIPS):
-        grads_ref[at] = jnp.sum(grads_z_ref[:, at].astype(F32), axis=0).astype(BF16)
+        term = early_ref[:, at] if at < Z_EARLY else late_ref[:, at - Z_EARLY]
+        grads_ref[at] = jnp.sum(term.astype(F32), axis=0).astype(BF16)
     side = side_ref[chip % 2].astype(F32) + side_in_ref[...].astype(F32)
     win_ref[...] = side[:, TP * FR :]
     for at in range(TP):
         out_w_ref[at] = side[:, at * FR : (at + 1) * FR].astype(BF16)
 
 
-def weight_terms(parts, query_grad, cosine, sine, normed, normed_other, grads_z, side, side_in):
+def attend_back(
+    stats_all, cosine, sine, side, side_in, kv_all, pair_all, early, late, normed, normed_other
+):
+    streamed = (kv_all, pair_all, early, late, normed, normed_other)
     return compute(
-        weight_kernel,
-        "weight_terms",
-        (parts, query_grad, cosine, sine, normed, normed_other, grads_z, side, side_in),
-        [
-            jax.ShapeDtypeStruct((2 * CHIPS, 3 * HD, FR), BF16),
-            jax.ShapeDtypeStruct(grads_z.shape[1:], BF16),
+        attend_back_kernel,
+        "attend_back",
+        (stats_all, cosine, sine, side, side_in) + streamed,
+        [
+            jax.ShapeDtypeStruct((4, 2, 2, X_ROWS, FR), BF16),
+            jax.ShapeDtypeStruct((2, 2, 4, Y_ROWS, FR), BF16),
+            jax.ShapeDtypeStruct((CHIPS,) + late.shape[2:], BF16),
             jax.ShapeDtypeStruct((32, DD), F32),
             jax.ShapeDtypeStruct((TP, 32, FR), BF16),
         ],
-        limit=28,
-    )
-
-
-def weight_sum_kernel(part_ref, grads_ref, out_w_ref, out_ref, depth_ref):
+        [pltpu.VMEM(array.shape, BF16) for array in streamed] + [pltpu.SemaphoreType.DMA((6,))],
+        hbm=6,
+        limit=36,
+    )
+
+
+def middle_kernel(x_ref, y_ref, grads_x_ref, x_sum_ref, y_sum_ref, grads_ref):
+    for y in range(2):
+        for c in range(2):
+            terms = [x_ref[x, c, y].astype(F32) for x in range(4)]
+            x_sum_ref[y, c] = (terms[0] + terms[1] + terms[2] + terms[3]).astype(BF16)
+    for x in range(4):
+        for c in range(2):
+            term = y_ref[0, c, x].astype(F32) + y_ref[1, c, x].astype(F32)
+            y_sum_ref[x, c] = term.astype(BF16)
+    grads_ref[...] = jnp.sum(grads_x_ref[...].astype(F32), axis=0).astype(BF16)
+
+
+def middle_sum(x_in, y_in, grads_x):
+    return compute(
+        middle_kernel,
+        "middle_sum",
+        (x_in, y_in, grads_x),
+        [
+            jax.ShapeDtypeStruct((2, 2, X_ROWS, FR), BF16),
+            jax.ShapeDtypeStruct((4, 2, Y_ROWS, FR), BF16),
+            jax.ShapeDtypeStruct(grads_x.shape[1:], BF16),
+        ],
+        limit=16,
+    )
+
+
+def last_kernel(x_own_ref, x_in_ref, y_in_ref, grads_ref, out_w_ref, out_ref, depth_ref):
+    at_y = lax.axis_index("seq") // 2 % 2
+    totals = []
     for head in range(2):
-        total = jnp.sum(part_ref[head].astype(F32), axis=0).T
-        for kind in range(3):
-            out_ref[kind, :, head * HD : (head + 1) * HD] = total[:, kind * HD : (kind + 1) * HD]
-    out_ref[3] = out_w_ref[...].astype(F32).reshape(FR, 2 * HD)
+        x_part = x_own_ref[at_y, head].astype(F32) + x_in_ref[head].astype(F32)
+        terms = [y_in_ref[x, head].astype(F32) for x in range(4)]
+        y_part = terms[0] + terms[1] + terms[2] + terms[3]
+        totals.append(jnp.concatenate([x_part, y_part], axis=0).T)
+    pieces = [totals[head][:, kind * HD : (kind + 1) * HD] for kind in range(3) for head in range(2)]
+    pieces.append(out_w_ref[...].astype(F32).reshape(FR, 2 * HD))
+    out_ref[...] = jnp.concatenate(pieces, axis=1).reshape(FR, 4, 2 * HD)
     depth_ref[...] = jnp.sum(jnp.sum(grads_ref[...].astype(F32), axis=0), axis=0)
 
 
-def weight_sum(parts, grads_all, out_all):
+def last_sum(x_own, x_in, y_in, grads, out_all):
     return compute(
-        weight_sum_kernel,
-        "weight_sum",
-        (parts, grads_all, out_all),
-        [
-            jax.ShapeDtypeStruct((4, FR, 2 * HD), F32),
-            jax.ShapeDtypeStruct(grads_all.shape[2:], F32),
+        last_kernel,
+        "last_sum",
+        (x_own, x_in, y_in, grads, out_all),
+        [
+            jax.ShapeDtypeStruct((FR, 4, 2 * HD), F32),
+            jax.ShapeDtypeStruct(grads.shape[2:], F32),
         ],
         limit=16,
     )
@@ -955,22 +1250,18 @@
     total_frames = FR * seq_count
     loss_scale = 1.0 / math.sqrt(total_frames * book_count)
 
-    cosine, sine = angle_tables(seq_index * FR, FR)
+    cosine, sine = angle_tables(chip * FR2, FR2)
     normed, kv, query, out_w = start(hidden_in, temporal_weight_stack, cosine, sine)
-    kv_all, query_two, w_half = exchange_keys(kv, query, out_w)
+    kv_all, query, w_half = exchange_keys(kv, query, out_w)
     kv_all = kv_all.reshape(CHIPS, FR2, 2 * HD)
+    query = query.reshape(FR2, HD)
 
     depth_in = depth_in.reshape(seq_count, TP, -1, DD)
-    attended, probs, out_t, inverse = attend(kv_all, query_two)
+    attended, out_t, level = attend(kv_all, query)
     att_all, w_other = exchange_attended(attended, w_half)
     merged, rounded, latent_parts = merge(att_all, w_half, w_other, hidden_in, depth_in)
     latent_parts, att_other, rounded_other = exchange_latent(latent_parts, att_all, rounded)
-    before = jnp.concatenate(
-        [jnp.full((depth_frames, 1), -1, jnp.int32), audio_codes[:, :-1]], axis=1
-    ).reshape(-1, 1)
-    message, grads = depth(
-        latent_parts, depth_stack, before, audio_codes.reshape(-1, 1), width, loss_scale
-    )
+    message, grads = depth(latent_parts, audio_codes, depth_stack, width, loss_scale)
     grads = grads.reshape(CHIPS, 2, TP, -1, DD)
     messages, grads_other = exchange_message(message, grads)
     cotangent_parts, side, grads = unmerge(
@@ -986,20 +1277,34 @@
         grads,
         depth_in,
     )
-    cotangent_parts, side = exchange_cotangent(cotangent_parts, side.reshape(4, 2, 32, -1))
-
-    cosine, sine = angle_tables(chip * FR2, FR2)
-    key_parts, query_grad, side = attend_back(
-        probs, kv_all, query_two, cotangent_parts, out_t, inverse, cosine, sine, side
-    )
-    key_parts, grads_z, side_in, normed_other = exchange_key_grads(
-        key_parts, grads.reshape(CHIPS, 2, 4, -1, DD), side, normed
-    )
-    parts, grads, grad_win, out_parts = weight_terms(
-        key_parts, query_grad, cosine, sine, normed, normed_other, grads_z, side, side_in
-    )
-    grad_temporal, grad_depth = weight_sum(*exchange_weights(parts, grads, out_parts))
-    return grad_temporal.transpose(1, 0, 2), grad_win, grad_depth
+    grads = grads.reshape(CHIPS, 2, 4, -1, DD)
+    cotangent_parts, side, early = exchange_cotangent(
+        cotangent_parts, side.reshape(4, 2, 32, -1), grads
+    )
+    pair, stats, side = prepare(cotangent_parts, query, out_t, level, side)
+    pair_all, stats_all, late, side_in, normed_other = exchange_grads(
+        pair, stats, grads, side, normed
+    )
+    x_first, y_first, grads, grad_win, out_parts = attend_back(
+        stats_all,
+        cosine,
+        sine,
+        side,
+        side_in,
+        kv_all,
+        pair_all.reshape(CHIPS, FR2, 2 * HD),
+        early,
+        late,
+        normed,
+        normed_other,
+    )
+    x_in, y_in, grads, out_all = exchange_first(
+        x_first, y_first, grads.reshape(4, 2, 2, -1, DD), out_parts
+    )
+    x_own, y_sum, grads = middle_sum(x_in, y_in, grads)
+    x_in, y_in, grads = exchange_second(x_own, y_sum, grads)
+    grad_temporal, grad_depth = last_sum(x_own, x_in, y_in, grads, out_all)
+    return grad_temporal, grad_win, grad_depth
 
 
 def solution(mesh):

time: 246 us -> 219 us (0.89)
  local copies, waits for them, and re-layouts: 25.8 us -> 5.74 us
  Pallas kernels: 216 us -> 211 us
    unnamed x63 -> x9, local copies, waits for them, and re-layouts: 22.9 us -> 5.74 us
    pallas_call x7 -> x8, Pallas kernels: 188 us -> 176 us  [exchange(): pl.pallas_call(kernel, name=name, out_shape=outs, in_specs=[ANY] * len(in...]
    pallas_call x7 -> x8, Pallas kernels: 22.3 us -> 28.7 us  [compute(): pl.pallas_call(kernel, name=name, out_shape=outs, in_specs=[VMEM] * (len(...]
where the time goes in v5:
time: 219 us
  Pallas kernels  211 us (96%)
  local copies, waits for them, and re-layouts  5.74 us (3%)
    pallas_call x8, Pallas kernels, exchange(): pl.pallas_call(kernel, name=name, out_shape=outs, in_specs=[ANY] * len(in...  176 us
    pallas_call x8, Pallas kernels, compute(): pl.pallas_call(kernel, name=name, out_shape=outs, in_specs=[VMEM] * (len(...  28.7 us
    pallas_call x1, Pallas kernels, start(): pl.pallas_call(start_kernel, name='start', grid=(steps,), out_shape=[jax....  6.13 us
    unnamed x9, local copies, waits for them, and re-layouts  5.74 us

profile of v5, /device:TPU:1, one launch (start us, length us, event | category | flops | bytes accessed | tf_op | source)
XLA Modules:
  0.0 218.6 jit_solution(7031003652801718567)
XLA Ops:
  0.7 0.8 copy.8.code_ref
  1.4 1.0 multiply_sine_fusion
  2.4 0.0 copy-start.1
  2.4 3.4 %copy-done.1 = bf16[4096,4,256]{2,1,0:T(4,128)(2,1)S(1)} copy-done((bf16[4096,4,256]{2,1,0:T(4,128)(2,1)S(1)}, bf16[4096,4,256]{2,1,0:T(4,128)(2,1)}, u32[]{:S(2)}) %copy-start.1) | copy-done | bytes 8388632
  5.8 0.0 copy-start.2
  5.8 1.6 copy-done.2
  7.4 6.1 %start.1 = (bf16[256,4096]{1,0:T(8,128)(2,1)S(1)}, bf16[2,256,256]{2,1,0:T(8,128)(2,1)S(1)}, bf16[2,256,128]{2,1,0:T(8,128)(2,1)S(1)}, bf16[8,512,256]{2,1,0:T(8,128)(2,1)S(1)}) custom-call(bf16[256,4096]{1,0:T(8,128)(2,1)S(1)} %copy-done.2, bf16[4096,4,256]{2,1,0:T(4,128)(2,1)S(1)} %copy-done.1, f32[512,64]{1,0:T(8,128)S(1)} %get-tuple-element.110.cos_ref, ...), custom_call_target="tpu_custom_call" | custom-call | tf_op jit(solution)/shard_map/start/pallas_call | solution.py:714
  13.5 0.0 copy-start
  13.5 25.0 %exchange_keys.1 = (bf16[8,2,256,256]{3,2,1,0:T(8,128)(2,1)S(1)}, bf16[2,256,128]{2,1,0:T(8,128)(2,1)S(1)}, bf16[8,256,256]{2,1,0:T(8,128)(2,1)S(1)}) custom-call(bf16[2,256,256]{2,1,0:T(8,128)(2,1)S(1)} %get-tuple-element.56.kv, bf16[2,256,128]{2,1,0:T(8,128)(2,1)S(1)} %get-tuple-element.57.query, bf16[8,512,256]{2,1,0:T(8,128)(2,1)S(1)} %get-tuple-element.58.out_w), custom_call_target="tpu_custom_call" | custom-call | tf_op jit(solution)/shard_map/exchange_keys/pallas_call | solution.py:130
  38.6 1.0 attend.1
  39.5 18.6 %exchange_attended.1 = (bf16[16,256,128]{2,1,0:T(8,128)(2,1)S(1)}, bf16[8,256,256]{2,1,0:T(8,128)(2,1)S(1)}) custom-call(bf16[512,128]{1,0:T(8,128)(2,1)S(1)} %get-tuple-element.61.source, bf16[8,256,256]{2,1,0:T(8,128)(2,1)S(1)} %get-tuple-element.62.w_half.half_ref), custom_call_target="tpu_custom_call" | custom-call | tf_op jit(solution)/shard_map/exchange_attended/pallas_call | solution.py:130
  58.2 0.0 copy-done
  58.2 0.0 copy-start.3
  58.2 1.7 merge.1
  59.9 8.7 %exchange_latent.1 = (bf16[8,32,768]{2,1,0:T(8,128)(2,1)S(1)}, bf16[16,256,128]{2,1,0:T(8,128)(2,1)S(1)}, bf16[256,512]{1,0:T(8,128)(2,1)S(1)}) custom-call(bf16[8,32,768]{2,1,0:T(8,128)(2,1)S(1)} %get-tuple-element.65.source, bf16[16,256,128]{2,1,0:T(8,128)(2,1)S(1)} %get-tuple-element.63.att_ref.att_all, ...), custom_call_target="tpu_custom_call" | custom-call | tf_op jit(solution)/shard_map/exchange_latent/pallas_call | solution.py:130
  68.7 0.0 copy-done.3
  68.7 10.6 %depth.1 = (bf16[32,768]{1,0:T(8,128)(2,1)S(1)}, bf16[4096,512]{1,0:T(8,128)(2,1)S(1)}) custom-call(bf16[8,32,768]{2,1,0:T(8,128)(2,1)S(1)} %get-tuple-element.67.part_ref, s32[32,8]{1,0:T(8,128)S(1)} %copy.8.code_ref, bf16[4096,512]{1,0:T(8,128)(2,1)S(1)} %copy-done.3), custom_call_target="tpu_custom_call" | custom-call | tf_op jit(solution)/shard_map/depth/pallas_call | solution.py:657
  79.3 11.5 %exchange_message.1 = (bf16[2,8,32,768]{3,2,1,0:T(8,128)(2,1)S(1)}, bf16[8,8,32,512]{3,2,1,0:T(8,128)(2,1)S(1)}) custom-call(bf16[32,768]{1,0:T(8,128)(2,1)S(1)} %get-tuple-element.68.source, bf16[8,2,8,32,512]{4,3,2,1,0:T(8,128)(2,1)S(1)} %bitcast.10), custom_call_target="tpu_custom_call" | custom-call | tf_op jit(solution)/shard_map/exchange_message/pallas_call | solution.py:130
  90.8 2.9 %unmerge.1 = (bf16[16,256,128]{2,1,0:T(8,128)(2,1)S(1)}, bf16[8,32,2560]{2,1,0:T(8,128)(2,1)S(1)}, bf16[8,8,32,512]{3,2,1,0:T(8,128)(2,1)S(1)}) custom-call(bf16[2,8,32,768]{3,2,1,0:T(8,128)(2,1)S(1)} %get-tuple-element.70.message_ref, f32[256,512]{1,0:T(8,128)S(1)} %get-tuple-element.71.merged_ref, bf16[256,512]{1,0:T(8,128)(2,1)S(1)} %get-tuple-element.66.merged.round_ref, ...), custom_call_target="tpu_custom_call" | custom-call | tf_op jit(solution)/shard_map/unmerge/pallas_call | solution.py:657
  93.7 42.3 %exchange_cotangent.1 = (bf16[2,8,256,128]{3,2,1,0:T(8,128)(2,1)S(1)}, bf16[4,2,32,2560]{3,2,1,0:T(8,128)(2,1)S(1)}, bf16[4,3,2,32,512]{4,3,2,1,0:T(8,128)(2,1)S(1)}) custom-call(bf16[16,256,128]{2,1,0:T(8,128)(2,1)S(1)} %get-tuple-element.75.source, bf16[4,2,32,2560]{3,2,1,0:T(8,128)(2,1)S(1)} %bitcast.17, bf16[8,2,4,32,512]{4,3,2,1,0:T(8,128)(2,1)S(1)} %bitcast.12), custom_call_target="tpu_custom_call" | custom-call | tf_op jit(solution)/shard_map/exchange_cotangent/pallas_call | solution.py:130
  136.0 0.4 prepare.1
  136.5 26.7 %exchange_grads.1 = (bf16[8,2,256,256]{3,2,1,0:T(8,128)(2,1)S(1)}, f32[8,8,512]{2,1,0:T(8,128)S(1)}, bf16[4,5,2,32,512]{4,3,2,1,0:T(8,128)(2,1)S(1)}, bf16[32,2560]{1,0:T(8,128)(2,1)S(1)}, bf16[256,4096]{1,0:T(8,128)(2,1)S(1)}) custom-call(bf16[2,256,256]{2,1,0:T(8,128)(2,1)S(1)} %get-tuple-element.82.pair, f32[8,512]{1,0:T(8,128)S(1)} %get-tuple-element.83.stats, ...), custom_call_target="tpu_custom_call" | custom-call | tf_op jit(solution)/shard_map/exchange_grads/pallas_call | solution.py:130
  163.2 10.2 %attend_back.1 = (bf16[4,2,2,160,256]{4,3,2,1,0:T(8,128)(2,1)S(1)}, bf16[2,2,4,224,256]{4,3,2,1,0:T(8,128)(2,1)S(1)}, bf16[8,2,32,512]{3,2,1,0:T(8,128)(2,1)S(1)...) custom-call(f32[8,8,512]{2,1,0:T(8,128)S(1)} %get-tuple-element.86.stats_ref, f32[512,64]{1,0:T(8,128)S(1)} %get-tuple-element.110.cos_ref, ...), custom_call_target="tpu_custom_call" | custom-call | tf_op jit(solution)/shard_map/attend_back/pallas_call | solution.py:657
  173.4 29.2 %exchange_first.1 = (bf16[4,2,2,160,256]{4,3,2,1,0:T(8,128)(2,1)S(1)}, bf16[2,2,4,224,256]{4,3,2,1,0:T(8,128)(2,1)S(1)}, bf16[4,2,2,32,512]{4,3,2,1,0:T(8,128)(2,1)S(1)}, bf16[8,32,256]{2,1,0:T(8,128)(2,1)S(1)}) custom-call(bf16[4,2,2,160,256]{4,3,2,1,0:T(8,128)(2,1)S(1)} %get-tuple-element.92.x_first, ...), custom_call_target="tpu_custom_call" | custom-call | tf_op jit(solution)/shard_map/exchange_first/pallas_call | solution.py:130
  202.6 0.4 middle_sum.1
  203.0 14.2 %exchange_second.1 = (bf16[2,160,256]{2,1,0:T(8,128)(2,1)S(1)}, bf16[4,2,224,256]{3,2,1,0:T(8,128)(2,1)S(1)}, bf16[2,2,32,512]{3,2,1,0:T(8,128)(2,1)S(1)}) custom-call(bf16[2,2,160,256]{3,2,1,0:T(8,128)(2,1)S(1)} %get-tuple-element.99.x_sum.x_own_ref, bf16[4,2,224,256]{3,2,1,0:T(8,128)(2,1)S(1)} %get-tuple-element.100.y_sum, ...), custom_call_target="tpu_custom_call" | custom-call | tf_op jit(solution)/shard_map/exchange_second/pallas_call | solution.py:130
  217.2 1.4 last_sum.1
  (2 shorter events, 0.0 us)
Async XLA Ops:
  2.4 3.4 %copy-start.1 = (bf16[4096,4,256]{2,1,0:T(4,128)(2,1)S(1)}, bf16[4096,4,256]{2,1,0:T(4,128)(2,1)}, u32[]{:S(2)}) copy-start(bf16[4096,4,256]{2,1,0:T(4,128)(2,1)} %w_ref.1) | copy-start | bytes 25165828
  5.8 1.6 copy-start.2
  13.5 44.7 %copy-start = (bf16[4096,512]{1,0:T(8,128)(2,1)S(1)}, bf16[4096,512]{1,0:T(8,128)(2,1)}, u32[]{:S(2)}) copy-start(bf16[4096,512]{1,0:T(8,128)(2,1)} %param.7) | copy-start | bytes 12582916
  58.2 10.5 %copy-start.3 = (bf16[4096,512]{1,0:T(8,128)(2,1)S(1)}, bf16[4096,512]{1,0:T(8,128)(2,1)}, u32[]{:S(2)}) copy-start(bf16[4096,512]{1,0:T(8,128)(2,1)} %stack_hbm.1) | copy-start | bytes 12582916

commit v6 on v5

--- a/solution.py
+++ b/solution.py
@@ -31,7 +31,7 @@
 TP_ORDER = (4, 1, 3, 5, 7, 2, 6)
 CHIP_ORDER = (2, 6, 1, 4, 3, 7, 5)
 LOG_SCALE = math.log2(math.e) / math.sqrt(HD)
-Z_EARLY = 3
+Z_EARLY = 1
 Z_LATE = CHIPS - Z_EARLY
 X_ROWS = 160
 Y_ROWS = 224
@@ -73,13 +73,14 @@
 
 
 def run_exchange(
-    peers, jobs, locals_, send_sems, recv_sems, forwards=(), relay=None, relay_after=()
+    peers, jobs, locals_, send_sems, recv_sems, forwards=(), relay=None, relay_after=0
 ):
     barrier = pltpu.get_barrier_semaphore()
     for peer in peers:
         pl.semaphore_signal(barrier, inc=1, device_id=peer, device_id_type=MESH)
     pl.semaphore_wait(barrier, len(peers))
     copies = []
+    arrived = set()
 
     def begin(source, target, device, *when):
         number = len(copies)
@@ -97,8 +98,22 @@
             copy.start()
         copies.append((copy, when))
 
-    for job in jobs:
+    first = jobs if relay is None else jobs[:relay_after]
+    for job in first:
         begin(*job)
+    if relay is not None:
+        total = len(jobs)
+
+        def settle():
+            for number in range(relay_after):
+                copies[number][0].wait_recv()
+                arrived.add(number)
+
+        def go_on():
+            for job in jobs[relay_after:]:
+                begin(*job)
+
+        finish = relay(total, send_sems, recv_sems, settle, go_on)
     for source, bounce, target, sem in locals_:
         copy = pltpu.make_async_copy(source, bounce, sem)
         copy.start()
@@ -106,16 +121,12 @@
         copy = pltpu.make_async_copy(bounce, target, sem)
         copy.start()
         copy.wait()
-    arrived = set()
     for number, job in forwards:
         copies[number][0].wait_recv()
         arrived.add(number)
         begin(*job)
     if relay is not None:
-        for number in relay_after:
-            copies[number][0].wait_recv()
-            arrived.add(number)
-        relay(len(copies), send_sems, recv_sems)
+        finish()
     for number, (copy, when) in enumerate(copies):
         if when:
             pl.when(when[0])(copy.wait_send)
@@ -148,7 +159,7 @@
 RELAY_COPIES = 23
 
 
-def relay_blocks(own, slot, mirrored, base, send_sems, recv_sems):
+def relay_blocks(own, slot, mirrored, base, send_sems, recv_sems, settle, go_on):
     seq, chip, core, tp = place()
     at_x, at_y = chip // 2, chip % 2
     column = 3 - at_x if mirrored else at_x
@@ -159,7 +170,7 @@
 
     def block(source, item):
         row = 1 - at_y if item == 2 else at_y
-        return slot(real(source) * 2 + row, 0 if item == 0 else 1)
+        return slot(real(source) * 2 + row, core if item == 0 else 1 - core)
 
     def copy(number, source, target, x, y):
         return pltpu.make_async_remote_copy(
@@ -179,16 +190,14 @@
             there = block(source, item)
             here = there if relayed or item == 2 else own(item)
             hops[source, target, item] = copy(at * 3 + item, here, there, real(target), at_y)
-    across_a = copy(18, own(0), slot(chip, 0), at_x, 1 - at_y)
-    across_b = copy(19, own(1), slot(chip, 1), at_x, 1 - at_y)
+    across_a = copy(18, own(0), slot(chip, core), at_x, 1 - at_y)
+    across_b = copy(19, own(1), slot(chip, 1 - core), at_x, 1 - at_y)
     across = [
         copy(20 + source, block(source, 0), block(source, 0), at_x, 1 - at_y)
         for source in range(3)
     ]
     sends_b = (line == 0) | (column < 3)
     gets_b = (line == 1) | (column < 3)
-    pl.when(line == 0)(across_a.start)
-    pl.when(sends_b)(across_b.start)
 
     def begin(items):
         for at in range(3):
@@ -200,7 +209,22 @@
                     if at == 0:
                         hops[0, 3, item].start()
 
-    begin((0, 1))
+    pl.when(line == 0)(across_a.start)
+    begin((0,))
+    settle()
+    pl.when(sends_b)(across_b.start)
+    begin((1,))
+    go_on()
+
+    def finish():
+        finish_relay(
+            column, line, sends_b, gets_b, begin, hops, across_a, across_b, across
+        )
+
+    return finish
+
+
+def finish_relay(column, line, sends_b, gets_b, begin, hops, across_a, across_b, across):
     pl.when(gets_b)(across_b.wait_recv)
     begin((2,))
 
@@ -282,14 +306,12 @@
         peers.append(other)
         jobs.append((out_w.at[other[1], half], w_half.at[tp], other))
 
-    def relay(base, send_sems, recv_sems):
-        relay_blocks(
-            lambda part: kv_all.at[chip, part],
+    def relay(*rest):
+        return relay_blocks(
+            lambda item: kv_all.at[chip, 1 - core] if item else kv.at[core],
             lambda source, part: kv_all.at[source, part],
             False,
-            base,
-            send_sems,
-            recv_sems,
+            *rest,
         )
 
     run_exchange(
@@ -303,7 +325,7 @@
         send_sems,
         recv_sems,
         relay=relay,
-        relay_after=(0,),
+        relay_after=1,
     )
 
 
@@ -502,14 +524,12 @@
     jobs.append((normed, normed_other, partner))
     peers.append(partner)
 
-    def relay(base, send_sems, recv_sems):
-        relay_blocks(
-            lambda part: pair.at[part],
+    def relay(*rest):
+        return relay_blocks(
+            lambda item: pair.at[1 - core if item else core],
             lambda source, part: pair_all.at[source, part],
             True,
-            base,
-            send_sems,
-            recv_sems,
+            *rest,
         )
 
     run_exchange(
@@ -665,77 +685,71 @@
     )(*ins)
 
 
+START_STEPS = 8
+
+
 def start_kernel(
-    hidden_ref, w_ref, cos_ref, sin_ref, normed_ref, kv_ref, query_ref, out_w_ref, total_ref
-):
-    step = pl.program_id(0)
+    hidden_ref, cos_ref, sin_ref, w_hbm, normed_ref, kv_ref, query_ref, out_w_ref, total_ref, w_ref, sems
+):
+    depth_rows = w_ref.shape[1]
+    copies = [
+        fetch(w_hbm.at[pl.ds(step * depth_rows, depth_rows)], w_ref.at[step], sems.at[step])
+        for step in range(START_STEPS)
+    ]
+    hidden = hidden_ref[...].astype(F32)
+    normed_ref[...] = (hidden * rms_scale(hidden)).astype(BF16)
+    pieces = depth_rows // (TP * 32)
+    for step in range(START_STEPS):
+        copies[step].wait()
+        weights = w_ref[step].reshape(depth_rows, 8 * HD)
+        normed = normed_ref[:, step * depth_rows : (step + 1) * depth_rows]
+        term = dot_nn(normed, weights[:, : 6 * HD])
+        if step:
+            total_ref[...] += term
+        else:
+            total_ref[...] = term
+        out_w = weights[:, 6 * HD :].reshape(pieces, TP, 32, 2 * HD)
+        for at in range(TP):
+            for piece in range(pieces):
+                low = (step * pieces + piece) * 32
+                out_w_ref[at, low : low + 32] = out_w[piece, at]
     own = pl.ds(pl.multiple_of(lax.axis_index("seq") % 2 * FR, FR), FR)
-    depth_rows = w_ref.shape[0]
-
-    @pl.when(step == 0)
-    def _():
-        hidden = hidden_ref[...].astype(F32)
-        normed_ref[...] = (hidden * rms_scale(hidden)).astype(BF16)
-        total_ref[...] = jnp.zeros_like(total_ref)
-
-    normed = normed_ref[:, pl.ds(pl.multiple_of(step * depth_rows, depth_rows), depth_rows)]
-    weights = w_ref[...].reshape(depth_rows, 8 * HD)
-    total_ref[...] += dot_nn(normed, weights[:, : 6 * HD])
-    out_w = weights[:, 6 * HD :].reshape(-1, TP, 32, 2 * HD)
-    for at in range(TP):
-        for piece in range(out_w.shape[0]):
-            out_w_ref[at, piece * 32 : (piece + 1) * 32] = out_w[piece, at]
-
-    @pl.when(step == pl.num_programs(0) - 1)
-    def _():
-        cosine, sine = cos_ref[own], sin_ref[own]
-
-        def turned(at):
-            lower = total_ref[:, at : at + HD // 2]
-            upper = total_ref[:, at + HD // 2 : at + HD]
-            return jnp.concatenate(
-                [lower * cosine - upper * sine, upper * cosine + lower * sine], axis=1
-            ).astype(BF16)
-
-        for head in range(2):
-            query_ref[head] = turned(head * HD)
-            kv_ref[head, :, :HD] = turned((2 + head) * HD)
-            at = (4 + head) * HD
-            kv_ref[head, :, HD:] = total_ref[:, at : at + HD].astype(BF16)
+    cosine, sine = cos_ref[own], sin_ref[own]
+
+    def turned(at):
+        lower = total_ref[:, at : at + HD // 2]
+        upper = total_ref[:, at + HD // 2 : at + HD]
+        return jnp.concatenate(
+            [lower * cosine - upper * sine, upper * cosine + lower * sine], axis=1
+        ).astype(BF16)
+
+    for head in range(2):
+        query_ref[head] = turned(head * HD)
+        kv_ref[head, :, :HD] = turned((2 + head) * HD)
+        at = (4 + head) * HD
+        kv_ref[head, :, HD:] = total_ref[:, at : at + HD].astype(BF16)
 
 
 def start(hidden, weights, cosine, sine):
-    steps = 8
-    depth_rows = weights.shape[0] // steps
-
-    def whole(*shape):
-        return pl.BlockSpec(shape, lambda step: (0,) * len(shape))
-
-    return pl.pallas_call(
+    depth_rows = weights.shape[0] // START_STEPS
+    return compute(
         start_kernel,
-        name="start",
-        grid=(steps,),
-        out_shape=[
+        "start",
+        (hidden, cosine, sine, weights),
+        [
             jax.ShapeDtypeStruct(hidden.shape, BF16),
             jax.ShapeDtypeStruct((2, FR, 2 * HD), BF16),
             jax.ShapeDtypeStruct((2, FR, HD), BF16),
             jax.ShapeDtypeStruct((TP, NS, 2 * HD), BF16),
         ],
-        in_specs=[
-            whole(*hidden.shape),
-            pl.BlockSpec((depth_rows, 4, 2 * HD), lambda step: (step, 0, 0)),
-            whole(*cosine.shape),
-            whole(*sine.shape),
-        ],
-        out_specs=[
-            whole(*hidden.shape),
-            whole(2, FR, 2 * HD),
-            whole(2, FR, HD),
-            pl.BlockSpec((TP, depth_rows // TP, 2 * HD), lambda step: (0, step, 0)),
-        ],
-        scratch_shapes=[pltpu.VMEM((FR, 6 * HD), F32)],
-        compiler_params=pltpu.CompilerParams(vmem_limit_bytes=24 * MIB),
-    )(hidden, weights, cosine, sine)
+        [
+            pltpu.VMEM((FR, 6 * HD), F32),
+            pltpu.VMEM((START_STEPS, depth_rows) + weights.shape[1:], BF16),
+            pltpu.SemaphoreType.DMA((START_STEPS,)),
+        ],
+        hbm=1,
+        limit=32,
+    )
 
 
 def attend_kernel(kv_ref, query_ref, out_ref, out_t_ref, level_ref, score_ref):

time: 219 us -> 206 us (0.941)
  Pallas kernels: 211 us -> 196 us
    pallas_call x8, Pallas kernels: 176 us -> 162 us  [exchange(): pl.pallas_call(kernel, name=name, out_shape=outs, in_specs=[ANY] * len(in...]
    pallas_call x1 -> x0, Pallas kernels: 6.13 us -> none  [start(): pl.pallas_call(start_kernel, name='start', grid=(steps,), out_shape=[jax....]
    pallas_call x8 -> x9, Pallas kernels: 28.7 us -> 34 us  [compute(): pl.pallas_call(kernel, name=name, out_shape=outs, in_specs=[VMEM] * (len(...]
    unnamed x9 -> x11, local copies, waits for them, and re-layouts: 5.74 us -> 7.92 us
where the time goes in v6:
time: 206 us; the launch traced here: 205 us
  Pallas kernels  196 us (95%)
  local copies, waits for them, and re-layouts  7.92 us (4%)
    pallas_call x8, Pallas kernels, exchange(): pl.pallas_call(kernel, name=name, out_shape=outs, in_specs=[ANY] * len(in...  162 us
    pallas_call x9, Pallas kernels, compute(): pl.pallas_call(kernel, name=name, out_shape=outs, in_specs=[VMEM] * (len(...  34 us
    unnamed x11, local copies, waits for them, and re-layouts  7.92 us

profile of v6, /device:TPU:1, one launch (start us, length us, event | category | flops | bytes accessed | tf_op | source)
XLA Modules:
  0.0 205.3 jit_solution(10782414730195140791)
XLA Ops:
  0.7 0.8 copy.8.code_ref
  1.4 1.0 multiply_sine_fusion
  2.4 0.0 copy-start.1
  2.4 3.4 %copy-done.1 = bf16[4096,4,256]{2,1,0:T(4,128)(2,1)S(1)} copy-done((bf16[4096,4,256]{2,1,0:T(4,128)(2,1)S(1)}, bf16[4096,4,256]{2,1,0:T(4,128)(2,1)}, u32[]{:S(2)}) %copy-start.1) | copy-done | bytes 8388632
  5.8 0.0 copy-start.2
  5.8 1.6 copy-done.2
  7.4 0.0 copy-start.3
  7.4 5.4 %start.1 = (bf16[256,4096]{1,0:T(8,128)(2,1)S(1)}, bf16[2,256,256]{2,1,0:T(8,128)(2,1)S(1)}, bf16[2,256,128]{2,1,0:T(8,128)(2,1)S(1)}, bf16[8,512,256]{2,1,0:T(8,128)(2,1)S(1)}) custom-call(bf16[256,4096]{1,0:T(8,128)(2,1)S(1)} %copy-done.2, f32[512,64]{1,0:T(8,128)S(1)} %get-tuple-element.110.cos_ref, f32[512,64]{1,0:T(8,128)S(1)} %get-tuple-element.109.sin_ref, ...), custom_call_target="tpu_custom_call" | custom-call | tf_op jit(solution)/shard_map/start/pallas_call | solution.py:677
  12.8 0.0 copy-start
  12.8 25.6 %exchange_keys.1 = (bf16[8,2,256,256]{3,2,1,0:T(8,128)(2,1)S(1)}, bf16[2,256,128]{2,1,0:T(8,128)(2,1)S(1)}, bf16[8,256,256]{2,1,0:T(8,128)(2,1)S(1)}) custom-call(bf16[2,256,256]{2,1,0:T(8,128)(2,1)S(1)} %get-tuple-element.56.kv, bf16[2,256,128]{2,1,0:T(8,128)(2,1)S(1)} %get-tuple-element.57.query, bf16[8,512,256]{2,1,0:T(8,128)(2,1)S(1)} %get-tuple-element.58.out_w), custom_call_target="tpu_custom_call" | custom-call | tf_op jit(solution)/shard_map/exchange_keys/pallas_call | solution.py:141
  38.4 1.0 attend.1
  39.4 17.9 %exchange_attended.1 = (bf16[16,256,128]{2,1,0:T(8,128)(2,1)S(1)}, bf16[8,256,256]{2,1,0:T(8,128)(2,1)S(1)}) custom-call(bf16[512,128]{1,0:T(8,128)(2,1)S(1)} %get-tuple-element.61.source, bf16[8,256,256]{2,1,0:T(8,128)(2,1)S(1)} %get-tuple-element.62.w_half.half_ref), custom_call_target="tpu_custom_call" | custom-call | tf_op jit(solution)/shard_map/exchange_attended/pallas_call | solution.py:141
  57.4 0.0 copy-done.3
  57.4 0.0 copy-done
  57.4 1.7 merge.1
  59.1 8.7 %exchange_latent.1 = (bf16[8,32,768]{2,1,0:T(8,128)(2,1)S(1)}, bf16[16,256,128]{2,1,0:T(8,128)(2,1)S(1)}, bf16[256,512]{1,0:T(8,128)(2,1)S(1)}) custom-call(bf16[8,32,768]{2,1,0:T(8,128)(2,1)S(1)} %get-tuple-element.65.source, bf16[16,256,128]{2,1,0:T(8,128)(2,1)S(1)} %get-tuple-element.63.att_ref.att_all, ...), custom_call_target="tpu_custom_call" | custom-call | tf_op jit(solution)/shard_map/exchange_latent/pallas_call | solution.py:141
  67.8 0.0 copy-start.4
  67.9 2.2 %copy-done.4 = bf16[4096,512]{1,0:T(8,128)(2,1)S(1)} copy-done((bf16[4096,512]{1,0:T(8,128)(2,1)S(1)}, bf16[4096,512]{1,0:T(8,128)(2,1)}, u32[]{:S(2)}) %copy-start.4) | copy-done | bytes 4194328
  70.0 10.6 %depth.1 = (bf16[32,768]{1,0:T(8,128)(2,1)S(1)}, bf16[4096,512]{1,0:T(8,128)(2,1)S(1)}) custom-call(bf16[8,32,768]{2,1,0:T(8,128)(2,1)S(1)} %get-tuple-element.67.part_ref, s32[32,8]{1,0:T(8,128)S(1)} %copy.8.code_ref, bf16[4096,512]{1,0:T(8,128)(2,1)S(1)} %copy-done.4), custom_call_target="tpu_custom_call" | custom-call | tf_op jit(solution)/shard_map/depth/pallas_call | solution.py:677
  80.6 11.2 %exchange_message.1 = (bf16[2,8,32,768]{3,2,1,0:T(8,128)(2,1)S(1)}, bf16[8,8,32,512]{3,2,1,0:T(8,128)(2,1)S(1)}) custom-call(bf16[32,768]{1,0:T(8,128)(2,1)S(1)} %get-tuple-element.68.source, bf16[8,2,8,32,512]{4,3,2,1,0:T(8,128)(2,1)S(1)} %bitcast.10), custom_call_target="tpu_custom_call" | custom-call | tf_op jit(solution)/shard_map/exchange_message/pallas_call | solution.py:141
  91.9 2.9 %unmerge.1 = (bf16[16,256,128]{2,1,0:T(8,128)(2,1)S(1)}, bf16[8,32,2560]{2,1,0:T(8,128)(2,1)S(1)}, bf16[8,8,32,512]{3,2,1,0:T(8,128)(2,1)S(1)}) custom-call(bf16[2,8,32,768]{3,2,1,0:T(8,128)(2,1)S(1)} %get-tuple-element.70.message_ref, f32[256,512]{1,0:T(8,128)S(1)} %get-tuple-element.71.merged_ref, bf16[256,512]{1,0:T(8,128)(2,1)S(1)} %get-tuple-element.66.merged.round_ref, ...), custom_call_target="tpu_custom_call" | custom-call | tf_op jit(solution)/shard_map/unmerge/pallas_call | solution.py:677
  94.8 29.5 %exchange_cotangent.1 = (bf16[2,8,256,128]{3,2,1,0:T(8,128)(2,1)S(1)}, bf16[4,2,32,2560]{3,2,1,0:T(8,128)(2,1)S(1)}, bf16[4,1,2,32,512]{4,3,2,1,0:T(8,128)(2,1)S(1)}) custom-call(bf16[16,256,128]{2,1,0:T(8,128)(2,1)S(1)} %get-tuple-element.75.source, bf16[4,2,32,2560]{3,2,1,0:T(8,128)(2,1)S(1)} %bitcast.17, bf16[8,2,4,32,512]{4,3,2,1,0:T(8,128)(2,1)S(1)} %bitcast.12), custom_call_target="tpu_custom_call" | custom-call | tf_op jit(solution)/shard_map/exchange_cotangent/pallas_call | solution.py:141
  124.3 0.4 prepare.1
  124.7 29.1 %exchange_grads.1 = (bf16[8,2,256,256]{3,2,1,0:T(8,128)(2,1)S(1)}, f32[8,8,512]{2,1,0:T(8,128)S(1)}, bf16[4,7,2,32,512]{4,3,2,1,0:T(8,128)(2,1)S(1)}, bf16[32,2560]{1,0:T(8,128)(2,1)S(1)}, bf16[256,4096]{1,0:T(8,128)(2,1)S(1)}) custom-call(bf16[2,256,256]{2,1,0:T(8,128)(2,1)S(1)} %get-tuple-element.82.pair, f32[8,512]{1,0:T(8,128)S(1)} %get-tuple-element.83.stats, ...), custom_call_target="tpu_custom_call" | custom-call | tf_op jit(solution)/shard_map/exchange_grads/pallas_call | solution.py:141
  153.9 10.2 %attend_back.1 = (bf16[4,2,2,160,256]{4,3,2,1,0:T(8,128)(2,1)S(1)}, bf16[2,2,4,224,256]{4,3,2,1,0:T(8,128)(2,1)S(1)}, bf16[8,2,32,512]{3,2,1,0:T(8,128)(2,1)S(1)...) custom-call(f32[8,8,512]{2,1,0:T(8,128)S(1)} %get-tuple-element.86.stats_ref, f32[512,64]{1,0:T(8,128)S(1)} %get-tuple-element.110.cos_ref, ...), custom_call_target="tpu_custom_call" | custom-call | tf_op jit(solution)/shard_map/attend_back/pallas_call | solution.py:677
  164.1 25.6 %exchange_first.1 = (bf16[4,2,2,160,256]{4,3,2,1,0:T(8,128)(2,1)S(1)}, bf16[2,2,4,224,256]{4,3,2,1,0:T(8,128)(2,1)S(1)}, bf16[4,2,2,32,512]{4,3,2,1,0:T(8,128)(2,1)S(1)}, bf16[8,32,256]{2,1,0:T(8,128)(2,1)S(1)}) custom-call(bf16[4,2,2,160,256]{4,3,2,1,0:T(8,128)(2,1)S(1)} %get-tuple-element.92.x_first, ...), custom_call_target="tpu_custom_call" | custom-call | tf_op jit(solution)/shard_map/exchange_first/pallas_call | solution.py:141
  189.6 0.4 middle_sum.1
  190.1 13.8 %exchange_second.1 = (bf16[2,160,256]{2,1,0:T(8,128)(2,1)S(1)}, bf16[4,2,224,256]{3,2,1,0:T(8,128)(2,1)S(1)}, bf16[2,2,32,512]{3,2,1,0:T(8,128)(2,1)S(1)}) custom-call(bf16[2,2,160,256]{3,2,1,0:T(8,128)(2,1)S(1)} %get-tuple-element.99.x_sum.x_own_ref, bf16[4,2,224,256]{3,2,1,0:T(8,128)(2,1)S(1)} %get-tuple-element.100.y_sum, ...), custom_call_target="tpu_custom_call" | custom-call | tf_op jit(solution)/shard_map/exchange_second/pallas_call | solution.py:141
  203.9 1.4 last_sum.1
  (2 shorter events, 0.0 us)
Async XLA Ops:
  2.4 3.4 %copy-start.1 = (bf16[4096,4,256]{2,1,0:T(4,128)(2,1)S(1)}, bf16[4096,4,256]{2,1,0:T(4,128)(2,1)}, u32[]{:S(2)}) copy-start(bf16[4096,4,256]{2,1,0:T(4,128)(2,1)} %w_hbm.1) | copy-start | bytes 25165828
  5.8 1.6 copy-start.2
  7.4 50.0 %copy-start.3 = (bf16[256,4096]{1,0:T(8,128)(2,1)S(1)}, bf16[256,4096]{1,0:T(8,128)(2,1)}, u32[]{:S(2)}) copy-start(bf16[256,4096]{1,0:T(8,128)(2,1)} %hidden_ref.3) | copy-start | bytes 6291460
  12.8 44.6 %copy-start = (bf16[4096,512]{1,0:T(8,128)(2,1)S(1)}, bf16[4096,512]{1,0:T(8,128)(2,1)}, u32[]{:S(2)}) copy-start(bf16[4096,512]{1,0:T(8,128)(2,1)} %param.7) | copy-start | bytes 12582916
  67.8 2.2 %copy-start.4 = (bf16[4096,512]{1,0:T(8,128)(2,1)S(1)}, bf16[4096,512]{1,0:T(8,128)(2,1)}, u32[]{:S(2)}) copy-start(bf16[4096,512]{1,0:T(8,128)(2,1)} %stack_hbm.1) | copy-start | bytes 12582916

commit v7 on v6

--- a/solution.py
+++ b/solution.py
@@ -33,8 +33,10 @@
 LOG_SCALE = math.log2(math.e) / math.sqrt(HD)
 Z_EARLY = 1
 Z_LATE = CHIPS - Z_EARLY
-X_ROWS = 160
-Y_ROWS = 224
+KEY_FIRST = 128
+PAIR_FIRST = 256
+X_ROWS = 176
+Y_ROWS = 208
 
 
 def dot_nn(left, right):
@@ -170,7 +172,7 @@
 
     def block(source, item):
         row = 1 - at_y if item == 2 else at_y
-        return slot(real(source) * 2 + row, core if item == 0 else 1 - core)
+        return slot(real(source) * 2 + row, item)
 
     def copy(number, source, target, x, y):
         return pltpu.make_async_remote_copy(
@@ -190,8 +192,8 @@
             there = block(source, item)
             here = there if relayed or item == 2 else own(item)
             hops[source, target, item] = copy(at * 3 + item, here, there, real(target), at_y)
-    across_a = copy(18, own(0), slot(chip, core), at_x, 1 - at_y)
-    across_b = copy(19, own(1), slot(chip, 1 - core), at_x, 1 - at_y)
+    across_a = copy(18, own(0), slot(chip, 0), at_x, 1 - at_y)
+    across_b = copy(19, own(1), slot(chip, 1), at_x, 1 - at_y)
     across = [
         copy(20 + source, block(source, 0), block(source, 0), at_x, 1 - at_y)
         for source in range(3)
@@ -275,6 +277,14 @@
                 across[source].wait()
 
 
+def first_part(core, rows):
+    return pl.ds(pl.multiple_of(core * (FR2 - rows), 16), rows)
+
+
+def rest_part(core, rows):
+    return pl.ds(pl.multiple_of((1 - core) * rows, 16), FR2 - rows)
+
+
 def near_peers(seq, chip, core, tp):
     x, y = chip // 2, chip % 2
     return [
@@ -300,25 +310,41 @@
     peers = near_peers(seq, chip, core, tp)
     partner = peers[-1]
     half = pl.ds(core * FR, FR)
-    jobs = [(kv.at[1 - core], kv_all.at[chip, core], partner)]
+    own = pl.ds(pl.multiple_of(core * FR, FR), FR)
+    jobs = [(kv.at[1 - core], kv_all.at[chip, own], partner)]
     jobs.append((query.at[1 - core], query_two.at[core], partner))
     for other in tp_peers(seq, tp):
         peers.append(other)
         jobs.append((out_w.at[other[1], half], w_half.at[tp], other))
 
-    def relay(*rest):
+    def part(item):
+        return rest_part(core, KEY_FIRST) if item else first_part(core, KEY_FIRST)
+
+    inner = pl.ds(pl.multiple_of(core * (FR - KEY_FIRST), 16), KEY_FIRST)
+
+    def relay(base, send_sems, recv_sems, settle, go_on):
+        def settle_both():
+            for source, target in ((kv.at[core], kv_bounce), (kv_bounce, kv_all.at[chip, own])):
+                copy = pltpu.make_async_copy(source, target, sem)
+                copy.start()
+                copy.wait()
+            settle()
+
         return relay_blocks(
-            lambda item: kv_all.at[chip, 1 - core] if item else kv.at[core],
-            lambda source, part: kv_all.at[source, part],
+            lambda item: kv_all.at[chip, part(1)] if item else kv.at[core, inner],
+            lambda source, item: kv_all.at[source, part(1 if item else 0)],
             False,
-            *rest,
+            base,
+            send_sems,
+            recv_sems,
+            settle_both,
+            go_on,
         )
 
     run_exchange(
         peers,
         jobs,
         [
-            (kv.at[core], kv_bounce, kv_all.at[chip, core], sem),
             (query.at[core], query_bounce, query_two.at[core], sem),
             (out_w.at[tp, half], w_bounce, w_half.at[tp], sem),
         ],
@@ -336,7 +362,7 @@
         1,
         (kv, query, out_w),
         [
-            jax.ShapeDtypeStruct((CHIPS, 2, FR, 2 * HD), BF16),
+            jax.ShapeDtypeStruct((CHIPS, FR2, 2 * HD), BF16),
             jax.ShapeDtypeStruct((2, FR, HD), BF16),
             jax.ShapeDtypeStruct((TP, FR, 2 * HD), BF16),
         ],
@@ -524,10 +550,13 @@
     jobs.append((normed, normed_other, partner))
     peers.append(partner)
 
+    def part(item):
+        return rest_part(core, PAIR_FIRST) if item else first_part(core, PAIR_FIRST)
+
     def relay(*rest):
         return relay_blocks(
-            lambda item: pair.at[1 - core if item else core],
-            lambda source, part: pair_all.at[source, part],
+            lambda item: pair.at[part(item)],
+            lambda source, item: pair_all.at[source, part(item)],
             True,
             *rest,
         )
@@ -809,10 +838,12 @@
 
 
 def merge_kernel(
-    att_ref, half_ref, other_ref, hidden_ref, depth_in_hbm, merged_ref, round_ref, part_ref, depth_in_ref, sem
+    att_ref, half_ref, other_ref, hidden_ref, depth_in_hbm, stack_hbm,
+    merged_ref, round_ref, part_ref, stack_ref, depth_in_ref, sem, stack_sem,
 ):
     seq, chip, core, tp = place()
     copy = fetch(depth_in_hbm.at[:, tp], depth_in_ref, sem)
+    stack_copy = fetch(stack_hbm, stack_ref, stack_sem)
     width = hidden_ref.shape[1]
     group = width // 2
     row_at = lax.broadcasted_iota(jnp.int32, (group, FR), 0)
@@ -840,40 +871,41 @@
     part_ref[:, :, :DD] = latent.astype(BF16).reshape(TP, FR // TP, DD)
     part_ref[:, :, DD : DD + HD] = jnp.broadcast_to(coarse, (FR, HD)).reshape(TP, FR // TP, HD)
     part_ref[:, :, DD + HD :] = jnp.broadcast_to(fine, (FR, HD)).reshape(TP, FR // TP, HD)
-
-
-def merge(att_all, w_half, w_other, hidden, depth_in):
+    stack_copy.wait()
+
+
+def merge(att_all, w_half, w_other, hidden, depth_in, stack):
     return compute(
         merge_kernel,
         "merge",
-        (att_all, w_half, w_other, hidden, depth_in),
+        (att_all, w_half, w_other, hidden, depth_in, stack),
         [
             jax.ShapeDtypeStruct((FR, NS), F32),
             jax.ShapeDtypeStruct((FR, NS), BF16),
             jax.ShapeDtypeStruct((TP, FR // TP, DD + 2 * HD), BF16),
-        ],
-        [pltpu.VMEM((2 * CHIPS, 32, DD), BF16), pltpu.SemaphoreType.DMA],
-        hbm=1,
+            jax.ShapeDtypeStruct(stack.shape, BF16),
+        ],
+        [
+            pltpu.VMEM((2 * CHIPS, 32, DD), BF16),
+            pltpu.SemaphoreType.DMA,
+            pltpu.SemaphoreType.DMA,
+        ],
+        hbm=2,
         limit=24,
     )
 
 
 def depth_kernel(
-    width, loss_scale, part_ref, code_ref, stack_hbm, message_ref, grad_ref, prob_ref, stack_ref, sems
-):
-    frames, books = code_ref.shape
-    pieces = ((3072, 1024), (0, 1536), (1536, 512), (2048, 1024))
-    copies = [
-        fetch(stack_hbm.at[pl.ds(low, rows)], stack_ref.at[pl.ds(low, rows)], sems.at[at])
-        for at, (low, rows) in enumerate(pieces)
-    ]
+    width, loss_scale, part_ref, code_ref, stack_ref, message_ref, grad_ref, prob_ref
+):
+    books, frames = code_ref.shape
     grid = (frames, books, books)
     row_at = lax.broadcasted_iota(jnp.int32, grid, 1)
     col_at = lax.broadcasted_iota(jnp.int32, grid, 2)
-    spread = jnp.broadcast_to(code_ref[...][:, None, :], grid)
+    spread = jnp.broadcast_to(code_ref[...].astype(F32).T[:, None, :], grid)
 
     def column(wanted):
-        picked = jnp.where(wanted, spread + 1, 0).astype(F32)
+        picked = jnp.where(wanted, spread + 1.0, 0.0)
         picked = jnp.sum(picked, axis=-1, keepdims=True).reshape(frames * books, 1)
         return picked - 1.0
 
@@ -888,11 +920,9 @@
     latent = jnp.broadcast_to(latent[:, None, :], (frames, books, DD)).reshape(tokens, DD)
     vocab_at = lax.broadcasted_iota(jnp.int32, (tokens, VOCAB), 1).astype(F32)
     hot = jnp.where(before == vocab_at, 1.0, 0.0).astype(BF16)
-    copies[0].wait()
     stream = latent + dot_nn(hot, stack_ref[4 * DD + VOCAB :])
     stream_scale = rms_scale(stream)
     stream_norm = (stream * stream_scale).astype(BF16)
-    copies[1].wait()
     qkv_rows = stack_ref[: 3 * DD]
     proj = dot_nt(stream_norm, qkv_rows).astype(BF16)
     row_at = lax.broadcasted_iota(jnp.int32, (tokens, tokens), 0)
@@ -911,12 +941,10 @@
         prob_ref[head] = probs
         mixed.append(dot_nn(probs.astype(BF16), values))
     mixed = jnp.concatenate(mixed, axis=1).astype(BF16)
-    copies[2].wait()
     out_rows = stack_ref[3 * DD : 4 * DD]
     resid = stream + dot_nt(mixed, out_rows)
     resid_scale = rms_scale(resid)
     resid_norm = (resid * resid_scale).astype(BF16)
-    copies[3].wait()
     head_rows = stack_ref[4 * DD : 4 * DD + VOCAB]
     logits = dot_nt(resid_norm, head_rows)
     weights = jnp.exp(logits - jnp.max(logits, axis=-1, keepdims=True))
@@ -969,10 +997,7 @@
         ],
         [
             pltpu.VMEM((DD // DHD, tokens, tokens), F32),
-            pltpu.VMEM(stack.shape, BF16),
-            pltpu.SemaphoreType.DMA((4,)),
-        ],
-        hbm=1,
+        ],
         limit=32,
     )
 
@@ -1079,8 +1104,8 @@
     part_ref, query_ref, out_t_ref, level_ref, side_x_ref, pair_ref, stats_ref, side_ref
 ):
     gradient = jnp.sum(part_ref[...].astype(F32), axis=1).reshape(FR2, HD).astype(BF16)
-    pair_ref[:, :, :HD] = query_ref[...].reshape(2, FR, HD)
-    pair_ref[:, :, HD:] = gradient.reshape(2, FR, HD)
+    pair_ref[:, :HD] = query_ref[...]
+    pair_ref[:, HD:] = gradient
     inner = jnp.sum(gradient.astype(F32).T * out_t_ref[...], axis=0, keepdims=True)
     stats_ref[...] = jnp.concatenate(
         [level_ref[...], inner, jnp.zeros((6, FR2), F32)], axis=0
@@ -1094,7 +1119,7 @@
         "prepare",
         (parts, query, out_t, level, side_x),
         [
-            jax.ShapeDtypeStruct((2, FR, 2 * HD), BF16),
+            jax.ShapeDtypeStruct((FR2, 2 * HD), BF16),
             jax.ShapeDtypeStruct((8, FR2), F32),
             jax.ShapeDtypeStruct(side_x.shape[1:], BF16),
         ],
@@ -1267,15 +1292,16 @@
     cosine, sine = angle_tables(chip * FR2, FR2)
     normed, kv, query, out_w = start(hidden_in, temporal_weight_stack, cosine, sine)
     kv_all, query, w_half = exchange_keys(kv, query, out_w)
-    kv_all = kv_all.reshape(CHIPS, FR2, 2 * HD)
     query = query.reshape(FR2, HD)
 
     depth_in = depth_in.reshape(seq_count, TP, -1, DD)
     attended, out_t, level = attend(kv_all, query)
     att_all, w_other = exchange_attended(attended, w_half)
-    merged, rounded, latent_parts = merge(att_all, w_half, w_other, hidden_in, depth_in)
+    merged, rounded, latent_parts, depth_stack = merge(
+        att_all, w_half, w_other, hidden_in, depth_in, depth_stack
+    )
     latent_parts, att_other, rounded_other = exchange_latent(latent_parts, att_all, rounded)
-    message, grads = depth(latent_parts, audio_codes, depth_stack, width, loss_scale)
+    message, grads = depth(latent_parts, audio_codes.T, depth_stack, width, loss_scale)
     grads = grads.reshape(CHIPS, 2, TP, -1, DD)
     messages, grads_other = exchange_message(message, grads)
     cotangent_parts, side, grads = unmerge(
@@ -1306,7 +1332,7 @@
         side,
         side_in,
         kv_all,
-        pair_all.reshape(CHIPS, FR2, 2 * HD),
+        pair_all,
         early,
         late,
         normed,

time: 206 us -> 199 us (0.966)
  Pallas kernels: 196 us -> 192 us
  local copies, waits for them, and re-layouts: 7.92 us -> 4.99 us
    pallas_call x8, Pallas kernels: 162 us -> 158 us  [exchange(): pl.pallas_call(kernel, name=name, out_shape=outs, in_specs=[ANY] * len(in...]
    unnamed x11 -> x12, local copies, waits for them, and re-layouts: 7.92 us -> 4.99 us
where the time goes in v7:
time: 199 us; the launch traced here: 198 us
  Pallas kernels  192 us (96%)
  local copies, waits for them, and re-layouts  4.99 us (3%)
    pallas_call x8, Pallas kernels, exchange(): pl.pallas_call(kernel, name=name, out_shape=outs, in_specs=[ANY] * len(in...  158 us
    pallas_call x9, Pallas kernels, compute(): pl.pallas_call(kernel, name=name, out_shape=outs, in_specs=[VMEM] * (len(...  33.6 us
    unnamed x12, local copies, waits for them, and re-layouts  4.99 us

profile of v7, /device:TPU:1, one launch (start us, length us, event | category | flops | bytes accessed | tf_op | source)
XLA Modules:
  0.0 198.3 jit_solution(9326755113927715383)
XLA Ops:
  0.7 1.0 multiply_sine_fusion
  1.7 0.0 copy-start.1
  1.7 3.4 %copy-done.1 = bf16[4096,4,256]{2,1,0:T(4,128)(2,1)S(1)} copy-done((bf16[4096,4,256]{2,1,0:T(4,128)(2,1)S(1)}, bf16[4096,4,256]{2,1,0:T(4,128)(2,1)}, u32[]{:S(2)}) %copy-start.1) | copy-done | bytes 8388632
  5.0 0.0 copy-start.2
  5.0 1.6 copy-done.2
  6.6 0.0 copy-start.3
  6.6 0.0 copy-start.4
  6.6 5.4 %start.1 = (bf16[256,4096]{1,0:T(8,128)(2,1)S(1)}, bf16[2,256,256]{2,1,0:T(8,128)(2,1)S(1)}, bf16[2,256,128]{2,1,0:T(8,128)(2,1)S(1)}, bf16[8,512,256]{2,1,0:T(8,128)(2,1)S(1)}) custom-call(bf16[256,4096]{1,0:T(8,128)(2,1)S(1)} %copy-done.2, f32[512,64]{1,0:T(8,128)S(1)} %get-tuple-element.112.cos_ref, f32[512,64]{1,0:T(8,128)S(1)} %get-tuple-element.111.sin_ref, ...), custom_call_target="tpu_custom_call" | custom-call | tf_op jit(solution)/shard_map/start/pallas_call | solution.py:706
  12.0 0.0 copy-start
  12.0 27.1 %exchange_keys.1 = (bf16[8,512,256]{2,1,0:T(8,128)(2,1)S(1)}, bf16[2,256,128]{2,1,0:T(8,128)(2,1)S(1)}, bf16[8,256,256]{2,1,0:T(8,128)(2,1)S(1)}) custom-call(bf16[2,256,256]{2,1,0:T(8,128)(2,1)S(1)} %get-tuple-element.57.kv, bf16[2,256,128]{2,1,0:T(8,128)(2,1)S(1)} %get-tuple-element.58.query, bf16[8,512,256]{2,1,0:T(8,128)(2,1)S(1)} %get-tuple-element.59.out_w), custom_call_target="tpu_custom_call" | custom-call | tf_op jit(solution)/shard_map/exchange_keys/pallas_call | solution.py:143
  39.1 1.0 attend.1
  40.1 17.0 %exchange_attended.1 = (bf16[16,256,128]{2,1,0:T(8,128)(2,1)S(1)}, bf16[8,256,256]{2,1,0:T(8,128)(2,1)S(1)}) custom-call(bf16[512,128]{1,0:T(8,128)(2,1)S(1)} %get-tuple-element.62.source, bf16[8,256,256]{2,1,0:T(8,128)(2,1)S(1)} %get-tuple-element.63.w_half.half_ref), custom_call_target="tpu_custom_call" | custom-call | tf_op jit(solution)/shard_map/exchange_attended/pallas_call | solution.py:143
  57.1 0.0 copy-done.3
  57.1 0.0 copy-done.4
  57.1 0.0 copy-done
  57.1 0.0 copy-start.5
  57.1 2.0 %merge.1 = (f32[256,512]{1,0:T(8,128)S(1)}, bf16[256,512]{1,0:T(8,128)(2,1)S(1)}, bf16[8,32,768]{2,1,0:T(8,128)(2,1)S(1)}, bf16[4096,512]{1,0:T(8,128)(2,1)S(1)}) custom-call(bf16[16,256,128]{2,1,0:T(8,128)(2,1)S(1)} %get-tuple-element.64.att_ref.att_all, bf16[8,256,256]{2,1,0:T(8,128)(2,1)S(1)} %get-tuple-element.63.w_half.half_ref, ...), custom_call_target="tpu_custom_call" | custom-call | tf_op jit(solution)/shard_map/merge/pallas_call | solution.py:706
  59.1 8.7 %exchange_latent.1 = (bf16[8,32,768]{2,1,0:T(8,128)(2,1)S(1)}, bf16[16,256,128]{2,1,0:T(8,128)(2,1)S(1)}, bf16[256,512]{1,0:T(8,128)(2,1)S(1)}) custom-call(bf16[8,32,768]{2,1,0:T(8,128)(2,1)S(1)} %get-tuple-element.66.source, bf16[16,256,128]{2,1,0:T(8,128)(2,1)S(1)} %get-tuple-element.64.att_ref.att_all, ...), custom_call_target="tpu_custom_call" | custom-call | tf_op jit(solution)/shard_map/exchange_latent/pallas_call | solution.py:143
  67.8 0.0 copy-done.5
  67.8 9.9 %depth.1 = (bf16[32,768]{1,0:T(8,128)(2,1)S(1)}, bf16[4096,512]{1,0:T(8,128)(2,1)S(1)}) custom-call(bf16[8,32,768]{2,1,0:T(8,128)(2,1)S(1)} %get-tuple-element.68.part_ref, s32[8,32]{1,0:T(8,128)S(1)} %bitcast.17, bf16[4096,512]{1,0:T(8,128)(2,1)S(1)} %get-tuple-element.69.stack_ref), custom_call_target="tpu_custom_call" | custom-call | tf_op jit(solution)/shard_map/depth/pallas_call | solution.py:706
  77.8 11.2 %exchange_message.1 = (bf16[2,8,32,768]{3,2,1,0:T(8,128)(2,1)S(1)}, bf16[8,8,32,512]{3,2,1,0:T(8,128)(2,1)S(1)}) custom-call(bf16[32,768]{1,0:T(8,128)(2,1)S(1)} %get-tuple-element.70.source, bf16[8,2,8,32,512]{4,3,2,1,0:T(8,128)(2,1)S(1)} %bitcast.9), custom_call_target="tpu_custom_call" | custom-call | tf_op jit(solution)/shard_map/exchange_message/pallas_call | solution.py:143
  89.0 2.9 %unmerge.1 = (bf16[16,256,128]{2,1,0:T(8,128)(2,1)S(1)}, bf16[8,32,2560]{2,1,0:T(8,128)(2,1)S(1)}, bf16[8,8,32,512]{3,2,1,0:T(8,128)(2,1)S(1)}) custom-call(bf16[2,8,32,768]{3,2,1,0:T(8,128)(2,1)S(1)} %get-tuple-element.72.message_ref, f32[256,512]{1,0:T(8,128)S(1)} %get-tuple-element.73.merged_ref, bf16[256,512]{1,0:T(8,128)(2,1)S(1)} %get-tuple-element.67.merged.round_ref, ...), custom_call_target="tpu_custom_call" | custom-call | tf_op jit(solution)/shard_map/unmerge/pallas_call | solution.py:706
  91.8 28.2 %exchange_cotangent.1 = (bf16[2,8,256,128]{3,2,1,0:T(8,128)(2,1)S(1)}, bf16[4,2,32,2560]{3,2,1,0:T(8,128)(2,1)S(1)}, bf16[4,1,2,32,512]{4,3,2,1,0:T(8,128)(2,1)S(1)}) custom-call(bf16[16,256,128]{2,1,0:T(8,128)(2,1)S(1)} %get-tuple-element.77.source, bf16[4,2,32,2560]{3,2,1,0:T(8,128)(2,1)S(1)} %bitcast.13, bf16[8,2,4,32,512]{4,3,2,1,0:T(8,128)(2,1)S(1)} %bitcast.11), custom_call_target="tpu_custom_call" | custom-call | tf_op jit(solution)/shard_map/exchange_cotangent/pallas_call | solution.py:143
  120.0 0.4 prepare.1
  120.5 26.6 %exchange_grads.1 = (bf16[8,512,256]{2,1,0:T(8,128)(2,1)S(1)}, f32[8,8,512]{2,1,0:T(8,128)S(1)}, bf16[4,7,2,32,512]{4,3,2,1,0:T(8,128)(2,1)S(1)}, bf16[32,2560]{1,0:T(8,128)(2,1)S(1)}, bf16[256,4096]{1,0:T(8,128)(2,1)S(1)}) custom-call(bf16[512,256]{1,0:T(8,128)(2,1)S(1)} %get-tuple-element.84.pair, f32[8,512]{1,0:T(8,128)S(1)} %get-tuple-element.85.stats, ...), custom_call_target="tpu_custom_call" | custom-call | tf_op jit(solution)/shard_map/exchange_grads/pallas_call | solution.py:143
  147.1 10.2 %attend_back.1 = (bf16[4,2,2,176,256]{4,3,2,1,0:T(8,128)(2,1)S(1)}, bf16[2,2,4,208,256]{4,3,2,1,0:T(8,128)(2,1)S(1)}, bf16[8,2,32,512]{3,2,1,0:T(8,128)(2,1)S(1)...) custom-call(f32[8,8,512]{2,1,0:T(8,128)S(1)} %get-tuple-element.88.stats_ref, f32[512,64]{1,0:T(8,128)S(1)} %get-tuple-element.112.cos_ref, ...), custom_call_target="tpu_custom_call" | custom-call | tf_op jit(solution)/shard_map/attend_back/pallas_call | solution.py:706
  157.3 25.7 %exchange_first.1 = (bf16[4,2,2,176,256]{4,3,2,1,0:T(8,128)(2,1)S(1)}, bf16[2,2,4,208,256]{4,3,2,1,0:T(8,128)(2,1)S(1)}, bf16[4,2,2,32,512]{4,3,2,1,0:T(8,128)(2,1)S(1)}, bf16[8,32,256]{2,1,0:T(8,128)(2,1)S(1)}) custom-call(bf16[4,2,2,176,256]{4,3,2,1,0:T(8,128)(2,1)S(1)} %get-tuple-element.94.x_first, ...), custom_call_target="tpu_custom_call" | custom-call | tf_op jit(solution)/shard_map/exchange_first/pallas_call | solution.py:143
  183.0 0.4 middle_sum.1
  183.4 13.5 %exchange_second.1 = (bf16[2,176,256]{2,1,0:T(8,128)(2,1)S(1)}, bf16[4,2,208,256]{3,2,1,0:T(8,128)(2,1)S(1)}, bf16[2,2,32,512]{3,2,1,0:T(8,128)(2,1)S(1)}) custom-call(bf16[2,2,176,256]{3,2,1,0:T(8,128)(2,1)S(1)} %get-tuple-element.101.x_sum.x_own_ref, bf16[4,2,208,256]{3,2,1,0:T(8,128)(2,1)S(1)} %get-tuple-element.102.y_sum, ...), custom_call_target="tpu_custom_call" | custom-call | tf_op jit(solution)/shard_map/exchange_second/pallas_call | solution.py:143
  196.9 1.4 last_sum.1
  (2 shorter events, 0.0 us)
Async XLA Ops:
  1.7 3.4 %copy-start.1 = (bf16[4096,4,256]{2,1,0:T(4,128)(2,1)S(1)}, bf16[4096,4,256]{2,1,0:T(4,128)(2,1)}, u32[]{:S(2)}) copy-start(bf16[4096,4,256]{2,1,0:T(4,128)(2,1)} %w_hbm.1) | copy-start | bytes 25165828
  5.0 1.6 copy-start.2
  6.6 50.4 %copy-start.3 = (bf16[256,4096]{1,0:T(8,128)(2,1)S(1)}, bf16[256,4096]{1,0:T(8,128)(2,1)}, u32[]{:S(2)}) copy-start(bf16[256,4096]{1,0:T(8,128)(2,1)} %hidden_ref.3) | copy-start | bytes 6291460
  6.6 50.4 %copy-start.4 = (bf16[4096,512]{1,0:T(8,128)(2,1)S(1)}, bf16[4096,512]{1,0:T(8,128)(2,1)}, u32[]{:S(2)}) copy-start(bf16[4096,512]{1,0:T(8,128)(2,1)} %stack_hbm.1) | copy-start | bytes 12582916
  12.0 45.1 %copy-start = (bf16[4096,512]{1,0:T(8,128)(2,1)S(1)}, bf16[4096,512]{1,0:T(8,128)(2,1)}, u32[]{:S(2)}) copy-start(bf16[4096,512]{1,0:T(8,128)(2,1)} %param.7) | copy-start | bytes 12582916
  57.1 10.8 %copy-start.5 = (s32[32,8]{0,1:T(8,128)S(1)}, s32[32,8]{0,1:T(8,128)}, u32[]{:S(2)}) copy-start(s32[32,8]{0,1:T(8,128)} %param.9) | copy-start | bytes 3076

commit v8 on v7

--- a/solution.py
+++ b/solution.py
@@ -937,7 +937,7 @@
         values = proj[:, 2 * DD + low : 2 * DD + low + DHD]
         scores = jnp.where(allowed, dot_nt(queries, keys) * depth_scale, MASKED)
         weights = jnp.exp(scores - jnp.max(scores, axis=-1, keepdims=True))
-        probs = weights / jnp.sum(weights, axis=-1, keepdims=True)
+        probs = weights * (1.0 / jnp.sum(weights, axis=-1, keepdims=True))
         prob_ref[head] = probs
         mixed.append(dot_nn(probs.astype(BF16), values))
     mixed = jnp.concatenate(mixed, axis=1).astype(BF16)
@@ -948,7 +948,7 @@
     head_rows = stack_ref[4 * DD : 4 * DD + VOCAB]
     logits = dot_nt(resid_norm, head_rows)
     weights = jnp.exp(logits - jnp.max(logits, axis=-1, keepdims=True))
-    logit_probs = weights / jnp.sum(weights, axis=-1, keepdims=True)
+    logit_probs = weights * (1.0 / jnp.sum(weights, axis=-1, keepdims=True))
     target = jnp.where(codes == vocab_at, 1.0, 0.0)
     logit_grad = ((logit_probs - target) * loss_scale).astype(BF16)
     grad_ref[4 * DD : 4 * DD + VOCAB] = dot_tn(logit_grad, resid_norm).astype(BF16)

time: 199 us -> 199 us (level)
  no operation moved by 1% of the time
where the time goes in v8:
time: 199 us; the launch traced here: 198 us
  Pallas kernels  192 us (96%)
  local copies, waits for them, and re-layouts  4.99 us (3%)
    pallas_call x8, Pallas kernels, exchange(): pl.pallas_call(kernel, name=name, out_shape=outs, in_specs=[ANY] * len(in...  158 us
    pallas_call x9, Pallas kernels, compute(): pl.pallas_call(kernel, name=name, out_shape=outs, in_specs=[VMEM] * (len(...  33.6 us
    unnamed x12, local copies, waits for them, and re-layouts  4.99 us

profile of v8, /device:TPU:1, one launch (start us, length us, event | category | flops | bytes accessed | tf_op | source)
XLA Modules:
  0.0 198.3 jit_solution(9326755113927715383)
XLA Ops:
  0.7 1.0 multiply_sine_fusion
  1.7 0.0 copy-start.1
  1.7 3.4 %copy-done.1 = bf16[4096,4,256]{2,1,0:T(4,128)(2,1)S(1)} copy-done((bf16[4096,4,256]{2,1,0:T(4,128)(2,1)S(1)}, bf16[4096,4,256]{2,1,0:T(4,128)(2,1)}, u32[]{:S(2)}) %copy-start.1) | copy-done | bytes 8388632
  5.0 0.0 copy-start.2
  5.0 1.6 copy-done.2
  6.6 0.0 copy-start.3
  6.6 0.0 copy-start.4
  6.6 5.4 %start.1 = (bf16[256,4096]{1,0:T(8,128)(2,1)S(1)}, bf16[2,256,256]{2,1,0:T(8,128)(2,1)S(1)}, bf16[2,256,128]{2,1,0:T(8,128)(2,1)S(1)}, bf16[8,512,256]{2,1,0:T(8,128)(2,1)S(1)}) custom-call(bf16[256,4096]{1,0:T(8,128)(2,1)S(1)} %copy-done.2, f32[512,64]{1,0:T(8,128)S(1)} %get-tuple-element.112.cos_ref, f32[512,64]{1,0:T(8,128)S(1)} %get-tuple-element.111.sin_ref, ...), custom_call_target="tpu_custom_call" | custom-call | tf_op jit(solution)/shard_map/start/pallas_call | solution.py:706
  12.0 0.0 copy-start
  12.0 27.1 %exchange_keys.1 = (bf16[8,512,256]{2,1,0:T(8,128)(2,1)S(1)}, bf16[2,256,128]{2,1,0:T(8,128)(2,1)S(1)}, bf16[8,256,256]{2,1,0:T(8,128)(2,1)S(1)}) custom-call(bf16[2,256,256]{2,1,0:T(8,128)(2,1)S(1)} %get-tuple-element.57.kv, bf16[2,256,128]{2,1,0:T(8,128)(2,1)S(1)} %get-tuple-element.58.query, bf16[8,512,256]{2,1,0:T(8,128)(2,1)S(1)} %get-tuple-element.59.out_w), custom_call_target="tpu_custom_call" | custom-call | tf_op jit(solution)/shard_map/exchange_keys/pallas_call | solution.py:143
  39.1 1.0 attend.1
  40.1 17.0 %exchange_attended.1 = (bf16[16,256,128]{2,1,0:T(8,128)(2,1)S(1)}, bf16[8,256,256]{2,1,0:T(8,128)(2,1)S(1)}) custom-call(bf16[512,128]{1,0:T(8,128)(2,1)S(1)} %get-tuple-element.62.source, bf16[8,256,256]{2,1,0:T(8,128)(2,1)S(1)} %get-tuple-element.63.w_half.half_ref), custom_call_target="tpu_custom_call" | custom-call | tf_op jit(solution)/shard_map/exchange_attended/pallas_call | solution.py:143
  57.1 0.0 copy-done.3
  57.1 0.0 copy-done.4
  57.1 0.0 copy-done
  57.1 0.0 copy-start.5
  57.1 2.0 %merge.1 = (f32[256,512]{1,0:T(8,128)S(1)}, bf16[256,512]{1,0:T(8,128)(2,1)S(1)}, bf16[8,32,768]{2,1,0:T(8,128)(2,1)S(1)}, bf16[4096,512]{1,0:T(8,128)(2,1)S(1)}) custom-call(bf16[16,256,128]{2,1,0:T(8,128)(2,1)S(1)} %get-tuple-element.64.att_ref.att_all, bf16[8,256,256]{2,1,0:T(8,128)(2,1)S(1)} %get-tuple-element.63.w_half.half_ref, ...), custom_call_target="tpu_custom_call" | custom-call | tf_op jit(solution)/shard_map/merge/pallas_call | solution.py:706
  59.1 8.7 %exchange_latent.1 = (bf16[8,32,768]{2,1,0:T(8,128)(2,1)S(1)}, bf16[16,256,128]{2,1,0:T(8,128)(2,1)S(1)}, bf16[256,512]{1,0:T(8,128)(2,1)S(1)}) custom-call(bf16[8,32,768]{2,1,0:T(8,128)(2,1)S(1)} %get-tuple-element.66.source, bf16[16,256,128]{2,1,0:T(8,128)(2,1)S(1)} %get-tuple-element.64.att_ref.att_all, ...), custom_call_target="tpu_custom_call" | custom-call | tf_op jit(solution)/shard_map/exchange_latent/pallas_call | solution.py:143
  67.8 0.0 copy-done.5
  67.8 9.9 %depth.1 = (bf16[32,768]{1,0:T(8,128)(2,1)S(1)}, bf16[4096,512]{1,0:T(8,128)(2,1)S(1)}) custom-call(bf16[8,32,768]{2,1,0:T(8,128)(2,1)S(1)} %get-tuple-element.68.part_ref, s32[8,32]{1,0:T(8,128)S(1)} %bitcast.17, bf16[4096,512]{1,0:T(8,128)(2,1)S(1)} %get-tuple-element.69.stack_ref), custom_call_target="tpu_custom_call" | custom-call | tf_op jit(solution)/shard_map/depth/pallas_call | solution.py:706
  77.8 11.2 %exchange_message.1 = (bf16[2,8,32,768]{3,2,1,0:T(8,128)(2,1)S(1)}, bf16[8,8,32,512]{3,2,1,0:T(8,128)(2,1)S(1)}) custom-call(bf16[32,768]{1,0:T(8,128)(2,1)S(1)} %get-tuple-element.70.source, bf16[8,2,8,32,512]{4,3,2,1,0:T(8,128)(2,1)S(1)} %bitcast.9), custom_call_target="tpu_custom_call" | custom-call | tf_op jit(solution)/shard_map/exchange_message/pallas_call | solution.py:143
  89.0 2.9 %unmerge.1 = (bf16[16,256,128]{2,1,0:T(8,128)(2,1)S(1)}, bf16[8,32,2560]{2,1,0:T(8,128)(2,1)S(1)}, bf16[8,8,32,512]{3,2,1,0:T(8,128)(2,1)S(1)}) custom-call(bf16[2,8,32,768]{3,2,1,0:T(8,128)(2,1)S(1)} %get-tuple-element.72.message_ref, f32[256,512]{1,0:T(8,128)S(1)} %get-tuple-element.73.merged_ref, bf16[256,512]{1,0:T(8,128)(2,1)S(1)} %get-tuple-element.67.merged.round_ref, ...), custom_call_target="tpu_custom_call" | custom-call | tf_op jit(solution)/shard_map/unmerge/pallas_call | solution.py:706
  91.8 28.2 %exchange_cotangent.1 = (bf16[2,8,256,128]{3,2,1,0:T(8,128)(2,1)S(1)}, bf16[4,2,32,2560]{3,2,1,0:T(8,128)(2,1)S(1)}, bf16[4,1,2,32,512]{4,3,2,1,0:T(8,128)(2,1)S(1)}) custom-call(bf16[16,256,128]{2,1,0:T(8,128)(2,1)S(1)} %get-tuple-element.77.source, bf16[4,2,32,2560]{3,2,1,0:T(8,128)(2,1)S(1)} %bitcast.13, bf16[8,2,4,32,512]{4,3,2,1,0:T(8,128)(2,1)S(1)} %bitcast.11), custom_call_target="tpu_custom_call" | custom-call | tf_op jit(solution)/shard_map/exchange_cotangent/pallas_call | solution.py:143
  120.0 0.4 prepare.1
  120.5 26.6 %exchange_grads.1 = (bf16[8,512,256]{2,1,0:T(8,128)(2,1)S(1)}, f32[8,8,512]{2,1,0:T(8,128)S(1)}, bf16[4,7,2,32,512]{4,3,2,1,0:T(8,128)(2,1)S(1)}, bf16[32,2560]{1,0:T(8,128)(2,1)S(1)}, bf16[256,4096]{1,0:T(8,128)(2,1)S(1)}) custom-call(bf16[512,256]{1,0:T(8,128)(2,1)S(1)} %get-tuple-element.84.pair, f32[8,512]{1,0:T(8,128)S(1)} %get-tuple-element.85.stats, ...), custom_call_target="tpu_custom_call" | custom-call | tf_op jit(solution)/shard_map/exchange_grads/pallas_call | solution.py:143
  147.1 10.2 %attend_back.1 = (bf16[4,2,2,176,256]{4,3,2,1,0:T(8,128)(2,1)S(1)}, bf16[2,2,4,208,256]{4,3,2,1,0:T(8,128)(2,1)S(1)}, bf16[8,2,32,512]{3,2,1,0:T(8,128)(2,1)S(1)...) custom-call(f32[8,8,512]{2,1,0:T(8,128)S(1)} %get-tuple-element.88.stats_ref, f32[512,64]{1,0:T(8,128)S(1)} %get-tuple-element.112.cos_ref, ...), custom_call_target="tpu_custom_call" | custom-call | tf_op jit(solution)/shard_map/attend_back/pallas_call | solution.py:706
  157.3 25.7 %exchange_first.1 = (bf16[4,2,2,176,256]{4,3,2,1,0:T(8,128)(2,1)S(1)}, bf16[2,2,4,208,256]{4,3,2,1,0:T(8,128)(2,1)S(1)}, bf16[4,2,2,32,512]{4,3,2,1,0:T(8,128)(2,1)S(1)}, bf16[8,32,256]{2,1,0:T(8,128)(2,1)S(1)}) custom-call(bf16[4,2,2,176,256]{4,3,2,1,0:T(8,128)(2,1)S(1)} %get-tuple-element.94.x_first, ...), custom_call_target="tpu_custom_call" | custom-call | tf_op jit(solution)/shard_map/exchange_first/pallas_call | solution.py:143
  183.0 0.4 middle_sum.1
  183.4 13.5 %exchange_second.1 = (bf16[2,176,256]{2,1,0:T(8,128)(2,1)S(1)}, bf16[4,2,208,256]{3,2,1,0:T(8,128)(2,1)S(1)}, bf16[2,2,32,512]{3,2,1,0:T(8,128)(2,1)S(1)}) custom-call(bf16[2,2,176,256]{3,2,1,0:T(8,128)(2,1)S(1)} %get-tuple-element.101.x_sum.x_own_ref, bf16[4,2,208,256]{3,2,1,0:T(8,128)(2,1)S(1)} %get-tuple-element.102.y_sum, ...), custom_call_target="tpu_custom_call" | custom-call | tf_op jit(solution)/shard_map/exchange_second/pallas_call | solution.py:143
  196.9 1.4 last_sum.1
  (2 shorter events, 0.0 us)
Async XLA Ops:
  1.7 3.4 %copy-start.1 = (bf16[4096,4,256]{2,1,0:T(4,128)(2,1)S(1)}, bf16[4096,4,256]{2,1,0:T(4,128)(2,1)}, u32[]{:S(2)}) copy-start(bf16[4096,4,256]{2,1,0:T(4,128)(2,1)} %w_hbm.1) | copy-start | bytes 25165828
  5.0 1.6 copy-start.2
  6.6 50.4 %copy-start.3 = (bf16[256,4096]{1,0:T(8,128)(2,1)S(1)}, bf16[256,4096]{1,0:T(8,128)(2,1)}, u32[]{:S(2)}) copy-start(bf16[256,4096]{1,0:T(8,128)(2,1)} %hidden_ref.3) | copy-start | bytes 6291460
  6.6 50.4 %copy-start.4 = (bf16[4096,512]{1,0:T(8,128)(2,1)S(1)}, bf16[4096,512]{1,0:T(8,128)(2,1)}, u32[]{:S(2)}) copy-start(bf16[4096,512]{1,0:T(8,128)(2,1)} %stack_hbm.1) | copy-start | bytes 12582916
  12.0 45.1 %copy-start = (bf16[4096,512]{1,0:T(8,128)(2,1)S(1)}, bf16[4096,512]{1,0:T(8,128)(2,1)}, u32[]{:S(2)}) copy-start(bf16[4096,512]{1,0:T(8,128)(2,1)} %param.7) | copy-start | bytes 12582916
  57.1 10.8 %copy-start.5 = (s32[32,8]{0,1:T(8,128)S(1)}, s32[32,8]{0,1:T(8,128)}, u32[]{:S(2)}) copy-start(s32[32,8]{0,1:T(8,128)} %param.9) | copy-start | bytes 3076
